TPU v7x, 32 devices: a whole 2x2x4 slice. The times are simulated.
32 devices in a mesh: layer: 2 (over y), row: 4 (over x, core), col: 4 (over z).
Axes of the slice: x: 2, y: 2, z: 4, core: 2. Of those that a mesh axis runs over, the one named last changes fastest.
Arguments:
- inverse_rows: bfloat16 [43008, 21504], P(('layer', 'col'), 'row'), parts along dimension 0
- hess_weight: float32 [43008, 512], P(('layer', 'row', 'col')), parts along dimension 0, may hold values from -6 to 6
- pruned_start: float32 [43008, 512], P(('layer', 'row', 'col')), parts along dimension 0, may hold values from -6 to 6
- dual_start: float32 [43008, 512], P(('layer', 'row', 'col')), parts along dimension 0, may hold values from -3 to 3
- prune_mask: int32 [43008, 512], P(('layer', 'row', 'col')), parts along dimension 0, may hold values 0 or 1
- dual_rate: int32 [1024], P('layer'), parts along dimension 0, may hold values from 0 to 3
Outputs:
- repaired: float32 [43008, 512], P(('layer', 'row', 'col')), parts along dimension 0
- duals: float32 [43008, 512], P(('layer', 'row', 'col')), parts along dimension 0
There are 2 independent parts, one for each index of `layer`. A program takes and returns all parts, laid end to end along the dimension named above; each array names one. Nothing has to cross between parts.
All inputs are finite; a program needn't handle non-finite values. No bound on the sum of `prune_mask` on one device may be relied on, other than what follows from the above.
Results may differ from a plain program's by a relative error of at most 0.0031.
Values may be sent and summed in bfloat16 or wider, within the bound.
No kernel may reach another device: no remote copies, remote signals or barrier semaphores. Data moves between devices by JAX's collectives and lax.ppermute only.
A program may use at most 256 MiB of HBM per device.

v0:
```python
import jax
import jax.numpy as jnp
from jax import lax
from jax.sharding import PartitionSpec as P

ITERS = 3


def local(inverse_rows, hess_weight, pruned_start, dual_start, prune_mask, dual_rate):
    kept = prune_mask.astype(jnp.float32)
    step_size = 0.5 + 0.25 * dual_rate.astype(jnp.float32)
    projected = pruned_start
    scaled = dual_start
    for iteration in range(ITERS):
        right_side = (hess_weight + projected - scaled).astype(jnp.bfloat16)
        partial_value = jnp.dot(
            inverse_rows,
            lax.all_gather(right_side, "col", axis=0, tiled=True),
            preferred_element_type=jnp.float32,
        )
        iterate = lax.psum_scatter(partial_value, "row", scatter_dimension=0, tiled=True)
        projected = kept * (iterate + scaled)
        scaled = scaled + step_size[None, :] * (iterate - projected)
    return (projected, scaled)


def solution(mesh):
    in_specs = (
        P(("layer", "col"), "row"),
        P(("layer", "row", "col"), None),
        P(("layer", "row", "col"), None),
        P(("layer", "row", "col"), None),
        P(("layer", "row", "col"), None),
        P("layer"),
    )
    out_specs = (P(("layer", "row", "col"), None), P(("layer", "row", "col"), None))
    return jax.shard_map(local, mesh=mesh, in_specs=in_specs, out_specs=out_specs, check_vma=False)
```

profile of v0, /device:TPU:16, one launch (start us, length us, event | category | flops | bytes accessed | tf_op | source)
XLA Modules:
  0.0 779.0 jit_solution(7685462392194461329)
XLA Ops:
  7.2 0.0 all-gather.4.cloned.1.call-start
  7.2 5.3 subtract_convert_fusion.2
  12.5 0.0 all-gather.4.cloned.1.call-update
  12.6 0.0 reduce-scatter.10.cloned.1.call-start
  12.6 101.9 %all-gather.4.cloned.1.call-done = bf16[5376,512]{1,0:T(8,128)(2,1)} async-done(((bf16[1344,512]{1,0:T(8,128)(2,1)}), bf16[5376,512]{1,0:T(8,128)(2,1)}) %all-gather.4.cloned.1.call-update) | async-done | bytes 5505040 | tf_op jit(solution)/shard_map/all_gather | solution.py:18
  114.5 37.5 %convolution_bitcast_fusion.2 = f32[5376,512]{0,1:T(8,128)} fusion(bf16[5376,512]{1,0:T(8,128)(2,1)} %all-gather.4.cloned.1.call-done, bf16[5376,5376]{1,0:T(8,128)(2,1)} %param.6), kind=kOutput, calls=%fused_computation.2 | convolution fusion | flops 29595009024 | bytes 74317824 | tf_op jit(solution)/shard_map/dot_general | solution.py:16
  152.0 12.1 %copy.24 = f32[5376,512]{1,0:T(8,128)} copy(f32[5376,512]{0,1:T(8,128)} %convolution_bitcast_fusion.2) | data formatting | bytes 22020096
  164.1 0.0 reduce-scatter.10.cloned.1.call-update
  164.2 0.0 all-gather.6.cloned.1.call-start
  164.2 2.2 copy.16
  166.5 3.4 copy.20
  169.8 0.0 copy-start.1
  169.8 4.0 copy.15
  173.8 0.0 copy-done.1
  173.8 79.2 %reduce-scatter.10.cloned.1.call-done = f32[1344,512]{1,0:T(8,128)} async-done(((f32[5376,512]{1,0:T(8,128)}), f32[1344,512]{1,0:T(8,128)}) %reduce-scatter.10.cloned.1.call-update) | async-done | bytes 2752528
  253.0 3.4 copy.25
  256.4 5.7 subtract_convert_fusion.1
  262.0 2.5 copy.19
  264.5 0.0 all-gather.6.cloned.1.call-update
  264.5 0.2 reduce-scatter.12.cloned.1.call-start
  264.8 100.7 %all-gather.6.cloned.1.call-done = bf16[5376,512]{1,0:T(8,128)(2,1)} async-done(((bf16[1344,512]{1,0:T(8,128)(2,1)}), bf16[5376,512]{1,0:T(8,128)(2,1)}) %all-gather.6.cloned.1.call-update) | async-done | bytes 5505040 | tf_op jit(solution)/shard_map/all_gather | solution.py:18
  365.4 37.5 %convolution_bitcast_fusion.1 = f32[5376,512]{0,1:T(8,128)} fusion(bf16[5376,512]{1,0:T(8,128)(2,1)} %all-gather.6.cloned.1.call-done, bf16[5376,5376]{1,0:T(8,128)(2,1)} %param.6), kind=kOutput, calls=%fused_computation.1 | convolution fusion | flops 29595009024 | bytes 74317824 | tf_op jit(solution)/shard_map/dot_general | solution.py:16
  402.9 12.1 %copy.26 = f32[5376,512]{1,0:T(8,128)} copy(f32[5376,512]{0,1:T(8,128)} %convolution_bitcast_fusion.1) | data formatting | bytes 22020096
  415.0 0.0 reduce-scatter.12.cloned.1.call-update
  415.0 0.0 all-gather.8.cloned.1.call-start
  415.1 88.8 %reduce-scatter.12.cloned.1.call-done = f32[1344,512]{1,0:T(8,128)} async-done(((f32[5376,512]{1,0:T(8,128)}), f32[1344,512]{1,0:T(8,128)}) %reduce-scatter.12.cloned.1.call-update) | async-done | bytes 2752528
  503.9 3.5 copy.27
  507.3 7.2 subtract_convert_fusion
  514.5 2.5 copy.21
  517.0 0.0 all-gather.8.cloned.1.call-update
  517.0 0.3 reduce-scatter.14.cloned.1.call-start
  517.3 100.6 %all-gather.8.cloned.1.call-done = bf16[5376,512]{1,0:T(8,128)(2,1)} async-done(((bf16[1344,512]{1,0:T(8,128)(2,1)}), bf16[5376,512]{1,0:T(8,128)(2,1)}) %all-gather.8.cloned.1.call-update) | async-done | bytes 5505040 | tf_op jit(solution)/shard_map/all_gather | solution.py:18
  617.9 37.5 %convolution_bitcast_fusion = f32[5376,512]{0,1:T(8,128)} fusion(bf16[5376,512]{1,0:T(8,128)(2,1)} %all-gather.8.cloned.1.call-done, bf16[5376,5376]{1,0:T(8,128)(2,1)} %param.6), kind=kOutput, calls=%fused_computation | convolution fusion | flops 29595009024 | bytes 74317824 | tf_op jit(solution)/shard_map/dot_general | solution.py:16
  655.4 12.1 %copy.28 = f32[5376,512]{1,0:T(8,128)} copy(f32[5376,512]{0,1:T(8,128)} %convolution_bitcast_fusion) | data formatting | bytes 22020096
  667.5 0.0 reduce-scatter.14.cloned.1.call-update
  667.5 88.8 %reduce-scatter.14.cloned.1.call-done = f32[1344,512]{1,0:T(8,128)} async-done(((f32[5376,512]{1,0:T(8,128)}), f32[1344,512]{1,0:T(8,128)}) %reduce-scatter.14.cloned.1.call-update) | async-done | bytes 2752528
  756.4 3.4 copy.29
  759.7 6.8 multiply_add_fusion
  766.5 0.0 copy-start
  766.5 3.5 copy.23
  770.0 0.0 copy-done
  770.0 2.2 copy.22
  (1 shorter events, 0.0 us)
Async XLA Ops:
  7.2 107.4 %all-gather.4.cloned.1.call-start = ((), (), s32[]{:S(2)}) async-start(), calls=%async_computation.3 | async-start | bytes 6881280 | tf_op jit(solution)/shard_map/all_gather | solution.py:18
  12.6 240.4 %reduce-scatter.10.cloned.1.call-start = ((), (), s32[]{:S(2)}) async-start(), calls=%async_computation.6 | async-start | bytes 13762560
  164.2 201.3 %all-gather.6.cloned.1.call-start = ((), (), s32[]{:S(2)}) async-start(), calls=%async_computation.4 | async-start | bytes 6881280 | tf_op jit(solution)/shard_map/all_gather | solution.py:18
  169.8 4.0 copy-start.1
  264.5 239.3 %reduce-scatter.12.cloned.1.call-start = ((), (), s32[]{:S(2)}) async-start(), calls=%async_computation.7 | async-start | bytes 13762560
  415.0 202.9 %all-gather.8.cloned.1.call-start = ((), (), s32[]{:S(2)}) async-start(), calls=%async_computation.5 | async-start | bytes 6881280 | tf_op jit(solution)/shard_map/all_gather | solution.py:18
  517.0 239.3 %reduce-scatter.14.cloned.1.call-start = ((), (), s32[]{:S(2)}) async-start(), calls=%async_computation.8 | async-start | bytes 13762560
  766.5 3.5 copy-start
Sparse Core Ops, SparseCore 0:
  12.7 101.7 all-gather.3
  164.3 88.6 reduce-scatter.9
  264.6 100.7 all-gather.5
  415.1 88.6 reduce-scatter.11
  517.1 100.7 all-gather.7
  667.6 88.6 reduce-scatter.13
where the time goes:
time: 781 us; the launch traced here: 779 us
  waiting for transfers between devices  560 us (72%)
  matrix products  112 us (14%)
  local copies, waits for them, and re-layouts  66.6 us (9%)
  other arithmetic  24.9 us (3%)
  between operations  14.1 us (2%)
    all_gather x3, waiting for transfers between devices, local(): lax.all_gather(right_side, 'col', axis=0, tiled=True)  303 us
    unnamed x9, waiting for transfers between devices  257 us
    dot_general x3, matrix products, local(): jnp.dot(inverse_rows, lax.all_gather(right_side, 'col', axis=0, tiled=Tru...  112 us
    unnamed x15, local copies, waits for them, and re-layouts  61.6 us
    convert_element_type x3, other arithmetic, local(): right_side = (hess_weight + projected - scaled).astype(jnp.bfloat16)  18.2 us
  transfers between devices with their start and end apart: 6, of which 6 were waited for; matrix products, arithmetic and copies ran while one was open for 1% of the time, Pallas kernels for 0%

commit v1 on v0

v1 whole, which is shorter than its diff:
```python
import jax
import jax.numpy as jnp
from jax import lax
from jax.experimental import pallas as pl
from jax.experimental.pallas import tpu as pltpu
from jax.sharding import PartitionSpec as P

ITERS = 3
CHUNKS = 2
BF16 = jnp.bfloat16
F32 = jnp.float32

OUTER = [(0, 1), (1, 0), (2, 3), (3, 2)]
INNER = [(1, 2), (2, 1)]
SKIP = [(0, 2), (3, 1)]
ENDS = [(1, 0), (2, 3)]
CORE = [(0, 1), (1, 0), (2, 3), (3, 2)]
ACROSS = [(0, 2), (2, 0), (1, 3), (3, 1)]


def first_pair_kernel(place, matrix, own, near, out, pair, sems):
    shard = own.shape[0]

    @pl.when(pl.program_id(0) == 0)
    def _():
        here = pl.multiple_of(place[1] * shard, 16)
        there = pl.multiple_of((1 - place[1]) * shard, 16)
        copies = [
            pltpu.make_async_copy(own, pair.at[pl.ds(here, shard)], sems.at[0]),
            pltpu.make_async_copy(near, pair.at[pl.ds(there, shard)], sems.at[1]),
        ]
        for copy in copies:
            copy.start()
        for copy in copies:
            copy.wait()

    out[...] = jnp.dot(matrix[...], pair[...], preferred_element_type=F32)


def first_pair(place, matrix, own, near, tile):
    shard, width = own.shape
    slab = matrix.shape[0]
    return pl.pallas_call(
        first_pair_kernel,
        grid_spec=pltpu.PrefetchScalarGridSpec(
            num_scalar_prefetch=1,
            grid=(slab // tile,),
            in_specs=[
                pl.BlockSpec((tile, 2 * shard), lambda i, place: (i, place[0])),
                pl.BlockSpec(memory_space=pl.ANY),
                pl.BlockSpec(memory_space=pl.ANY),
            ],
            out_specs=pl.BlockSpec((tile, width), lambda i, place: (i, 0)),
            scratch_shapes=[pltpu.VMEM((2 * shard, width), BF16), pltpu.SemaphoreType.DMA((2,))],
        ),
        out_shape=jax.ShapeDtypeStruct((slab, width), F32),
        compiler_params=pltpu.CompilerParams(vmem_limit_bytes=32 * 2**20),
        cost_estimate=pl.CostEstimate(
            flops=4 * slab * shard * width, bytes_accessed=4 * slab * shard + 4 * slab * width, transcendentals=0
        ),
        name="first_pair",
    )(place, matrix, own, near)


def second_pair_kernel(place, matrix, before, end_a, end_b, mid_a, mid_b, send, keep, pair, sems):
    shard = end_a.shape[0]
    step = pl.program_id(0)
    half_steps = pl.num_programs(0) // 2

    @pl.when(step == 0)
    def _():
        here = pl.multiple_of((1 - place[0]) * shard, 16)
        there = pl.multiple_of(place[0] * shard, 16)

        def fetch(a, b):
            copies = [
                pltpu.make_async_copy(a, pair.at[pl.ds(here, shard)], sems.at[0]),
                pltpu.make_async_copy(b, pair.at[pl.ds(there, shard)], sems.at[1]),
            ]
            for copy in copies:
                copy.start()
            for copy in copies:
                copy.wait()

        @pl.when(place[1] == 1)
        def _():
            fetch(end_a, end_b)

        @pl.when(place[1] == 0)
        def _():
            fetch(mid_a, mid_b)

    total = before[...] + jnp.dot(matrix[...], pair[...], preferred_element_type=F32)

    @pl.when(step < half_steps)
    def _():
        send[...] = total.astype(BF16)

    @pl.when(step >= half_steps)
    def _():
        keep[...] = total


def second_pair(place, matrix, before, ends, mids, tile):
    shard, width = ends[0].shape
    steps = shard // tile

    def row(i, place):
        return jnp.where(i < steps, place[2], place[3]) * steps + lax.rem(i, steps)

    return pl.pallas_call(
        second_pair_kernel,
        grid_spec=pltpu.PrefetchScalarGridSpec(
            num_scalar_prefetch=1,
            grid=(2 * steps,),
            in_specs=[
                pl.BlockSpec((tile, 2 * shard), lambda i, place: (row(i, place), place[0])),
                pl.BlockSpec((tile, width), lambda i, place: (row(i, place), 0)),
            ]
            + [pl.BlockSpec(memory_space=pl.ANY)] * 4,
            out_specs=[
                pl.BlockSpec((tile, width), lambda i, place: (jnp.minimum(i, steps - 1), 0)),
                pl.BlockSpec((tile, width), lambda i, place: (jnp.maximum(i - steps, 0), 0)),
            ],
            scratch_shapes=[pltpu.VMEM((2 * shard, width), BF16), pltpu.SemaphoreType.DMA((2,))],
        ),
        out_shape=[jax.ShapeDtypeStruct((shard, width), BF16), jax.ShapeDtypeStruct((shard, width), F32)],
        compiler_params=pltpu.CompilerParams(vmem_limit_bytes=32 * 2**20),
        cost_estimate=pl.CostEstimate(
            flops=8 * shard * shard * width, bytes_accessed=8 * shard * shard + 14 * shard * width, transcendentals=0
        ),
        name="second_pair",
    )(place, matrix, before, *ends, *mids)


def pipelined(inverse_rows, hess_weight, pruned_start, dual_start, prune_mask, dual_rate):
    shard, out = hess_weight.shape
    width = out // CHUNKS
    tile = 672
    col = lax.axis_index("col")
    row = lax.axis_index("row")
    own_pair = col // 2
    at_end = (col == 0) | (col == 3)
    core = row % 2
    other_x = 1 - row // 2
    as_i32 = lambda *values: jnp.stack([jnp.asarray(value, jnp.int32) for value in values])
    first_place = as_i32(own_pair, col % 2)
    far_place = as_i32(1 - own_pair, at_end, 2 * other_x + 1 - core, 2 * other_x + core)
    near_place = as_i32(1 - own_pair, at_end, row + 1 - 2 * core, row)

    kept = prune_mask.astype(F32)
    step_size = (0.5 + 0.25 * dual_rate.astype(F32))[None, :]
    parts = [slice(chunk * width, (chunk + 1) * width) for chunk in range(CHUNKS)]
    projected = [pruned_start[:, part] for part in parts]
    scaled = [dual_start[:, part] for part in parts]
    for iteration in range(ITERS):
        for chunk, part in enumerate(parts):
            own = (hess_weight[:, part] + projected[chunk] - scaled[chunk]).astype(BF16)
            outer = lax.ppermute(own, "col", OUTER)
            inner = lax.ppermute(own, "col", INNER)
            skip = lax.ppermute(own, "col", SKIP)
            end_a = lax.ppermute(inner, "col", ENDS)
            end_b = lax.ppermute(skip, "col", ENDS)
            before = first_pair(first_place, inverse_rows, own, outer, tile)
            send, keep = second_pair(far_place, inverse_rows, before, (end_a, end_b), (inner, skip), tile)
            far = (keep + lax.ppermute(send, "row", CORE).astype(F32)).astype(BF16)
            send, keep = second_pair(near_place, inverse_rows, before, (end_a, end_b), (inner, skip), tile)
            near = keep + lax.ppermute(send, "row", CORE).astype(F32)
            iterate = near + lax.ppermute(far, "row", ACROSS).astype(F32)
            projected[chunk] = kept[:, part] * (iterate + scaled[chunk])
            scaled[chunk] = scaled[chunk] + step_size[:, part] * (iterate - projected[chunk])
    return jnp.concatenate(projected, 1), jnp.concatenate(scaled, 1)


def plain(inverse_rows, hess_weight, pruned_start, dual_start, prune_mask, dual_rate):
    kept = prune_mask.astype(F32)
    step_size = 0.5 + 0.25 * dual_rate.astype(F32)
    projected = pruned_start
    scaled = dual_start
    for iteration in range(ITERS):
        right_side = (hess_weight + projected - scaled).astype(BF16)
        partial_value = jnp.dot(
            inverse_rows,
            lax.all_gather(right_side, "col", axis=0, tiled=True),
            preferred_element_type=F32,
        )
        iterate = lax.psum_scatter(partial_value, "row", scatter_dimension=0, tiled=True)
        projected = kept * (iterate + scaled)
        scaled = scaled + step_size[None, :] * (iterate - projected)
    return (projected, scaled)


def solution(mesh):
    in_specs = (
        P(("layer", "col"), "row"),
        P(("layer", "row", "col"), None),
        P(("layer", "row", "col"), None),
        P(("layer", "row", "col"), None),
        P(("layer", "row", "col"), None),
        P("layer"),
    )
    out_specs = (P(("layer", "row", "col"), None), P(("layer", "row", "col"), None))
    four_by_four = mesh.shape["row"] == 4 and mesh.shape["col"] == 4
    local = pipelined if four_by_four else plain
    return jax.shard_map(local, mesh=mesh, in_specs=in_specs, out_specs=out_specs, check_vma=False)
```

time: 781 us -> 517 us (0.66)
  waiting for transfers between devices: 560 us -> 243 us
  Pallas kernels: 0 us -> 201 us
  matrix products: 112 us -> 0 us
  local copies, waits for them, and re-layouts: 66.6 us -> 1.01 us
  starting transfers between devices: 0.65 us -> 54 us
  between operations: 14.1 us -> 1.27 us
  other arithmetic: 24.9 us -> 14.4 us
    all_gather x3 -> x0, waiting for transfers between devices: 303 us -> none  [local(): lax.all_gather(right_side, 'col', axis=0, tiled=True)]
    unnamed x9 -> x0, waiting for transfers between devices: 257 us -> none
    ppermute x0 -> x48, waiting for transfers between devices: none -> 243 us  [the longest x6 126 us: pipelined(): inner = lax.ppermute(own, 'col', INNER)]
    pallas_call x0 -> x18, Pallas kernels: none -> 201 us  [the longest x12 107 us: second_pair(): pl.pallas_call(second_pair_kernel, grid_spec=pltpu.PrefetchScalarGridSpec...]
    dot_general x3 -> x0, matrix products: 112 us -> none  [local(): jnp.dot(inverse_rows, lax.all_gather(right_side, 'col', axis=0, tiled=Tru...]
    unnamed x15 -> x10, local copies, waits for them, and re-layouts: 61.6 us -> 1 us
    ppermute x0 -> x48, starting transfers between devices: none -> 54 us  [the longest x6 17.5 us: pipelined(): inner = lax.ppermute(own, 'col', INNER)]
    convert_element_type x3 -> x10, other arithmetic: 18.2 us -> 9.65 us  [the longest x3 8.32 us: pipelined(): own = (hess_weight[:, part] + projected[chunk] - scaled[chunk]).astype(BF16)]
  transfers between devices with their start and end apart: 6 -> 48, of which waited for: 6 -> 15; matrix products, arithmetic and copies ran while one was open for 1% -> 0% of each run, Pallas kernels for 0% -> 39%
where the time goes in v1:
time: 517 us; the launch traced here: 515 us
  waiting for transfers between devices  243 us (47%)
  Pallas kernels  201 us (39%)
  starting transfers between devices  54 us (10%)
  other arithmetic  14.4 us (3%)
    ppermute x6, waiting for transfers between devices, pipelined(): inner = lax.ppermute(own, 'col', INNER)  126 us
    pallas_call x12, Pallas kernels, second_pair(): pl.pallas_call(second_pair_kernel, grid_spec=pltpu.PrefetchScalarGridSpec...  107 us
    pallas_call x6, Pallas kernels, first_pair(): pl.pallas_call(first_pair_kernel, grid_spec=pltpu.PrefetchScalarGridSpec(...  93.9 us
    ppermute x6, waiting for transfers between devices, pipelined(): iterate = near + lax.ppermute(far, 'row', ACROSS).astype(F32)  88.2 us
    ppermute x6, waiting for transfers between devices, pipelined(): outer = lax.ppermute(own, 'col', OUTER)  28.2 us
    ppermute x6, starting transfers between devices, pipelined(): inner = lax.ppermute(own, 'col', INNER)  17.5 us
  transfers between devices with their start and end apart: 48, of which 15 were waited for; matrix products, arithmetic and copies ran while one was open for 0% of the time, Pallas kernels for 39%

profile of v1, /device:TPU:16, one launch (start us, length us, event | category | flops | bytes accessed | tf_op | source)
XLA Modules:
  0.0 514.6 jit_solution(16418113365692754542)
XLA Ops:
  0.6 4.8 subtract_convert_fusion.5
  5.4 1.6 collective-permute-start
  7.0 1.9 collective-permute-start.1
  8.9 1.3 collective-permute-start.3
  10.2 3.9 collective-permute-start.25
  14.1 1.3 collective-permute-start.27
  15.6 8.4 %collective-permute-done.near = bf16[1344,256]{1,0:T(8,128)(2,1)} collective-permute-done((bf16[1344,256]{1,0:T(8,128)(2,1)}, bf16[1344,256]{1,0:T(8,128)(2,1)}, u32[]{:S(2)}, u32[]{:S(2)}) %collective-permute-start) | collective-permute-done | bytes 688160 | tf_op jit(solution)/shard_map/ppermute | solution.py:159
  24.5 32.4 %collective-permute-done.1.mid_a = bf16[1344,256]{1,0:T(8,128)(2,1)S(1)} collective-permute-done((bf16[1344,256]{1,0:T(8,128)(2,1)}, bf16[1344,256]{1,0:T(8,128)(2,1)S(1)}, u32[]{:S(2)}, u32[]{:S(2)}) %collective-permute-start.1) | collective-permute-done | bytes 688160 | tf_op jit(solution)/shard_map/ppermute | solution.py:160
  56.9 1.3 collective-permute-start.2
  58.3 1.3 collective-permute-start.4
  59.6 10.6 %collective-permute-done.25.mid_a = bf16[1344,256]{1,0:T(8,128)(2,1)S(1)} collective-permute-done((bf16[1344,256]{1,0:T(8,128)(2,1)S(1)}, bf16[1344,256]{1,0:T(8,128)(2,1)S(1)}, u32[]{:S(2)}, u32[]{:S(2)}) %collective-permute-start.25) | collective-permute-done | bytes 688160 | tf_op jit(solution)/shard_map/ppermute | solution.py:160
  70.2 1.3 collective-permute-start.26
  71.5 1.3 collective-permute-start.28
  72.9 16.6 %first_pair.6.before = f32[5376,256]{1,0:T(8,128)S(1)} custom-call(s32[2]{0:T(128)S(1)} %pad_add_fusion.2.place, bf16[5376,5376]{1,0:T(8,128)(2,1)} %matrix.35, bf16[1344,256]{1,0:T(8,128)(2,1)} %get-tuple-element.60.own, bf16[1344,256]{1,0:T(8,128)(2,1)} %collective-permute-done.near), custom_call_target="tpu_custom_call" | custom-call | flops 7398752256 | bytes 34406400 | tf_op jit(solution)/shard_map/first_pair/pallas_call | solution.py:43
  89.5 15.5 %first_pair.9.before = f32[5376,256]{1,0:T(8,128)S(1)} custom-call(s32[2]{0:T(128)S(1)} %pad_add_fusion.2.place, bf16[5376,5376]{1,0:T(8,128)(2,1)} %matrix.35, bf16[1344,256]{1,0:T(8,128)(2,1)S(1)} %get-tuple-element.61.own, bf16[1344,256]{1,0:T(8,128)(2,1)S(1)} %collective-permute-done.24.near), custom_call_target="tpu_custom_call" | custom-call | flops 7398752256 | bytes 34406400 | tf_op jit(solution)/shard_map/first_pair/pallas_call | solution.py:43
  105.0 8.9 %second_pair.13 = (bf16[1344,256]{1,0:T(8,128)(2,1)S(1)}, f32[1344,256]{1,0:T(8,128)S(1)}) custom-call(s32[4]{0:T(128)S(1)} %get-tuple-element.73.place, bf16[5376,5376]{1,0:T(8,128)(2,1)} %matrix.35, f32[5376,256]{1,0:T(8,128)S(1)} %first_pair.6.before, bf16[1344,256]{1,0:T(8,128)(2,1)S(1)} %collective-permute-done.2.end_a, ...), custom_call_target="tpu_custom_call" | custom-call | flops 3699376128 | bytes 19267584 | tf_op jit(solution)/shard_map/second_pair/pallas_call | solution.py:111
  114.0 8.9 %second_pair.12 = (bf16[1344,256]{1,0:T(8,128)(2,1)S(1)}, f32[1344,256]{1,0:T(8,128)S(1)}) custom-call(s32[4]{0:T(128)S(1)} %get-tuple-element.72.place, bf16[5376,5376]{1,0:T(8,128)(2,1)} %matrix.35, f32[5376,256]{1,0:T(8,128)S(1)} %first_pair.6.before, bf16[1344,256]{1,0:T(8,128)(2,1)S(1)} %collective-permute-done.2.end_a, ...), custom_call_target="tpu_custom_call" | custom-call | flops 3699376128 | bytes 19267584 | tf_op jit(solution)/shard_map/second_pair/pallas_call | solution.py:111
  123.5 8.9 %second_pair.19 = (bf16[1344,256]{1,0:T(8,128)(2,1)S(1)}, f32[1344,256]{1,0:T(8,128)S(1)}) custom-call(s32[4]{0:T(128)S(1)} %get-tuple-element.73.place, bf16[5376,5376]{1,0:T(8,128)(2,1)} %matrix.35, f32[5376,256]{1,0:T(8,128)S(1)} %first_pair.9.before, bf16[1344,256]{1,0:T(8,128)(2,1)S(1)} %collective-permute-done.26.end_a, ...), custom_call_target="tpu_custom_call" | custom-call | flops 3699376128 | bytes 19267584 | tf_op jit(solution)/shard_map/second_pair/pallas_call | solution.py:111
  132.6 8.9 %second_pair.18 = (bf16[1344,256]{1,0:T(8,128)(2,1)S(1)}, f32[1344,256]{1,0:T(8,128)S(1)}) custom-call(s32[4]{0:T(128)S(1)} %get-tuple-element.72.place, bf16[5376,5376]{1,0:T(8,128)(2,1)} %matrix.35, f32[5376,256]{1,0:T(8,128)S(1)} %first_pair.9.before, bf16[1344,256]{1,0:T(8,128)(2,1)S(1)} %collective-permute-done.26.end_a, ...), custom_call_target="tpu_custom_call" | custom-call | flops 3699376128 | bytes 19267584 | tf_op jit(solution)/shard_map/second_pair/pallas_call | solution.py:111
  142.2 1.6 collective-permute-start.7
  145.9 14.6 %collective-permute-done.7 = bf16[1344,256]{1,0:T(8,128)(2,1)S(1)} collective-permute-done((bf16[1344,256]{1,0:T(8,128)(2,1)S(1)}, bf16[1344,256]{1,0:T(8,128)(2,1)S(1)}, u32[]{:S(2)}, u32[]{:S(2)}) %collective-permute-start.7) | collective-permute-done | bytes 688160 | tf_op jit(solution)/shard_map/ppermute | solution.py:169
  160.6 13.8 %collective-permute-done.31 = bf16[1344,256]{1,0:T(8,128)(2,1)S(1)} collective-permute-done((bf16[1344,256]{1,0:T(8,128)(2,1)S(1)}, bf16[1344,256]{1,0:T(8,128)(2,1)S(1)}, u32[]{:S(2)}, u32[]{:S(2)}) %collective-permute-start.31) | collective-permute-done | bytes 688160 | tf_op jit(solution)/shard_map/ppermute | solution.py:169
  174.4 2.3 subtract_convert_fusion.4
  176.7 2.2 collective-permute-start.9
  178.9 1.3 collective-permute-start.11
  180.2 3.6 collective-permute-start.33
  183.8 1.3 collective-permute-start.35
  185.1 9.9 %collective-permute-done.8.near = bf16[1344,256]{1,0:T(8,128)(2,1)S(1)} collective-permute-done((bf16[1344,256]{1,0:T(8,128)(2,1)S(1)}, bf16[1344,256]{1,0:T(8,128)(2,1)S(1)}, u32[]{:S(2)}, u32[]{:S(2)}) %collective-permute-start.8) | collective-permute-done | bytes 688160 | tf_op jit(solution)/shard_map/ppermute | solution.py:159
  195.0 31.4 %collective-permute-done.9.mid_a = bf16[1344,256]{1,0:T(8,128)(2,1)S(1)} collective-permute-done((bf16[1344,256]{1,0:T(8,128)(2,1)S(1)}, bf16[1344,256]{1,0:T(8,128)(2,1)S(1)}, u32[]{:S(2)}, u32[]{:S(2)}) %collective-permute-start.9) | collective-permute-done | bytes 688160 | tf_op jit(solution)/shard_map/ppermute | solution.py:160
  226.4 1.3 collective-permute-start.10
  227.7 1.3 collective-permute-start.12
  229.1 10.2 %collective-permute-done.33.mid_a = bf16[1344,256]{1,0:T(8,128)(2,1)S(1)} collective-permute-done((bf16[1344,256]{1,0:T(8,128)(2,1)S(1)}, bf16[1344,256]{1,0:T(8,128)(2,1)S(1)}, u32[]{:S(2)}, u32[]{:S(2)}) %collective-permute-start.33) | collective-permute-done | bytes 688160 | tf_op jit(solution)/shard_map/ppermute | solution.py:160
  239.3 1.3 collective-permute-start.34
  240.7 1.5 collective-permute-start.36
  242.2 15.5 %first_pair.7.before = f32[5376,256]{1,0:T(8,128)S(1)} custom-call(s32[2]{0:T(128)S(1)} %pad_add_fusion.2.place, bf16[5376,5376]{1,0:T(8,128)(2,1)} %matrix.35, bf16[1344,256]{1,0:T(8,128)(2,1)S(1)} %get-tuple-element.52.own, bf16[1344,256]{1,0:T(8,128)(2,1)S(1)} %collective-permute-done.8.near), custom_call_target="tpu_custom_call" | custom-call | flops 7398752256 | bytes 34406400 | tf_op jit(solution)/shard_map/first_pair/pallas_call | solution.py:43
  257.7 15.5 %first_pair.10.before = f32[5376,256]{1,0:T(8,128)S(1)} custom-call(s32[2]{0:T(128)S(1)} %pad_add_fusion.2.place, bf16[5376,5376]{1,0:T(8,128)(2,1)} %matrix.35, bf16[1344,256]{1,0:T(8,128)(2,1)S(1)} %get-tuple-element.58.own, bf16[1344,256]{1,0:T(8,128)(2,1)S(1)} %collective-permute-done.32.near), custom_call_target="tpu_custom_call" | custom-call | flops 7398752256 | bytes 34406400 | tf_op jit(solution)/shard_map/first_pair/pallas_call | solution.py:43
  273.2 8.9 %second_pair.15 = (bf16[1344,256]{1,0:T(8,128)(2,1)S(1)}, f32[1344,256]{1,0:T(8,128)S(1)}) custom-call(s32[4]{0:T(128)S(1)} %get-tuple-element.73.place, bf16[5376,5376]{1,0:T(8,128)(2,1)} %matrix.35, f32[5376,256]{1,0:T(8,128)S(1)} %first_pair.7.before, bf16[1344,256]{1,0:T(8,128)(2,1)S(1)} %collective-permute-done.10.end_a, ...), custom_call_target="tpu_custom_call" | custom-call | flops 3699376128 | bytes 19267584 | tf_op jit(solution)/shard_map/second_pair/pallas_call | solution.py:111
  282.2 8.9 %second_pair.14 = (bf16[1344,256]{1,0:T(8,128)(2,1)S(1)}, f32[1344,256]{1,0:T(8,128)S(1)}) custom-call(s32[4]{0:T(128)S(1)} %get-tuple-element.72.place, bf16[5376,5376]{1,0:T(8,128)(2,1)} %matrix.35, f32[5376,256]{1,0:T(8,128)S(1)} %first_pair.7.before, bf16[1344,256]{1,0:T(8,128)(2,1)S(1)} %collective-permute-done.10.end_a, ...), custom_call_target="tpu_custom_call" | custom-call | flops 3699376128 | bytes 19267584 | tf_op jit(solution)/shard_map/second_pair/pallas_call | solution.py:111
  291.7 8.9 %second_pair.21 = (bf16[1344,256]{1,0:T(8,128)(2,1)S(1)}, f32[1344,256]{1,0:T(8,128)S(1)}) custom-call(s32[4]{0:T(128)S(1)} %get-tuple-element.73.place, bf16[5376,5376]{1,0:T(8,128)(2,1)} %matrix.35, f32[5376,256]{1,0:T(8,128)S(1)} %first_pair.10.before, bf16[1344,256]{1,0:T(8,128)(2,1)S(1)} %collective-permute-done.34.end_a, ...), custom_call_target="tpu_custom_call" | custom-call | flops 3699376128 | bytes 19267584 | tf_op jit(solution)/shard_map/second_pair/pallas_call | solution.py:111
  300.7 8.9 %second_pair.20 = (bf16[1344,256]{1,0:T(8,128)(2,1)S(1)}, f32[1344,256]{1,0:T(8,128)S(1)}) custom-call(s32[4]{0:T(128)S(1)} %get-tuple-element.72.place, bf16[5376,5376]{1,0:T(8,128)(2,1)} %matrix.35, f32[5376,256]{1,0:T(8,128)S(1)} %first_pair.10.before, bf16[1344,256]{1,0:T(8,128)(2,1)S(1)} %collective-permute-done.34.end_a, ...), custom_call_target="tpu_custom_call" | custom-call | flops 3699376128 | bytes 19267584 | tf_op jit(solution)/shard_map/second_pair/pallas_call | solution.py:111
  310.4 1.6 collective-permute-start.15
  312.7 16.0 %collective-permute-done.15 = bf16[1344,256]{1,0:T(8,128)(2,1)S(1)} collective-permute-done((bf16[1344,256]{1,0:T(8,128)(2,1)S(1)}, bf16[1344,256]{1,0:T(8,128)(2,1)S(1)}, u32[]{:S(2)}, u32[]{:S(2)}) %collective-permute-start.15) | collective-permute-done | bytes 688160 | tf_op jit(solution)/shard_map/ppermute | solution.py:169
  328.7 13.8 %collective-permute-done.39 = bf16[1344,256]{1,0:T(8,128)(2,1)S(1)} collective-permute-done((bf16[1344,256]{1,0:T(8,128)(2,1)S(1)}, bf16[1344,256]{1,0:T(8,128)(2,1)S(1)}, u32[]{:S(2)}, u32[]{:S(2)}) %collective-permute-start.39) | collective-permute-done | bytes 688160 | tf_op jit(solution)/shard_map/ppermute | solution.py:169
  342.6 1.3 subtract_convert_fusion.3
  343.9 2.2 collective-permute-start.17
  347.5 3.6 collective-permute-start.41
  352.4 9.9 %collective-permute-done.16.near = bf16[1344,256]{1,0:T(8,128)(2,1)S(1)} collective-permute-done((bf16[1344,256]{1,0:T(8,128)(2,1)S(1)}, bf16[1344,256]{1,0:T(8,128)(2,1)S(1)}, u32[]{:S(2)}, u32[]{:S(2)}) %collective-permute-start.16) | collective-permute-done | bytes 688160 | tf_op jit(solution)/shard_map/ppermute | solution.py:159
  362.3 31.4 %collective-permute-done.17.mid_a = bf16[1344,256]{1,0:T(8,128)(2,1)S(1)} collective-permute-done((bf16[1344,256]{1,0:T(8,128)(2,1)S(1)}, bf16[1344,256]{1,0:T(8,128)(2,1)S(1)}, u32[]{:S(2)}, u32[]{:S(2)}) %collective-permute-start.17) | collective-permute-done | bytes 688160 | tf_op jit(solution)/shard_map/ppermute | solution.py:160
  393.7 1.3 collective-permute-start.18
  395.0 1.3 collective-permute-start.20
  396.4 10.2 %collective-permute-done.41.mid_a = bf16[1344,256]{1,0:T(8,128)(2,1)S(1)} collective-permute-done((bf16[1344,256]{1,0:T(8,128)(2,1)S(1)}, bf16[1344,256]{1,0:T(8,128)(2,1)S(1)}, u32[]{:S(2)}, u32[]{:S(2)}) %collective-permute-start.41) | collective-permute-done | bytes 688160 | tf_op jit(solution)/shard_map/ppermute | solution.py:160
  406.6 1.3 collective-permute-start.42
  407.9 1.6 collective-permute-start.44
  409.5 15.5 %first_pair.8.before = f32[5376,256]{1,0:T(8,128)S(1)} custom-call(s32[2]{0:T(128)S(1)} %pad_add_fusion.2.place, bf16[5376,5376]{1,0:T(8,128)(2,1)} %matrix.35, bf16[1344,256]{1,0:T(8,128)(2,1)S(1)} %get-tuple-element.50.own, bf16[1344,256]{1,0:T(8,128)(2,1)S(1)} %collective-permute-done.16.near), custom_call_target="tpu_custom_call" | custom-call | flops 7398752256 | bytes 34406400 | tf_op jit(solution)/shard_map/first_pair/pallas_call | solution.py:43
  425.0 15.5 %first_pair.11.before = f32[5376,256]{1,0:T(8,128)S(1)} custom-call(s32[2]{0:T(128)S(1)} %pad_add_fusion.2.place, bf16[5376,5376]{1,0:T(8,128)(2,1)} %matrix.35, bf16[1344,256]{1,0:T(8,128)(2,1)S(1)} %get-tuple-element.66.own, bf16[1344,256]{1,0:T(8,128)(2,1)S(1)} %collective-permute-done.40.near), custom_call_target="tpu_custom_call" | custom-call | flops 7398752256 | bytes 34406400 | tf_op jit(solution)/shard_map/first_pair/pallas_call | solution.py:43
  440.5 8.9 %second_pair.17 = (bf16[1344,256]{1,0:T(8,128)(2,1)S(1)}, f32[1344,256]{1,0:T(8,128)S(1)}) custom-call(s32[4]{0:T(128)S(1)} %get-tuple-element.73.place, bf16[5376,5376]{1,0:T(8,128)(2,1)} %matrix.35, f32[5376,256]{1,0:T(8,128)S(1)} %first_pair.8.before, bf16[1344,256]{1,0:T(8,128)(2,1)S(1)} %collective-permute-done.18.end_a, ...), custom_call_target="tpu_custom_call" | custom-call | flops 3699376128 | bytes 19267584 | tf_op jit(solution)/shard_map/second_pair/pallas_call | solution.py:111
  449.5 8.9 %second_pair.16 = (bf16[1344,256]{1,0:T(8,128)(2,1)S(1)}, f32[1344,256]{1,0:T(8,128)S(1)}) custom-call(s32[4]{0:T(128)S(1)} %get-tuple-element.72.place, bf16[5376,5376]{1,0:T(8,128)(2,1)} %matrix.35, f32[5376,256]{1,0:T(8,128)S(1)} %first_pair.8.before, bf16[1344,256]{1,0:T(8,128)(2,1)S(1)} %collective-permute-done.18.end_a, ...), custom_call_target="tpu_custom_call" | custom-call | flops 3699376128 | bytes 19267584 | tf_op jit(solution)/shard_map/second_pair/pallas_call | solution.py:111
  459.0 8.9 %second_pair.23 = (bf16[1344,256]{1,0:T(8,128)(2,1)S(1)}, f32[1344,256]{1,0:T(8,128)S(1)}) custom-call(s32[4]{0:T(128)S(1)} %get-tuple-element.73.place, bf16[5376,5376]{1,0:T(8,128)(2,1)} %matrix.35, f32[5376,256]{1,0:T(8,128)S(1)} %first_pair.11.before, bf16[1344,256]{1,0:T(8,128)(2,1)S(1)} %collective-permute-done.42.end_a, ...), custom_call_target="tpu_custom_call" | custom-call | flops 3699376128 | bytes 19267584 | tf_op jit(solution)/shard_map/second_pair/pallas_call | solution.py:111
  468.1 8.9 %second_pair.22 = (bf16[1344,256]{1,0:T(8,128)(2,1)S(1)}, f32[1344,256]{1,0:T(8,128)S(1)}) custom-call(s32[4]{0:T(128)S(1)} %get-tuple-element.72.place, bf16[5376,5376]{1,0:T(8,128)(2,1)} %matrix.35, f32[5376,256]{1,0:T(8,128)S(1)} %first_pair.11.before, bf16[1344,256]{1,0:T(8,128)(2,1)S(1)} %collective-permute-done.42.end_a, ...), custom_call_target="tpu_custom_call" | custom-call | flops 3699376128 | bytes 19267584 | tf_op jit(solution)/shard_map/second_pair/pallas_call | solution.py:111
  477.7 1.6 collective-permute-start.23
  480.1 16.0 %collective-permute-done.23 = bf16[1344,256]{1,0:T(8,128)(2,1)S(1)} collective-permute-done((bf16[1344,256]{1,0:T(8,128)(2,1)S(1)}, bf16[1344,256]{1,0:T(8,128)(2,1)S(1)}, u32[]{:S(2)}, u32[]{:S(2)}) %collective-permute-start.23) | collective-permute-done | bytes 688160 | tf_op jit(solution)/shard_map/ppermute | solution.py:169
  496.1 13.8 %collective-permute-done.47 = bf16[1344,256]{1,0:T(8,128)(2,1)S(1)} collective-permute-done((bf16[1344,256]{1,0:T(8,128)(2,1)S(1)}, bf16[1344,256]{1,0:T(8,128)(2,1)S(1)}, u32[]{:S(2)}, u32[]{:S(2)}) %collective-permute-start.47) | collective-permute-done | bytes 688160 | tf_op jit(solution)/shard_map/ppermute | solution.py:169
  510.8 1.9 pad_maximum_fusion
  512.7 1.9 pad_maximum_fusion.1
  (77 shorter events, 12.2 us)
Async XLA Ops:
  5.4 18.6 %collective-permute-start = (bf16[1344,256]{1,0:T(8,128)(2,1)}, bf16[1344,256]{1,0:T(8,128)(2,1)}, u32[]{:S(2)}, u32[]{:S(2)}) collective-permute-start(bf16[1344,256]{1,0:T(8,128)(2,1)} %get-tuple-element.60.own), channel_id=1, source_target_pairs={{0,1},{1,0},{2,3},{3,2},{4,5},{5,4},{6,7},{7,6},{8,9},{9,8},{10,11... | collective-permute-start | bytes 2064392 | tf_op jit(solution)/shard_map/ppermute | solution.py:159
  7.0 49.9 %collective-permute-start.1 = (bf16[1344,256]{1,0:T(8,128)(2,1)}, bf16[1344,256]{1,0:T(8,128)(2,1)S(1)}, u32[]{:S(2)}, u32[]{:S(2)}) collective-permute-start(bf16[1344,256]{1,0:T(8,128)(2,1)} %get-tuple-element.60.own), channel_id=1, source_target_pairs={{1,2},{2,1},{5,6},{6,5},{9,10},{10,9},{13,14},{14,13},{17,18},{18,... | collective-permute-start | bytes 2064392 | tf_op jit(solution)/shard_map/ppermute | solution.py:160
  8.9 49.4 %collective-permute-start.3 = (bf16[1344,256]{1,0:T(8,128)(2,1)}, bf16[1344,256]{1,0:T(8,128)(2,1)S(1)}, u32[]{:S(2)}, u32[]{:S(2)}) collective-permute-start(bf16[1344,256]{1,0:T(8,128)(2,1)} %get-tuple-element.60.own), channel_id=1, source_target_pairs={{0,2},{3,1},{4,6},{7,5},{8,10},{11,9},{12,14},{15,13},{16,18},{19,... | collective-permute-start | bytes 2064392 | tf_op jit(solution)/shard_map/ppermute | solution.py:161
  10.2 60.0 %collective-permute-start.25 = (bf16[1344,256]{1,0:T(8,128)(2,1)S(1)}, bf16[1344,256]{1,0:T(8,128)(2,1)S(1)}, u32[]{:S(2)}, u32[]{:S(2)}) collective-permute-start(bf16[1344,256]{1,0:T(8,128)(2,1)S(1)} %get-tuple-element.61.own), channel_id=1, source_target_pairs={{1,2},{2,1},{5,6},{6,5},{9,10},{10,9},{13,14},{14,13},{17,18},{18,... | collective-permute-start | bytes 2064392 | tf_op jit(solution)/shard_map/ppermute | solution.py:160
  14.1 57.4 %collective-permute-start.27 = (bf16[1344,256]{1,0:T(8,128)(2,1)S(1)}, bf16[1344,256]{1,0:T(8,128)(2,1)S(1)}, u32[]{:S(2)}, u32[]{:S(2)}) collective-permute-start(bf16[1344,256]{1,0:T(8,128)(2,1)S(1)} %get-tuple-element.61.own), channel_id=1, source_target_pairs={{0,2},{3,1},{4,6},{7,5},{8,10},{11,9},{12,14},{15,13},{16,18},{19,... | collective-permute-start | bytes 2064392 | tf_op jit(solution)/shard_map/ppermute | solution.py:161
  24.0 65.4 %collective-permute-start.24 = (bf16[1344,256]{1,0:T(8,128)(2,1)S(1)}, bf16[1344,256]{1,0:T(8,128)(2,1)S(1)}, u32[]{:S(2)}, u32[]{:S(2)}) collective-permute-start(bf16[1344,256]{1,0:T(8,128)(2,1)S(1)} %get-tuple-element.61.own), channel_id=1, source_target_pairs={{0,1},{1,0},{2,3},{3,2},{4,5},{5,4},{6,7},{7,6},{8,9},{9,8},{10,11... | collective-permute-start | bytes 2064392 | tf_op jit(solution)/shard_map/ppermute | solution.py:159
  56.9 48.0 %collective-permute-start.2 = (bf16[1344,256]{1,0:T(8,128)(2,1)S(1)}, bf16[1344,256]{1,0:T(8,128)(2,1)S(1)}, u32[]{:S(2)}, u32[]{:S(2)}) collective-permute-start(bf16[1344,256]{1,0:T(8,128)(2,1)S(1)} %collective-permute-done.1.mid_a), channel_id=1, source_target_pairs={{1,0},{2,3},{5,4},{6,7},{9,8},{10,11},{13,12},{14,15},{17,16},{18,... | collective-permute-start | bytes 2064392 | tf_op jit(solution)/shard_map/ppermute | solution.py:162
  58.3 46.7 %collective-permute-start.4 = (bf16[1344,256]{1,0:T(8,128)(2,1)S(1)}, bf16[1344,256]{1,0:T(8,128)(2,1)S(1)}, u32[]{:S(2)}, u32[]{:S(2)}) collective-permute-start(bf16[1344,256]{1,0:T(8,128)(2,1)S(1)} %collective-permute-done.3.mid_b), channel_id=1, source_target_pairs={{1,0},{2,3},{5,4},{6,7},{9,8},{10,11},{13,12},{14,15},{17,16},{18,... | collective-permute-start | bytes 2064392 | tf_op jit(solution)/shard_map/ppermute | solution.py:163
  70.2 53.3 %collective-permute-start.26 = (bf16[1344,256]{1,0:T(8,128)(2,1)S(1)}, bf16[1344,256]{1,0:T(8,128)(2,1)S(1)}, u32[]{:S(2)}, u32[]{:S(2)}) collective-permute-start(bf16[1344,256]{1,0:T(8,128)(2,1)S(1)} %collective-permute-done.25.mid_a), channel_id=1, source_target_pairs={{1,0},{2,3},{5,4},{6,7},{9,8},{10,11},{13,12},{14,15},{17,16},{18,... | collective-permute-start | bytes 2064392 | tf_op jit(solution)/shard_map/ppermute | solution.py:162
  71.5 52.0 %collective-permute-start.28 = (bf16[1344,256]{1,0:T(8,128)(2,1)S(1)}, bf16[1344,256]{1,0:T(8,128)(2,1)S(1)}, u32[]{:S(2)}, u32[]{:S(2)}) collective-permute-start(bf16[1344,256]{1,0:T(8,128)(2,1)S(1)} %collective-permute-done.27.mid_b), channel_id=1, source_target_pairs={{1,0},{2,3},{5,4},{6,7},{9,8},{10,11},{13,12},{14,15},{17,16},{18,... | collective-permute-start | bytes 2064392 | tf_op jit(solution)/shard_map/ppermute | solution.py:163
  113.9 28.1 %collective-permute-start.6 = (bf16[1344,256]{1,0:T(8,128)(2,1)S(1)}, bf16[1344,256]{1,0:T(8,128)(2,1)S(1)}, u32[]{:S(2)}, u32[]{:S(2)}) collective-permute-start(bf16[1344,256]{1,0:T(8,128)(2,1)S(1)} %get-tuple-element.29), channel_id=1, source_target_pairs={{0,4},{4,0},{8,12},{12,8},{1,5},{5,1},{9,13},{13,9},{2,6},{6,2},{1... | collective-permute-start | bytes 2064392 | tf_op jit(solution)/shard_map/ppermute | solution.py:166
  123.0 23.0 %collective-permute-start.5 = (bf16[1344,256]{1,0:T(8,128)(2,1)S(1)}, bf16[1344,256]{1,0:T(8,128)(2,1)S(1)}, u32[]{:S(2)}, u32[]{:S(2)}) collective-permute-start(bf16[1344,256]{1,0:T(8,128)(2,1)S(1)} %get-tuple-element.27), channel_id=1, source_target_pairs={{0,4},{4,0},{8,12},{12,8},{1,5},{5,1},{9,13},{13,9},{2,6},{6,2},{1... | collective-permute-start | bytes 2064392 | tf_op jit(solution)/shard_map/ppermute | solution.py:168
  132.5 11.3 %collective-permute-start.30 = (bf16[1344,256]{1,0:T(8,128)(2,1)S(1)}, bf16[1344,256]{1,0:T(8,128)(2,1)S(1)}, u32[]{:S(2)}, u32[]{:S(2)}) collective-permute-start(bf16[1344,256]{1,0:T(8,128)(2,1)S(1)} %get-tuple-element.41), channel_id=1, source_target_pairs={{0,4},{4,0},{8,12},{12,8},{1,5},{5,1},{9,13},{13,9},{2,6},{6,2},{1... | collective-permute-start | bytes 2064392 | tf_op jit(solution)/shard_map/ppermute | solution.py:166
  141.5 4.4 collective-permute-start.29
  142.2 18.4 %collective-permute-start.7 = (bf16[1344,256]{1,0:T(8,128)(2,1)S(1)}, bf16[1344,256]{1,0:T(8,128)(2,1)S(1)}, u32[]{:S(2)}, u32[]{:S(2)}) collective-permute-start(bf16[1344,256]{1,0:T(8,128)(2,1)S(1)} %add_convert_fusion.5), channel_id=1, source_target_pairs={{0,8},{8,0},{4,12},{12,4},{1,9},{9,1},{5,13},{13,5},{2,10},{10,2},... | collective-permute-start | bytes 2064392 | tf_op jit(solution)/shard_map/ppermute | solution.py:169
  143.8 1.8 copy-start.3
  143.9 1.9 copy-start.4
  144.0 30.4 %collective-permute-start.31 = (bf16[1344,256]{1,0:T(8,128)(2,1)S(1)}, bf16[1344,256]{1,0:T(8,128)(2,1)S(1)}, u32[]{:S(2)}, u32[]{:S(2)}) collective-permute-start(bf16[1344,256]{1,0:T(8,128)(2,1)S(1)} %add_convert_fusion.2), channel_id=1, source_target_pairs={{0,8},{8,0},{4,12},{12,4},{1,9},{9,1},{5,13},{13,5},{2,10},{10,2},... | collective-permute-start | bytes 2064392 | tf_op jit(solution)/shard_map/ppermute | solution.py:169
  145.6 28.9 %copy-start = (f32[1344,512]{1,0:T(8,128)S(1)}, f32[1344,512]{1,0:T(8,128)}, u32[]{:S(2)}) copy-start(f32[1344,512]{1,0:T(8,128)} %param.7) | copy-start | bytes 8257540
  145.6 28.9 %copy-start.1 = (f32[1344,512]{1,0:T(8,128)S(1)}, f32[1344,512]{1,0:T(8,128)}, u32[]{:S(2)}) copy-start(f32[1344,512]{1,0:T(8,128)} %param.9) | copy-start | bytes 8257540
  176.7 18.4 %collective-permute-start.8 = (bf16[1344,256]{1,0:T(8,128)(2,1)S(1)}, bf16[1344,256]{1,0:T(8,128)(2,1)S(1)}, u32[]{:S(2)}, u32[]{:S(2)}) collective-permute-start(bf16[1344,256]{1,0:T(8,128)(2,1)S(1)} %get-tuple-element.52.own), channel_id=1, source_target_pairs={{0,1},{1,0},{2,3},{3,2},{4,5},{5,4},{6,7},{7,6},{8,9},{9,8},{10,11... | collective-permute-start | bytes 2064392 | tf_op jit(solution)/shard_map/ppermute | solution.py:159
  176.7 49.7 %collective-permute-start.9 = (bf16[1344,256]{1,0:T(8,128)(2,1)S(1)}, bf16[1344,256]{1,0:T(8,128)(2,1)S(1)}, u32[]{:S(2)}, u32[]{:S(2)}) collective-permute-start(bf16[1344,256]{1,0:T(8,128)(2,1)S(1)} %get-tuple-element.52.own), channel_id=1, source_target_pairs={{1,2},{2,1},{5,6},{6,5},{9,10},{10,9},{13,14},{14,13},{17,18},{18,... | collective-permute-start | bytes 2064392 | tf_op jit(solution)/shard_map/ppermute | solution.py:160
  178.9 48.9 %collective-permute-start.11 = (bf16[1344,256]{1,0:T(8,128)(2,1)S(1)}, bf16[1344,256]{1,0:T(8,128)(2,1)S(1)}, u32[]{:S(2)}, u32[]{:S(2)}) collective-permute-start(bf16[1344,256]{1,0:T(8,128)(2,1)S(1)} %get-tuple-element.52.own), channel_id=1, source_target_pairs={{0,2},{3,1},{4,6},{7,5},{8,10},{11,9},{12,14},{15,13},{16,18},{19,... | collective-permute-start | bytes 2064392 | tf_op jit(solution)/shard_map/ppermute | solution.py:161
  180.2 59.2 %collective-permute-start.33 = (bf16[1344,256]{1,0:T(8,128)(2,1)S(1)}, bf16[1344,256]{1,0:T(8,128)(2,1)S(1)}, u32[]{:S(2)}, u32[]{:S(2)}) collective-permute-start(bf16[1344,256]{1,0:T(8,128)(2,1)S(1)} %get-tuple-element.58.own), channel_id=1, source_target_pairs={{1,2},{2,1},{5,6},{6,5},{9,10},{10,9},{13,14},{14,13},{17,18},{18,... | collective-permute-start | bytes 2064392 | tf_op jit(solution)/shard_map/ppermute | solution.py:160
  183.8 56.8 %collective-permute-start.35 = (bf16[1344,256]{1,0:T(8,128)(2,1)S(1)}, bf16[1344,256]{1,0:T(8,128)(2,1)S(1)}, u32[]{:S(2)}, u32[]{:S(2)}) collective-permute-start(bf16[1344,256]{1,0:T(8,128)(2,1)S(1)} %get-tuple-element.58.own), channel_id=1, source_target_pairs={{0,2},{3,1},{4,6},{7,5},{8,10},{11,9},{12,14},{15,13},{16,18},{19,... | collective-permute-start | bytes 2064392 | tf_op jit(solution)/shard_map/ppermute | solution.py:161
  195.0 62.6 %collective-permute-start.32 = (bf16[1344,256]{1,0:T(8,128)(2,1)S(1)}, bf16[1344,256]{1,0:T(8,128)(2,1)S(1)}, u32[]{:S(2)}, u32[]{:S(2)}) collective-permute-start(bf16[1344,256]{1,0:T(8,128)(2,1)S(1)} %get-tuple-element.58.own), channel_id=1, source_target_pairs={{0,1},{1,0},{2,3},{3,2},{4,5},{5,4},{6,7},{7,6},{8,9},{9,8},{10,11... | collective-permute-start | bytes 2064392 | tf_op jit(solution)/shard_map/ppermute | solution.py:159
  226.4 46.7 %collective-permute-start.10 = (bf16[1344,256]{1,0:T(8,128)(2,1)S(1)}, bf16[1344,256]{1,0:T(8,128)(2,1)S(1)}, u32[]{:S(2)}, u32[]{:S(2)}) collective-permute-start(bf16[1344,256]{1,0:T(8,128)(2,1)S(1)} %collective-permute-done.9.mid_a), channel_id=1, source_target_pairs={{1,0},{2,3},{5,4},{6,7},{9,8},{10,11},{13,12},{14,15},{17,16},{18,... | collective-permute-start | bytes 2064392 | tf_op jit(solution)/shard_map/ppermute | solution.py:162
  227.7 45.4 %collective-permute-start.12 = (bf16[1344,256]{1,0:T(8,128)(2,1)S(1)}, bf16[1344,256]{1,0:T(8,128)(2,1)S(1)}, u32[]{:S(2)}, u32[]{:S(2)}) collective-permute-start(bf16[1344,256]{1,0:T(8,128)(2,1)S(1)} %collective-permute-done.11.mid_b), channel_id=1, source_target_pairs={{1,0},{2,3},{5,4},{6,7},{9,8},{10,11},{13,12},{14,15},{17,16},{18,... | collective-permute-start | bytes 2064392 | tf_op jit(solution)/shard_map/ppermute | solution.py:163
  239.3 52.4 %collective-permute-start.34 = (bf16[1344,256]{1,0:T(8,128)(2,1)S(1)}, bf16[1344,256]{1,0:T(8,128)(2,1)S(1)}, u32[]{:S(2)}, u32[]{:S(2)}) collective-permute-start(bf16[1344,256]{1,0:T(8,128)(2,1)S(1)} %collective-permute-done.33.mid_a), channel_id=1, source_target_pairs={{1,0},{2,3},{5,4},{6,7},{9,8},{10,11},{13,12},{14,15},{17,16},{18,... | collective-permute-start | bytes 2064392 | tf_op jit(solution)/shard_map/ppermute | solution.py:162
  240.7 51.0 %collective-permute-start.36 = (bf16[1344,256]{1,0:T(8,128)(2,1)S(1)}, bf16[1344,256]{1,0:T(8,128)(2,1)S(1)}, u32[]{:S(2)}, u32[]{:S(2)}) collective-permute-start(bf16[1344,256]{1,0:T(8,128)(2,1)S(1)} %collective-permute-done.35.mid_b), channel_id=1, source_target_pairs={{1,0},{2,3},{5,4},{6,7},{9,8},{10,11},{13,12},{14,15},{17,16},{18,... | collective-permute-start | bytes 2064392 | tf_op jit(solution)/shard_map/ppermute | solution.py:163
  282.1 28.1 %collective-permute-start.14 = (bf16[1344,256]{1,0:T(8,128)(2,1)S(1)}, bf16[1344,256]{1,0:T(8,128)(2,1)S(1)}, u32[]{:S(2)}, u32[]{:S(2)}) collective-permute-start(bf16[1344,256]{1,0:T(8,128)(2,1)S(1)} %get-tuple-element.33), channel_id=1, source_target_pairs={{0,4},{4,0},{8,12},{12,8},{1,5},{5,1},{9,13},{13,9},{2,6},{6,2},{1... | collective-permute-start | bytes 2064392 | tf_op jit(solution)/shard_map/ppermute | solution.py:166
  291.1 21.6 %collective-permute-start.13 = (bf16[1344,256]{1,0:T(8,128)(2,1)S(1)}, bf16[1344,256]{1,0:T(8,128)(2,1)S(1)}, u32[]{:S(2)}, u32[]{:S(2)}) collective-permute-start(bf16[1344,256]{1,0:T(8,128)(2,1)S(1)} %get-tuple-element.31), channel_id=1, source_target_pairs={{0,4},{4,0},{8,12},{12,8},{1,5},{5,1},{9,13},{13,9},{2,6},{6,2},{1... | collective-permute-start | bytes 2064392 | tf_op jit(solution)/shard_map/ppermute | solution.py:168
  300.6 11.3 %collective-permute-start.38 = (bf16[1344,256]{1,0:T(8,128)(2,1)S(1)}, bf16[1344,256]{1,0:T(8,128)(2,1)S(1)}, u32[]{:S(2)}, u32[]{:S(2)}) collective-permute-start(bf16[1344,256]{1,0:T(8,128)(2,1)S(1)} %get-tuple-element.45), channel_id=1, source_target_pairs={{0,4},{4,0},{8,12},{12,8},{1,5},{5,1},{9,13},{13,9},{2,6},{6,2},{1... | collective-permute-start | bytes 2064392 | tf_op jit(solution)/shard_map/ppermute | solution.py:166
  309.7 3.1 collective-permute-start.37
  310.4 18.4 %collective-permute-start.15 = (bf16[1344,256]{1,0:T(8,128)(2,1)S(1)}, bf16[1344,256]{1,0:T(8,128)(2,1)S(1)}, u32[]{:S(2)}, u32[]{:S(2)}) collective-permute-start(bf16[1344,256]{1,0:T(8,128)(2,1)S(1)} %add_convert_fusion.4), channel_id=1, source_target_pairs={{0,8},{8,0},{4,12},{12,4},{1,9},{9,1},{5,13},{13,5},{2,10},{10,2},... | collective-permute-start | bytes 2064392 | tf_op jit(solution)/shard_map/ppermute | solution.py:169
  311.9 30.6 %copy-start.2 = (f32[1344,256]{1,0:T(8,128)S(1)}, f32[1344,256]{1,0:T(8,128)}, u32[]{:S(2)}) copy-start(f32[1344,256]{1,0:T(8,128)} %get-tuple-element.59) | copy-start | bytes 4128772
  312.1 30.5 %collective-permute-start.39 = (bf16[1344,256]{1,0:T(8,128)(2,1)S(1)}, bf16[1344,256]{1,0:T(8,128)(2,1)S(1)}, u32[]{:S(2)}, u32[]{:S(2)}) collective-permute-start(bf16[1344,256]{1,0:T(8,128)(2,1)S(1)} %add_convert_fusion.1), channel_id=1, source_target_pairs={{0,8},{8,0},{4,12},{12,4},{1,9},{9,1},{5,13},{13,5},{2,10},{10,2},... | collective-permute-start | bytes 2064392 | tf_op jit(solution)/shard_map/ppermute | solution.py:169
  343.9 18.4 %collective-permute-start.16 = (bf16[1344,256]{1,0:T(8,128)(2,1)S(1)}, bf16[1344,256]{1,0:T(8,128)(2,1)S(1)}, u32[]{:S(2)}, u32[]{:S(2)}) collective-permute-start(bf16[1344,256]{1,0:T(8,128)(2,1)S(1)} %get-tuple-element.50.own), channel_id=1, source_target_pairs={{0,1},{1,0},{2,3},{3,2},{4,5},{5,4},{6,7},{7,6},{8,9},{9,8},{10,11... | collective-permute-start | bytes 2064392 | tf_op jit(solution)/shard_map/ppermute | solution.py:159
  343.9 49.8 %collective-permute-start.17 = (bf16[1344,256]{1,0:T(8,128)(2,1)S(1)}, bf16[1344,256]{1,0:T(8,128)(2,1)S(1)}, u32[]{:S(2)}, u32[]{:S(2)}) collective-permute-start(bf16[1344,256]{1,0:T(8,128)(2,1)S(1)} %get-tuple-element.50.own), channel_id=1, source_target_pairs={{1,2},{2,1},{5,6},{6,5},{9,10},{10,9},{13,14},{14,13},{17,18},{18,... | collective-permute-start | bytes 2064392 | tf_op jit(solution)/shard_map/ppermute | solution.py:160
  346.2 48.9 %collective-permute-start.19 = (bf16[1344,256]{1,0:T(8,128)(2,1)S(1)}, bf16[1344,256]{1,0:T(8,128)(2,1)S(1)}, u32[]{:S(2)}, u32[]{:S(2)}) collective-permute-start(bf16[1344,256]{1,0:T(8,128)(2,1)S(1)} %get-tuple-element.50.own), channel_id=1, source_target_pairs={{0,2},{3,1},{4,6},{7,5},{8,10},{11,9},{12,14},{15,13},{16,18},{19,... | collective-permute-start | bytes 2064392 | tf_op jit(solution)/shard_map/ppermute | solution.py:161
  347.5 59.1 %collective-permute-start.41 = (bf16[1344,256]{1,0:T(8,128)(2,1)S(1)}, bf16[1344,256]{1,0:T(8,128)(2,1)S(1)}, u32[]{:S(2)}, u32[]{:S(2)}) collective-permute-start(bf16[1344,256]{1,0:T(8,128)(2,1)S(1)} %get-tuple-element.66.own), channel_id=1, source_target_pairs={{1,2},{2,1},{5,6},{6,5},{9,10},{10,9},{13,14},{14,13},{17,18},{18,... | collective-permute-start | bytes 2064392 | tf_op jit(solution)/shard_map/ppermute | solution.py:160
  351.1 56.8 %collective-permute-start.43 = (bf16[1344,256]{1,0:T(8,128)(2,1)S(1)}, bf16[1344,256]{1,0:T(8,128)(2,1)S(1)}, u32[]{:S(2)}, u32[]{:S(2)}) collective-permute-start(bf16[1344,256]{1,0:T(8,128)(2,1)S(1)} %get-tuple-element.66.own), channel_id=1, source_target_pairs={{0,2},{3,1},{4,6},{7,5},{8,10},{11,9},{12,14},{15,13},{16,18},{19,... | collective-permute-start | bytes 2064392 | tf_op jit(solution)/shard_map/ppermute | solution.py:161
  362.3 62.7 %collective-permute-start.40 = (bf16[1344,256]{1,0:T(8,128)(2,1)S(1)}, bf16[1344,256]{1,0:T(8,128)(2,1)S(1)}, u32[]{:S(2)}, u32[]{:S(2)}) collective-permute-start(bf16[1344,256]{1,0:T(8,128)(2,1)S(1)} %get-tuple-element.66.own), channel_id=1, source_target_pairs={{0,1},{1,0},{2,3},{3,2},{4,5},{5,4},{6,7},{7,6},{8,9},{9,8},{10,11... | collective-permute-start | bytes 2064392 | tf_op jit(solution)/shard_map/ppermute | solution.py:159
  393.7 46.8 %collective-permute-start.18 = (bf16[1344,256]{1,0:T(8,128)(2,1)S(1)}, bf16[1344,256]{1,0:T(8,128)(2,1)S(1)}, u32[]{:S(2)}, u32[]{:S(2)}) collective-permute-start(bf16[1344,256]{1,0:T(8,128)(2,1)S(1)} %collective-permute-done.17.mid_a), channel_id=1, source_target_pairs={{1,0},{2,3},{5,4},{6,7},{9,8},{10,11},{13,12},{14,15},{17,16},{18,... | collective-permute-start | bytes 2064392 | tf_op jit(solution)/shard_map/ppermute | solution.py:162
  395.0 45.4 %collective-permute-start.20 = (bf16[1344,256]{1,0:T(8,128)(2,1)S(1)}, bf16[1344,256]{1,0:T(8,128)(2,1)S(1)}, u32[]{:S(2)}, u32[]{:S(2)}) collective-permute-start(bf16[1344,256]{1,0:T(8,128)(2,1)S(1)} %collective-permute-done.19.mid_b), channel_id=1, source_target_pairs={{1,0},{2,3},{5,4},{6,7},{9,8},{10,11},{13,12},{14,15},{17,16},{18,... | collective-permute-start | bytes 2064392 | tf_op jit(solution)/shard_map/ppermute | solution.py:163
  406.6 52.4 %collective-permute-start.42 = (bf16[1344,256]{1,0:T(8,128)(2,1)S(1)}, bf16[1344,256]{1,0:T(8,128)(2,1)S(1)}, u32[]{:S(2)}, u32[]{:S(2)}) collective-permute-start(bf16[1344,256]{1,0:T(8,128)(2,1)S(1)} %collective-permute-done.41.mid_a), channel_id=1, source_target_pairs={{1,0},{2,3},{5,4},{6,7},{9,8},{10,11},{13,12},{14,15},{17,16},{18,... | collective-permute-start | bytes 2064392 | tf_op jit(solution)/shard_map/ppermute | solution.py:162
  407.9 51.1 %collective-permute-start.44 = (bf16[1344,256]{1,0:T(8,128)(2,1)S(1)}, bf16[1344,256]{1,0:T(8,128)(2,1)S(1)}, u32[]{:S(2)}, u32[]{:S(2)}) collective-permute-start(bf16[1344,256]{1,0:T(8,128)(2,1)S(1)} %collective-permute-done.43.mid_b), channel_id=1, source_target_pairs={{1,0},{2,3},{5,4},{6,7},{9,8},{10,11},{13,12},{14,15},{17,16},{18,... | collective-permute-start | bytes 2064392 | tf_op jit(solution)/shard_map/ppermute | solution.py:163
  449.4 28.1 %collective-permute-start.22 = (bf16[1344,256]{1,0:T(8,128)(2,1)S(1)}, bf16[1344,256]{1,0:T(8,128)(2,1)S(1)}, u32[]{:S(2)}, u32[]{:S(2)}) collective-permute-start(bf16[1344,256]{1,0:T(8,128)(2,1)S(1)} %get-tuple-element.37), channel_id=1, source_target_pairs={{0,4},{4,0},{8,12},{12,8},{1,5},{5,1},{9,13},{13,9},{2,6},{6,2},{1... | collective-permute-start | bytes 2064392 | tf_op jit(solution)/shard_map/ppermute | solution.py:166
  458.5 21.6 %collective-permute-start.21 = (bf16[1344,256]{1,0:T(8,128)(2,1)S(1)}, bf16[1344,256]{1,0:T(8,128)(2,1)S(1)}, u32[]{:S(2)}, u32[]{:S(2)}) collective-permute-start(bf16[1344,256]{1,0:T(8,128)(2,1)S(1)} %get-tuple-element.35), channel_id=1, source_target_pairs={{0,4},{4,0},{8,12},{12,8},{1,5},{5,1},{9,13},{13,9},{2,6},{6,2},{1... | collective-permute-start | bytes 2064392 | tf_op jit(solution)/shard_map/ppermute | solution.py:168
  468.0 11.3 %collective-permute-start.46 = (bf16[1344,256]{1,0:T(8,128)(2,1)S(1)}, bf16[1344,256]{1,0:T(8,128)(2,1)S(1)}, u32[]{:S(2)}, u32[]{:S(2)}) collective-permute-start(bf16[1344,256]{1,0:T(8,128)(2,1)S(1)} %get-tuple-element.49), channel_id=1, source_target_pairs={{0,4},{4,0},{8,12},{12,8},{1,5},{5,1},{9,13},{13,9},{2,6},{6,2},{1... | collective-permute-start | bytes 2064392 | tf_op jit(solution)/shard_map/ppermute | solution.py:166
  477.0 3.1 collective-permute-start.45
  477.7 18.4 %collective-permute-start.23 = (bf16[1344,256]{1,0:T(8,128)(2,1)S(1)}, bf16[1344,256]{1,0:T(8,128)(2,1)S(1)}, u32[]{:S(2)}, u32[]{:S(2)}) collective-permute-start(bf16[1344,256]{1,0:T(8,128)(2,1)S(1)} %add_convert_fusion.3), channel_id=1, source_target_pairs={{0,8},{8,0},{4,12},{12,4},{1,9},{9,1},{5,13},{13,5},{2,10},{10,2},... | collective-permute-start | bytes 2064392 | tf_op jit(solution)/shard_map/ppermute | solution.py:169
  479.5 30.5 %collective-permute-start.47 = (bf16[1344,256]{1,0:T(8,128)(2,1)S(1)}, bf16[1344,256]{1,0:T(8,128)(2,1)S(1)}, u32[]{:S(2)}, u32[]{:S(2)}) collective-permute-start(bf16[1344,256]{1,0:T(8,128)(2,1)S(1)} %add_convert_fusion), channel_id=1, source_target_pairs={{0,8},{8,0},{4,12},{12,4},{1,9},{9,1},{5,13},{13,5},{2,10},{10,2},... | collective-permute-start | bytes 2064392 | tf_op jit(solution)/shard_map/ppermute | solution.py:169

commit v2 on v1

--- a/solution.py
+++ b/solution.py
@@ -18,7 +18,7 @@
 ACROSS = [(0, 2), (2, 0), (1, 3), (3, 1)]
 
 
-def first_pair_kernel(place, matrix, own, near, out, pair, sems):
+def first_pair_kernel(place, matrix, own, near, after, out, pair, sems):
     shard = own.shape[0]
 
     @pl.when(pl.program_id(0) == 0)
@@ -37,7 +37,7 @@
     out[...] = jnp.dot(matrix[...], pair[...], preferred_element_type=F32)
 
 
-def first_pair(place, matrix, own, near, tile):
+def first_pair(place, matrix, own, near, after, tile):
     shard, width = own.shape
     slab = matrix.shape[0]
     return pl.pallas_call(
@@ -49,6 +49,7 @@
                 pl.BlockSpec((tile, 2 * shard), lambda i, place: (i, place[0])),
                 pl.BlockSpec(memory_space=pl.ANY),
                 pl.BlockSpec(memory_space=pl.ANY),
+                pl.BlockSpec(memory_space=pl.ANY),
             ],
             out_specs=pl.BlockSpec((tile, width), lambda i, place: (i, 0)),
             scratch_shapes=[pltpu.VMEM((2 * shard, width), BF16), pltpu.SemaphoreType.DMA((2,))],
@@ -59,10 +60,10 @@
             flops=4 * slab * shard * width, bytes_accessed=4 * slab * shard + 4 * slab * width, transcendentals=0
         ),
         name="first_pair",
-    )(place, matrix, own, near)
-
-
-def second_pair_kernel(place, matrix, before, end_a, end_b, mid_a, mid_b, send, keep, pair, sems):
+    )(place, matrix, own, near, after)
+
+
+def second_pair_kernel(place, matrix, before, end_a, end_b, mid_a, mid_b, after, send, keep, pair, sems):
     shard = end_a.shape[0]
     step = pl.program_id(0)
     half_steps = pl.num_programs(0) // 2
@@ -101,7 +102,7 @@
         keep[...] = total
 
 
-def second_pair(place, matrix, before, ends, mids, tile):
+def second_pair(place, matrix, before, ends, mids, after, tile):
     shard, width = ends[0].shape
     steps = shard // tile
 
@@ -117,7 +118,7 @@
                 pl.BlockSpec((tile, 2 * shard), lambda i, place: (row(i, place), place[0])),
                 pl.BlockSpec((tile, width), lambda i, place: (row(i, place), 0)),
             ]
-            + [pl.BlockSpec(memory_space=pl.ANY)] * 4,
+            + [pl.BlockSpec(memory_space=pl.ANY)] * 5,
             out_specs=[
                 pl.BlockSpec((tile, width), lambda i, place: (jnp.minimum(i, steps - 1), 0)),
                 pl.BlockSpec((tile, width), lambda i, place: (jnp.maximum(i - steps, 0), 0)),
@@ -130,7 +131,7 @@
             flops=8 * shard * shard * width, bytes_accessed=8 * shard * shard + 14 * shard * width, transcendentals=0
         ),
         name="second_pair",
-    )(place, matrix, before, *ends, *mids)
+    )(place, matrix, before, *ends, *mids, after)
 
 
 def pipelined(inverse_rows, hess_weight, pruned_start, dual_start, prune_mask, dual_rate):
@@ -153,22 +154,49 @@
     parts = [slice(chunk * width, (chunk + 1) * width) for chunk in range(CHUNKS)]
     projected = [pruned_start[:, part] for part in parts]
     scaled = [dual_start[:, part] for part in parts]
-    for iteration in range(ITERS):
-        for chunk, part in enumerate(parts):
-            own = (hess_weight[:, part] + projected[chunk] - scaled[chunk]).astype(BF16)
-            outer = lax.ppermute(own, "col", OUTER)
-            inner = lax.ppermute(own, "col", INNER)
-            skip = lax.ppermute(own, "col", SKIP)
-            end_a = lax.ppermute(inner, "col", ENDS)
-            end_b = lax.ppermute(skip, "col", ENDS)
-            before = first_pair(first_place, inverse_rows, own, outer, tile)
-            send, keep = second_pair(far_place, inverse_rows, before, (end_a, end_b), (inner, skip), tile)
-            far = (keep + lax.ppermute(send, "row", CORE).astype(F32)).astype(BF16)
-            send, keep = second_pair(near_place, inverse_rows, before, (end_a, end_b), (inner, skip), tile)
-            near = keep + lax.ppermute(send, "row", CORE).astype(F32)
-            iterate = near + lax.ppermute(far, "row", ACROSS).astype(F32)
-            projected[chunk] = kept[:, part] * (iterate + scaled[chunk])
-            scaled[chunk] = scaled[chunk] + step_size[:, part] * (iterate - projected[chunk])
+
+    def right_side(chunk):
+        return (hess_weight[:, parts[chunk]] + projected[chunk] - scaled[chunk]).astype(BF16)
+
+    def gather(own):
+        outer = lax.ppermute(own, "col", OUTER)
+        inner = lax.ppermute(own, "col", INNER)
+        skip = lax.ppermute(own, "col", SKIP)
+        end_a = lax.ppermute(inner, "col", ENDS)
+        end_b = lax.ppermute(skip, "col", ENDS)
+        return own, outer, (end_a, end_b), (inner, skip)
+
+    def multiply_first(gathered, after):
+        own, outer, _, _ = gathered
+        return first_pair(first_place, inverse_rows, own, outer, after, 1344)
+
+    def multiply_rest(gathered, before, after):
+        _, _, ends, mids = gathered
+        send_far, keep_far = second_pair(far_place, inverse_rows, before, ends, mids, after, tile)
+        send_near, keep_near = second_pair(near_place, inverse_rows, before, ends, mids, keep_far, tile)
+        far = (keep_far + lax.ppermute(send_far, "row", CORE).astype(F32)).astype(BF16)
+        return far, keep_near, lax.ppermute(send_near, "row", CORE), lax.ppermute(far, "row", ACROSS)
+
+    def update(chunk, reduced):
+        _, near, core_sum, far_sum = reduced
+        iterate = near + core_sum.astype(F32) + far_sum.astype(F32)
+        projected[chunk] = kept[:, parts[chunk]] * (iterate + scaled[chunk])
+        scaled[chunk] = scaled[chunk] + step_size[:, parts[chunk]] * (iterate - projected[chunk])
+
+    gathered = gather(right_side(0))
+    before = multiply_first(gathered, gathered[0])
+    after = before
+    waiting = right_side(1)
+    waiting, _ = lax.optimization_barrier((waiting, gathered[3][1]))
+    for step in range(ITERS * CHUNKS):
+        chunk, last = step % CHUNKS, step == ITERS * CHUNKS - 1
+        upcoming = None if last else gather(waiting)
+        reduced = multiply_rest(gathered, before, after)
+        if not last:
+            before = multiply_first(upcoming, reduced[0])
+        update(chunk, reduced)
+        waiting = after = right_side(chunk)
+        gathered = upcoming
     return jnp.concatenate(projected, 1), jnp.concatenate(scaled, 1)
 
 

time: 517 us -> 414 us (0.80)
  waiting for transfers between devices: 243 us -> 126 us
  starting transfers between devices: 54 us -> 65 us
  Pallas kernels: 201 us -> 194 us
    ppermute x48, waiting for transfers between devices: 243 us -> 126 us  [the longest x6 58 us: gather(): inner = lax.ppermute(own, 'col', INNER)]
    ppermute x48, starting transfers between devices: 54 us -> 65 us  [the longest x6 18.2 us: gather(): inner = lax.ppermute(own, 'col', INNER)]
    pallas_call x6, Pallas kernels: 93.9 us -> 83.4 us  [first_pair(): pl.pallas_call(first_pair_kernel, grid_spec=pltpu.PrefetchScalarGridSpec(...]
  transfers between devices with their start and end apart: 48 -> 48, of which waited for: 15 -> 18; matrix products, arithmetic and copies ran while one was open for 0% -> 2% of each run, Pallas kernels for 39% -> 36%
where the time goes in v2:
time: 414 us; the launch traced here: 408 us
  Pallas kernels  194 us (47%)
  waiting for transfers between devices  126 us (30%)
  starting transfers between devices  65 us (16%)
  other arithmetic  17.3 us (4%)
  local copies, waits for them, and re-layouts  4.8 us (1%)
    pallas_call x12, Pallas kernels, second_pair(): pl.pallas_call(second_pair_kernel, grid_spec=pltpu.PrefetchScalarGridSpec...  110 us
    pallas_call x6, Pallas kernels, first_pair(): pl.pallas_call(first_pair_kernel, grid_spec=pltpu.PrefetchScalarGridSpec(...  83.4 us
    ppermute x6, waiting for transfers between devices, gather(): inner = lax.ppermute(own, 'col', INNER)  58 us
    ppermute x6, waiting for transfers between devices, gather(): skip = lax.ppermute(own, 'col', SKIP)  34 us
    ppermute x6, starting transfers between devices, gather(): inner = lax.ppermute(own, 'col', INNER)  18.2 us
    ppermute x6, waiting for transfers between devices, multiply_rest(): lax.ppermute(far, 'row', ACROSS)  17.3 us
    ppermute x6, waiting for transfers between devices, gather(): end_a = lax.ppermute(inner, 'col', ENDS)  16.1 us
    ppermute x6, starting transfers between devices, gather(): end_b = lax.ppermute(skip, 'col', ENDS)  12.7 us
  transfers between devices with their start and end apart: 48, of which 18 were waited for; matrix products, arithmetic and copies ran while one was open for 2% of the time, Pallas kernels for 36%

profile of v2, /device:TPU:16, one launch (start us, length us, event | category | flops | bytes accessed | tf_op | source)
XLA Modules:
  0.0 407.6 jit_solution(13279553957293893294)
XLA Ops:
  0.6 3.9 subtract_convert_fusion.6
  4.6 1.3 collective-permute-start.3
  5.9 2.4 collective-permute-start.1
  9.4 16.4 %collective-permute-done.3.mid_b = bf16[1344,256]{1,0:T(8,128)(2,1)S(1)} collective-permute-done((bf16[1344,256]{1,0:T(8,128)(2,1)S(1)}, bf16[1344,256]{1,0:T(8,128)(2,1)S(1)}, u32[]{:S(2)}, u32[]{:S(2)}) %collective-permute-start.3) | collective-permute-done | bytes 688160 | tf_op jit(solution)/shard_map/ppermute | solution.py:164
  27.0 2.4 collective-permute-start.10
  29.4 4.4 %collective-permute-start.4 = (bf16[1344,256]{1,0:T(8,128)(2,1)S(1)}, bf16[1344,256]{1,0:T(8,128)(2,1)S(1)}, u32[]{:S(2)}, u32[]{:S(2)}) collective-permute-start(bf16[1344,256]{1,0:T(8,128)(2,1)S(1)} %collective-permute-done.3.mid_b), channel_id=1, source_target_pairs={{1,0},{2,3},{5,4},{6,7},{9,8},{10,11},{13,12},{14,15},{17,16},{18,... | collective-permute-start | bytes 2064392 | tf_op jit(solution)/shard_map/ppermute | solution.py:166
  33.8 6.7 %collective-permute-done.1.mid_a = bf16[1344,256]{1,0:T(8,128)(2,1)S(1)} collective-permute-done((bf16[1344,256]{1,0:T(8,128)(2,1)S(1)}, bf16[1344,256]{1,0:T(8,128)(2,1)S(1)}, u32[]{:S(2)}, u32[]{:S(2)}) %collective-permute-start.1) | collective-permute-done | bytes 688160 | tf_op jit(solution)/shard_map/ppermute | solution.py:163
  40.5 1.3 collective-permute-start.2
  41.9 13.9 %first_pair.6.before.after = f32[5376,256]{1,0:T(8,128)S(1)} custom-call(s32[2]{0:T(128)S(1)} %pad_add_fusion.2.place, bf16[5376,5376]{1,0:T(8,128)(2,1)} %matrix.35, bf16[1344,256]{1,0:T(8,128)(2,1)S(1)} %get-tuple-element.63.own.after, bf16[1344,256]{1,0:T(8,128)(2,1)S(1)} %collective-permute-done.near, bf16[1344,256]{1,0:T(8,128)(2,1)S(1)} %get-tuple-element.63.own.after), custom_call_target="tpu_custom_call" | custom-call | flops 7398752256 | bytes 34406400 | tf_op jit(solution)/shard_map/first_pair/pallas_call | solution.py:43
  55.8 5.1 %collective-permute-done.2.end_a = bf16[1344,256]{1,0:T(8,128)(2,1)S(1)} collective-permute-done((bf16[1344,256]{1,0:T(8,128)(2,1)S(1)}, bf16[1344,256]{1,0:T(8,128)(2,1)S(1)}, u32[]{:S(2)}, u32[]{:S(2)}) %collective-permute-start.2) | collective-permute-done | bytes 688160 | tf_op jit(solution)/shard_map/ppermute | solution.py:165
  60.9 9.7 %second_pair.12 = (bf16[1344,256]{1,0:T(8,128)(2,1)}, f32[1344,256]{1,0:T(8,128)S(1)}) custom-call(s32[4]{0:T(128)S(1)} %pad_add_fusion.3.place, bf16[5376,5376]{1,0:T(8,128)(2,1)} %matrix.35, f32[5376,256]{1,0:T(8,128)S(1)} %first_pair.6.before.after, bf16[1344,256]{1,0:T(8,128)(2,1)S(1)} %collective-permute-done.2.end_a, ...), custom_call_target="tpu_custom_call" | custom-call | flops 3699376128 | bytes 19267584 | tf_op jit(solution)/shard_map/second_pair/pallas_call | solution.py:112
  70.8 3.6 convert_element_type.101
  74.5 2.5 collective-permute-start.9
  77.0 2.6 copy-done.1
  81.7 8.9 %second_pair.13 = (bf16[1344,256]{1,0:T(8,128)(2,1)S(1)}, f32[1344,256]{1,0:T(8,128)S(1)}) custom-call(s32[4]{0:T(128)S(1)} %pad_add_fusion.place, bf16[5376,5376]{1,0:T(8,128)(2,1)} %matrix.35, f32[5376,256]{1,0:T(8,128)S(1)} %copy-done.1, bf16[1344,256]{1,0:T(8,128)(2,1)S(1)} %copy-done.5, bf16[1344,256]{1,0:T(8,128)(2,1)S(1)} %copy-done.3, ...), custom_call_target="tpu_custom_call" | custom-call | flops 3699376128 | bytes 19267584 | tf_op jit(solution)/shard_map/second_pair/pallas_call | solution.py:112
  90.9 2.2 collective-permute-start.13
  93.2 1.3 collective-permute-start.11
  94.5 1.3 add_convert_fusion.5.after
  95.9 1.6 collective-permute-start.7
  97.4 14.1 %first_pair.7.before = f32[5376,256]{1,0:T(8,128)S(1)} custom-call(s32[2]{0:T(128)S(1)} %pad_add_fusion.2.place, bf16[5376,5376]{1,0:T(8,128)(2,1)} %matrix.35, bf16[1344,256]{1,0:T(8,128)(2,1)S(1)} %get-tuple-element.31.own, bf16[1344,256]{1,0:T(8,128)(2,1)S(1)} %collective-permute-done.9.near, bf16[1344,256]{1,0:T(8,128)(2,1)S(1)} %add_convert_fusion.5.after), custom_call_target="tpu_custom_call" | custom-call | flops 7398752256 | bytes 34406400 | tf_op jit(solution)/shard_map/first_pair/pallas_call | solution.py:43
  111.6 1.5 collective-permute-done.7
  113.9 9.2 %collective-permute-done.11.end_a = bf16[1344,256]{1,0:T(8,128)(2,1)S(1)} collective-permute-done((bf16[1344,256]{1,0:T(8,128)(2,1)}, bf16[1344,256]{1,0:T(8,128)(2,1)S(1)}, u32[]{:S(2)}, u32[]{:S(2)}) %collective-permute-start.11) | collective-permute-done | bytes 688160 | tf_op jit(solution)/shard_map/ppermute | solution.py:165
  123.1 10.0 %second_pair.14 = (bf16[1344,256]{1,0:T(8,128)(2,1)S(1)}, f32[1344,256]{1,0:T(8,128)S(1)}) custom-call(s32[4]{0:T(128)S(1)} %pad_add_fusion.3.place, bf16[5376,5376]{1,0:T(8,128)(2,1)} %matrix.35, f32[5376,256]{1,0:T(8,128)S(1)} %first_pair.7.before, bf16[1344,256]{1,0:T(8,128)(2,1)S(1)} %collective-permute-done.11.end_a, ...), custom_call_target="tpu_custom_call" | custom-call | flops 3699376128 | bytes 19267584 | tf_op jit(solution)/shard_map/second_pair/pallas_call | solution.py:112
  134.5 3.5 collective-permute-start.15
  139.0 10.0 %second_pair.15 = (bf16[1344,256]{1,0:T(8,128)(2,1)S(1)}, f32[1344,256]{1,0:T(8,128)S(1)}) custom-call(s32[4]{0:T(128)S(1)} %pad_add_fusion.place, bf16[5376,5376]{1,0:T(8,128)(2,1)} %matrix.35, f32[5376,256]{1,0:T(8,128)S(1)} %first_pair.7.before, bf16[1344,256]{1,0:T(8,128)(2,1)S(1)} %collective-permute-done.11.end_a, ...), custom_call_target="tpu_custom_call" | custom-call | flops 3699376128 | bytes 19267584 | tf_op jit(solution)/shard_map/second_pair/pallas_call | solution.py:112
  149.3 1.6 collective-permute-start.20
  150.8 3.4 collective-permute-done.17.mid_b
  154.3 1.8 collective-permute-start.18
  156.0 12.5 %collective-permute-done.15.mid_a = bf16[1344,256]{1,0:T(8,128)(2,1)S(1)} collective-permute-done((bf16[1344,256]{1,0:T(8,128)(2,1)S(1)}, bf16[1344,256]{1,0:T(8,128)(2,1)S(1)}, u32[]{:S(2)}, u32[]{:S(2)}) %collective-permute-start.15) | collective-permute-done | bytes 688160 | tf_op jit(solution)/shard_map/ppermute | solution.py:163
  168.6 1.3 collective-permute-start.16
  169.9 13.9 %first_pair.8.before = f32[5376,256]{1,0:T(8,128)S(1)} custom-call(s32[2]{0:T(128)S(1)} %pad_add_fusion.2.place, bf16[5376,5376]{1,0:T(8,128)(2,1)} %matrix.35, bf16[1344,256]{1,0:T(8,128)(2,1)S(1)} %get-tuple-element.61.after.own, bf16[1344,256]{1,0:T(8,128)(2,1)S(1)} %collective-permute-done.8.near, bf16[1344,256]{1,0:T(8,128)(2,1)S(1)} %add_convert_fusion.4.after), custom_call_target="tpu_custom_call" | custom-call | flops 7398752256 | bytes 34406400 | tf_op jit(solution)/shard_map/first_pair/pallas_call | solution.py:43
  185.0 8.9 %second_pair.16 = (bf16[1344,256]{1,0:T(8,128)(2,1)S(1)}, f32[1344,256]{1,0:T(8,128)S(1)}) custom-call(s32[4]{0:T(128)S(1)} %pad_add_fusion.3.place, bf16[5376,5376]{1,0:T(8,128)(2,1)} %matrix.35, f32[5376,256]{1,0:T(8,128)S(1)} %first_pair.8.before, bf16[1344,256]{1,0:T(8,128)(2,1)S(1)} %collective-permute-done.16.end_a, ...), custom_call_target="tpu_custom_call" | custom-call | flops 3699376128 | bytes 19267584 | tf_op jit(solution)/shard_map/second_pair/pallas_call | solution.py:112
  195.3 3.5 collective-permute-start.26
  199.8 8.9 %second_pair.17 = (bf16[1344,256]{1,0:T(8,128)(2,1)S(1)}, f32[1344,256]{1,0:T(8,128)S(1)}) custom-call(s32[4]{0:T(128)S(1)} %pad_add_fusion.place, bf16[5376,5376]{1,0:T(8,128)(2,1)} %matrix.35, f32[5376,256]{1,0:T(8,128)S(1)} %first_pair.8.before, bf16[1344,256]{1,0:T(8,128)(2,1)S(1)} %collective-permute-done.16.end_a, ...), custom_call_target="tpu_custom_call" | custom-call | flops 3699376128 | bytes 19267584 | tf_op jit(solution)/shard_map/second_pair/pallas_call | solution.py:112
  209.0 1.6 collective-permute-start.23
  210.6 4.6 %collective-permute-done.28.mid_b = bf16[1344,256]{1,0:T(8,128)(2,1)S(1)} collective-permute-done((bf16[1344,256]{1,0:T(8,128)(2,1)S(1)}, bf16[1344,256]{1,0:T(8,128)(2,1)S(1)}, u32[]{:S(2)}, u32[]{:S(2)}) %collective-permute-start.28) | collective-permute-done | bytes 688160 | tf_op jit(solution)/shard_map/ppermute | solution.py:164
  215.2 1.5 collective-permute-start.29
  216.7 12.9 %collective-permute-done.26.mid_a = bf16[1344,256]{1,0:T(8,128)(2,1)S(1)} collective-permute-done((bf16[1344,256]{1,0:T(8,128)(2,1)S(1)}, bf16[1344,256]{1,0:T(8,128)(2,1)S(1)}, u32[]{:S(2)}, u32[]{:S(2)}) %collective-permute-start.26) | collective-permute-done | bytes 688160 | tf_op jit(solution)/shard_map/ppermute | solution.py:163
  229.7 1.3 collective-permute-start.27
  231.0 13.9 %first_pair.9.before = f32[5376,256]{1,0:T(8,128)S(1)} custom-call(s32[2]{0:T(128)S(1)} %pad_add_fusion.2.place, bf16[5376,5376]{1,0:T(8,128)(2,1)} %matrix.35, bf16[1344,256]{1,0:T(8,128)(2,1)S(1)} %get-tuple-element.59.after.own, bf16[1344,256]{1,0:T(8,128)(2,1)S(1)} %collective-permute-done.25.near, bf16[1344,256]{1,0:T(8,128)(2,1)S(1)} %add_convert_fusion.3.after), custom_call_target="tpu_custom_call" | custom-call | flops 7398752256 | bytes 34406400 | tf_op jit(solution)/shard_map/first_pair/pallas_call | solution.py:43
  246.1 8.9 %second_pair.18 = (bf16[1344,256]{1,0:T(8,128)(2,1)S(1)}, f32[1344,256]{1,0:T(8,128)S(1)}) custom-call(s32[4]{0:T(128)S(1)} %pad_add_fusion.3.place, bf16[5376,5376]{1,0:T(8,128)(2,1)} %matrix.35, f32[5376,256]{1,0:T(8,128)S(1)} %first_pair.9.before, bf16[1344,256]{1,0:T(8,128)(2,1)S(1)} %collective-permute-done.27.end_a, ...), custom_call_target="tpu_custom_call" | custom-call | flops 3699376128 | bytes 19267584 | tf_op jit(solution)/shard_map/second_pair/pallas_call | solution.py:112
  255.2 1.3 collective-permute-start.33
  256.5 3.2 collective-permute-start.31
  260.7 8.9 %second_pair.19 = (bf16[1344,256]{1,0:T(8,128)(2,1)S(1)}, f32[1344,256]{1,0:T(8,128)S(1)}) custom-call(s32[4]{0:T(128)S(1)} %pad_add_fusion.place, bf16[5376,5376]{1,0:T(8,128)(2,1)} %matrix.35, f32[5376,256]{1,0:T(8,128)S(1)} %first_pair.9.before, bf16[1344,256]{1,0:T(8,128)(2,1)S(1)} %collective-permute-done.27.end_a, ...), custom_call_target="tpu_custom_call" | custom-call | flops 3699376128 | bytes 19267584 | tf_op jit(solution)/shard_map/second_pair/pallas_call | solution.py:112
  269.9 1.6 collective-permute-start.36
  271.4 4.8 %collective-permute-done.33.mid_b = bf16[1344,256]{1,0:T(8,128)(2,1)S(1)} collective-permute-done((bf16[1344,256]{1,0:T(8,128)(2,1)S(1)}, bf16[1344,256]{1,0:T(8,128)(2,1)S(1)}, u32[]{:S(2)}, u32[]{:S(2)}) %collective-permute-start.33) | collective-permute-done | bytes 688160 | tf_op jit(solution)/shard_map/ppermute | solution.py:164
  276.2 1.3 collective-permute-start.34
  277.6 12.9 %collective-permute-done.31.mid_a = bf16[1344,256]{1,0:T(8,128)(2,1)S(1)} collective-permute-done((bf16[1344,256]{1,0:T(8,128)(2,1)S(1)}, bf16[1344,256]{1,0:T(8,128)(2,1)S(1)}, u32[]{:S(2)}, u32[]{:S(2)}) %collective-permute-start.31) | collective-permute-done | bytes 688160 | tf_op jit(solution)/shard_map/ppermute | solution.py:163
  290.5 1.5 collective-permute-start.32
  292.1 13.9 %first_pair.10.before = f32[5376,256]{1,0:T(8,128)S(1)} custom-call(s32[2]{0:T(128)S(1)} %pad_add_fusion.2.place, bf16[5376,5376]{1,0:T(8,128)(2,1)} %matrix.35, bf16[1344,256]{1,0:T(8,128)(2,1)S(1)} %get-tuple-element.57.after.own, bf16[1344,256]{1,0:T(8,128)(2,1)S(1)} %collective-permute-done.24.near, bf16[1344,256]{1,0:T(8,128)(2,1)S(1)} %add_convert_fusion.2.after), custom_call_target="tpu_custom_call" | custom-call | flops 7398752256 | bytes 34406400 | tf_op jit(solution)/shard_map/first_pair/pallas_call | solution.py:43
  307.0 8.9 %second_pair.20 = (bf16[1344,256]{1,0:T(8,128)(2,1)S(1)}, f32[1344,256]{1,0:T(8,128)S(1)}) custom-call(s32[4]{0:T(128)S(1)} %pad_add_fusion.3.place, bf16[5376,5376]{1,0:T(8,128)(2,1)} %matrix.35, f32[5376,256]{1,0:T(8,128)S(1)} %first_pair.10.before, bf16[1344,256]{1,0:T(8,128)(2,1)S(1)} %collective-permute-done.32.end_a, ...), custom_call_target="tpu_custom_call" | custom-call | flops 3699376128 | bytes 19267584 | tf_op jit(solution)/shard_map/second_pair/pallas_call | solution.py:112
  317.3 3.2 collective-permute-start.41
  321.5 8.9 %second_pair.21 = (bf16[1344,256]{1,0:T(8,128)(2,1)S(1)}, f32[1344,256]{1,0:T(8,128)S(1)}) custom-call(s32[4]{0:T(128)S(1)} %pad_add_fusion.place, bf16[5376,5376]{1,0:T(8,128)(2,1)} %matrix.35, f32[5376,256]{1,0:T(8,128)S(1)} %first_pair.10.before, bf16[1344,256]{1,0:T(8,128)(2,1)S(1)} %collective-permute-done.32.end_a, ...), custom_call_target="tpu_custom_call" | custom-call | flops 3699376128 | bytes 19267584 | tf_op jit(solution)/shard_map/second_pair/pallas_call | solution.py:112
  330.7 1.6 collective-permute-start.39
  332.3 4.8 %collective-permute-done.43.mid_b = bf16[1344,256]{1,0:T(8,128)(2,1)S(1)} collective-permute-done((bf16[1344,256]{1,0:T(8,128)(2,1)S(1)}, bf16[1344,256]{1,0:T(8,128)(2,1)S(1)}, u32[]{:S(2)}, u32[]{:S(2)}) %collective-permute-start.43) | collective-permute-done | bytes 688160 | tf_op jit(solution)/shard_map/ppermute | solution.py:164
  337.1 1.3 collective-permute-start.44
  338.4 12.9 %collective-permute-done.41.mid_a = bf16[1344,256]{1,0:T(8,128)(2,1)S(1)} collective-permute-done((bf16[1344,256]{1,0:T(8,128)(2,1)S(1)}, bf16[1344,256]{1,0:T(8,128)(2,1)S(1)}, u32[]{:S(2)}, u32[]{:S(2)}) %collective-permute-start.41) | collective-permute-done | bytes 688160 | tf_op jit(solution)/shard_map/ppermute | solution.py:163
  351.4 1.3 collective-permute-start.42
  352.7 13.9 %first_pair.11.before = f32[5376,256]{1,0:T(8,128)S(1)} custom-call(s32[2]{0:T(128)S(1)} %pad_add_fusion.2.place, bf16[5376,5376]{1,0:T(8,128)(2,1)} %matrix.35, bf16[1344,256]{1,0:T(8,128)(2,1)S(1)} %get-tuple-element.55.after.own, bf16[1344,256]{1,0:T(8,128)(2,1)S(1)} %collective-permute-done.40.near, bf16[1344,256]{1,0:T(8,128)(2,1)S(1)} %add_convert_fusion.1.after), custom_call_target="tpu_custom_call" | custom-call | flops 7398752256 | bytes 34406400 | tf_op jit(solution)/shard_map/first_pair/pallas_call | solution.py:43
  367.9 8.9 %second_pair.22 = (bf16[1344,256]{1,0:T(8,128)(2,1)S(1)}, f32[1344,256]{1,0:T(8,128)S(1)}) custom-call(s32[4]{0:T(128)S(1)} %pad_add_fusion.3.place, bf16[5376,5376]{1,0:T(8,128)(2,1)} %matrix.35, f32[5376,256]{1,0:T(8,128)S(1)} %first_pair.11.before, bf16[1344,256]{1,0:T(8,128)(2,1)S(1)} %collective-permute-done.42.end_a, ...), custom_call_target="tpu_custom_call" | custom-call | flops 3699376128 | bytes 19267584 | tf_op jit(solution)/shard_map/second_pair/pallas_call | solution.py:112
  376.9 8.9 %second_pair.23 = (bf16[1344,256]{1,0:T(8,128)(2,1)S(1)}, f32[1344,256]{1,0:T(8,128)S(1)}) custom-call(s32[4]{0:T(128)S(1)} %pad_add_fusion.place, bf16[5376,5376]{1,0:T(8,128)(2,1)} %matrix.35, f32[5376,256]{1,0:T(8,128)S(1)} %first_pair.11.before, bf16[1344,256]{1,0:T(8,128)(2,1)S(1)} %collective-permute-done.42.end_a, ...), custom_call_target="tpu_custom_call" | custom-call | flops 3699376128 | bytes 19267584 | tf_op jit(solution)/shard_map/second_pair/pallas_call | solution.py:112
  386.6 1.6 collective-permute-start.47
  388.1 15.8 %collective-permute-done.47 = bf16[1344,256]{1,0:T(8,128)(2,1)S(1)} collective-permute-done((bf16[1344,256]{1,0:T(8,128)(2,1)S(1)}, bf16[1344,256]{1,0:T(8,128)(2,1)S(1)}, u32[]{:S(2)}, u32[]{:S(2)}) %collective-permute-start.47) | collective-permute-done | bytes 688160 | tf_op jit(solution)/shard_map/ppermute | solution.py:178
  404.4 3.1 pad_maximum_fusion
  (90 shorter events, 21.0 us)
Async XLA Ops:
  4.6 21.2 %collective-permute-start.3 = (bf16[1344,256]{1,0:T(8,128)(2,1)S(1)}, bf16[1344,256]{1,0:T(8,128)(2,1)S(1)}, u32[]{:S(2)}, u32[]{:S(2)}) collective-permute-start(bf16[1344,256]{1,0:T(8,128)(2,1)S(1)} %get-tuple-element.63.own.after), channel_id=1, source_target_pairs={{0,2},{3,1},{4,6},{7,5},{8,10},{11,9},{12,14},{15,13},{16,18},{19,... | collective-permute-start | bytes 2064392 | tf_op jit(solution)/shard_map/ppermute | solution.py:164
  5.9 34.7 %collective-permute-start.1 = (bf16[1344,256]{1,0:T(8,128)(2,1)S(1)}, bf16[1344,256]{1,0:T(8,128)(2,1)S(1)}, u32[]{:S(2)}, u32[]{:S(2)}) collective-permute-start(bf16[1344,256]{1,0:T(8,128)(2,1)S(1)} %get-tuple-element.63.own.after), channel_id=1, source_target_pairs={{1,2},{2,1},{5,6},{6,5},{9,10},{10,9},{13,14},{14,13},{17,18},{18,... | collective-permute-start | bytes 2064392 | tf_op jit(solution)/shard_map/ppermute | solution.py:163
  8.2 33.6 %collective-permute-start = (bf16[1344,256]{1,0:T(8,128)(2,1)S(1)}, bf16[1344,256]{1,0:T(8,128)(2,1)S(1)}, u32[]{:S(2)}, u32[]{:S(2)}) collective-permute-start(bf16[1344,256]{1,0:T(8,128)(2,1)S(1)} %get-tuple-element.63.own.after), channel_id=1, source_target_pairs={{0,1},{1,0},{2,3},{3,2},{4,5},{5,4},{6,7},{7,6},{8,9},{9,8},{10,11... | collective-permute-start | bytes 2064392 | tf_op jit(solution)/shard_map/ppermute | solution.py:162
  25.7 65.2 %collective-permute-start.12 = (bf16[1344,256]{1,0:T(8,128)(2,1)S(1)}, bf16[1344,256]{1,0:T(8,128)(2,1)}, u32[]{:S(2)}, u32[]{:S(2)}) collective-permute-start(bf16[1344,256]{1,0:T(8,128)(2,1)S(1)} %get-tuple-element.31.own), channel_id=1, source_target_pairs={{0,2},{3,1},{4,6},{7,5},{8,10},{11,9},{12,14},{15,13},{16,18},{19,... | collective-permute-start | bytes 2064392 | tf_op jit(solution)/shard_map/ppermute | solution.py:164
  27.0 66.2 %collective-permute-start.10 = (bf16[1344,256]{1,0:T(8,128)(2,1)S(1)}, bf16[1344,256]{1,0:T(8,128)(2,1)}, u32[]{:S(2)}, u32[]{:S(2)}) collective-permute-start(bf16[1344,256]{1,0:T(8,128)(2,1)S(1)} %get-tuple-element.31.own), channel_id=1, source_target_pairs={{1,2},{2,1},{5,6},{6,5},{9,10},{10,9},{13,14},{14,13},{17,18},{18,... | collective-permute-start | bytes 2064392 | tf_op jit(solution)/shard_map/ppermute | solution.py:163
  29.4 26.4 %collective-permute-start.4 = (bf16[1344,256]{1,0:T(8,128)(2,1)S(1)}, bf16[1344,256]{1,0:T(8,128)(2,1)S(1)}, u32[]{:S(2)}, u32[]{:S(2)}) collective-permute-start(bf16[1344,256]{1,0:T(8,128)(2,1)S(1)} %collective-permute-done.3.mid_b), channel_id=1, source_target_pairs={{1,0},{2,3},{5,4},{6,7},{9,8},{10,11},{13,12},{14,15},{17,16},{18,... | collective-permute-start | bytes 2064392 | tf_op jit(solution)/shard_map/ppermute | solution.py:166
  40.5 20.4 %collective-permute-start.2 = (bf16[1344,256]{1,0:T(8,128)(2,1)S(1)}, bf16[1344,256]{1,0:T(8,128)(2,1)S(1)}, u32[]{:S(2)}, u32[]{:S(2)}) collective-permute-start(bf16[1344,256]{1,0:T(8,128)(2,1)S(1)} %collective-permute-done.1.mid_a), channel_id=1, source_target_pairs={{1,0},{2,3},{5,4},{6,7},{9,8},{10,11},{13,12},{14,15},{17,16},{18,... | collective-permute-start | bytes 2064392 | tf_op jit(solution)/shard_map/ppermute | solution.py:165
  55.7 14.9 %copy-start = (f32[5376,256]{1,0:T(8,128)}, f32[5376,256]{1,0:T(8,128)S(1)}, u32[]{:S(2)}) copy-start(f32[5376,256]{1,0:T(8,128)S(1)} %first_pair.6.before.after) | copy-start | bytes 16515076
  55.7 15.0 %copy-start.9 = (s32[512]{0:T(512)S(1)}, s32[512]{0:T(512)}, u32[]{:S(2)}) copy-start(s32[512]{0:T(512)} %param.11) | copy-start | bytes 6148
  55.8 14.9 %copy-start.2 = (bf16[1344,256]{1,0:T(8,128)(2,1)}, bf16[1344,256]{1,0:T(8,128)(2,1)S(1)}, u32[]{:S(2)}) copy-start(bf16[1344,256]{1,0:T(8,128)(2,1)S(1)} %collective-permute-done.4.end_b) | copy-start | bytes 2064388
  60.9 9.7 %copy-start.4 = (bf16[1344,256]{1,0:T(8,128)(2,1)}, bf16[1344,256]{1,0:T(8,128)(2,1)S(1)}, u32[]{:S(2)}) copy-start(bf16[1344,256]{1,0:T(8,128)(2,1)S(1)} %collective-permute-done.2.end_a) | copy-start | bytes 2064388
  70.7 23.9 %collective-permute-start.6 = (bf16[1344,256]{1,0:T(8,128)(2,1)}, bf16[1344,256]{1,0:T(8,128)(2,1)}, u32[]{:S(2)}, u32[]{:S(2)}) collective-permute-start(bf16[1344,256]{1,0:T(8,128)(2,1)} %get-tuple-element.30), channel_id=1, source_target_pairs={{0,4},{4,0},{8,12},{12,8},{1,5},{5,1},{9,13},{13,9},{2,6},{6,2},{1... | collective-permute-start | bytes 2064392 | tf_op jit(solution)/shard_map/ppermute | solution.py:177
  74.5 23.0 %collective-permute-start.9 = (bf16[1344,256]{1,0:T(8,128)(2,1)S(1)}, bf16[1344,256]{1,0:T(8,128)(2,1)S(1)}, u32[]{:S(2)}, u32[]{:S(2)}) collective-permute-start(bf16[1344,256]{1,0:T(8,128)(2,1)S(1)} %get-tuple-element.31.own), channel_id=1, source_target_pairs={{0,1},{1,0},{2,3},{3,2},{4,5},{5,4},{6,7},{7,6},{8,9},{9,8},{10,11... | collective-permute-start | bytes 2064392 | tf_op jit(solution)/shard_map/ppermute | solution.py:162
  77.0 2.6 copy-start.1
  79.5 1.1 copy-start.3
  80.6 1.1 copy-start.5
  90.7 20.9 %collective-permute-start.5 = (bf16[1344,256]{1,0:T(8,128)(2,1)S(1)}, bf16[1344,256]{1,0:T(8,128)(2,1)S(1)}, u32[]{:S(2)}, u32[]{:S(2)}) collective-permute-start(bf16[1344,256]{1,0:T(8,128)(2,1)S(1)} %get-tuple-element.29), channel_id=1, source_target_pairs={{0,4},{4,0},{8,12},{12,8},{1,5},{5,1},{9,13},{13,9},{2,6},{6,2},{1... | collective-permute-start | bytes 2064392 | tf_op jit(solution)/shard_map/ppermute | solution.py:178
  90.9 23.0 %collective-permute-start.13 = (bf16[1344,256]{1,0:T(8,128)(2,1)}, bf16[1344,256]{1,0:T(8,128)(2,1)S(1)}, u32[]{:S(2)}, u32[]{:S(2)}) collective-permute-start(bf16[1344,256]{1,0:T(8,128)(2,1)} %collective-permute-done.12.mid_b), channel_id=1, source_target_pairs={{1,0},{2,3},{5,4},{6,7},{9,8},{10,11},{13,12},{14,15},{17,16},{18,... | collective-permute-start | bytes 2064392 | tf_op jit(solution)/shard_map/ppermute | solution.py:166
  93.2 29.9 %collective-permute-start.11 = (bf16[1344,256]{1,0:T(8,128)(2,1)}, bf16[1344,256]{1,0:T(8,128)(2,1)S(1)}, u32[]{:S(2)}, u32[]{:S(2)}) collective-permute-start(bf16[1344,256]{1,0:T(8,128)(2,1)} %collective-permute-done.10.mid_a), channel_id=1, source_target_pairs={{1,0},{2,3},{5,4},{6,7},{9,8},{10,11},{13,12},{14,15},{17,16},{18,... | collective-permute-start | bytes 2064392 | tf_op jit(solution)/shard_map/ppermute | solution.py:165
  95.8 17.2 %copy-start.6 = (f32[1344,512]{1,0:T(8,128)S(1)}, f32[1344,512]{1,0:T(8,128)}, u32[]{:S(2)}) copy-start(f32[1344,512]{1,0:T(8,128)} %convert_element_type.101) | copy-start | bytes 8257540
  95.9 17.2 %copy-start.7 = (f32[1344,512]{1,0:T(8,128)S(1)}, f32[1344,512]{1,0:T(8,128)}, u32[]{:S(2)}) copy-start(f32[1344,512]{1,0:T(8,128)} %param.7) | copy-start | bytes 8257540
  95.9 17.2 %copy-start.8 = (f32[1344,512]{1,0:T(8,128)S(1)}, f32[1344,512]{1,0:T(8,128)}, u32[]{:S(2)}) copy-start(f32[1344,512]{1,0:T(8,128)} %param.9) | copy-start | bytes 8257540
  95.9 17.2 %collective-permute-start.7 = (bf16[1344,256]{1,0:T(8,128)(2,1)S(1)}, bf16[1344,256]{1,0:T(8,128)(2,1)S(1)}, u32[]{:S(2)}, u32[]{:S(2)}) collective-permute-start(bf16[1344,256]{1,0:T(8,128)(2,1)S(1)} %add_convert_fusion.5.after), channel_id=1, source_target_pairs={{0,8},{8,0},{4,12},{12,4},{1,9},{9,1},{5,13},{13,5},{2,10},{10,2},... | collective-permute-start | bytes 2064392 | tf_op jit(solution)/shard_map/ppermute | solution.py:178
  133.1 16.0 %collective-permute-start.14 = (bf16[1344,256]{1,0:T(8,128)(2,1)S(1)}, bf16[1344,256]{1,0:T(8,128)(2,1)S(1)}, u32[]{:S(2)}, u32[]{:S(2)}) collective-permute-start(bf16[1344,256]{1,0:T(8,128)(2,1)S(1)} %get-tuple-element.33), channel_id=1, source_target_pairs={{0,4},{4,0},{8,12},{12,8},{1,5},{5,1},{9,13},{13,9},{2,6},{6,2},{1... | collective-permute-start | bytes 2064392 | tf_op jit(solution)/shard_map/ppermute | solution.py:177
  133.2 21.1 %collective-permute-start.17 = (bf16[1344,256]{1,0:T(8,128)(2,1)S(1)}, bf16[1344,256]{1,0:T(8,128)(2,1)S(1)}, u32[]{:S(2)}, u32[]{:S(2)}) collective-permute-start(bf16[1344,256]{1,0:T(8,128)(2,1)S(1)} %get-tuple-element.61.after.own), channel_id=1, source_target_pairs={{0,2},{3,1},{4,6},{7,5},{8,10},{11,9},{12,14},{15,13},{16,18},{19,... | collective-permute-start | bytes 2064392 | tf_op jit(solution)/shard_map/ppermute | solution.py:164
  134.5 34.1 %collective-permute-start.15 = (bf16[1344,256]{1,0:T(8,128)(2,1)S(1)}, bf16[1344,256]{1,0:T(8,128)(2,1)S(1)}, u32[]{:S(2)}, u32[]{:S(2)}) collective-permute-start(bf16[1344,256]{1,0:T(8,128)(2,1)S(1)} %get-tuple-element.61.after.own), channel_id=1, source_target_pairs={{1,2},{2,1},{5,6},{6,5},{9,10},{10,9},{13,14},{14,13},{17,18},{18,... | collective-permute-start | bytes 2064392 | tf_op jit(solution)/shard_map/ppermute | solution.py:163
  138.0 31.9 %collective-permute-start.8 = (bf16[1344,256]{1,0:T(8,128)(2,1)S(1)}, bf16[1344,256]{1,0:T(8,128)(2,1)S(1)}, u32[]{:S(2)}, u32[]{:S(2)}) collective-permute-start(bf16[1344,256]{1,0:T(8,128)(2,1)S(1)} %get-tuple-element.61.after.own), channel_id=1, source_target_pairs={{0,1},{1,0},{2,3},{3,2},{4,5},{5,4},{6,7},{7,6},{8,9},{9,8},{10,11... | collective-permute-start | bytes 2064392 | tf_op jit(solution)/shard_map/ppermute | solution.py:162
  149.0 34.7 %collective-permute-start.19 = (bf16[1344,256]{1,0:T(8,128)(2,1)S(1)}, bf16[1344,256]{1,0:T(8,128)(2,1)S(1)}, u32[]{:S(2)}, u32[]{:S(2)}) collective-permute-start(bf16[1344,256]{1,0:T(8,128)(2,1)S(1)} %get-tuple-element.35), channel_id=1, source_target_pairs={{0,4},{4,0},{8,12},{12,8},{1,5},{5,1},{9,13},{13,9},{2,6},{6,2},{1... | collective-permute-start | bytes 2064392 | tf_op jit(solution)/shard_map/ppermute | solution.py:178
  149.3 34.5 %collective-permute-start.20 = (bf16[1344,256]{1,0:T(8,128)(2,1)S(1)}, bf16[1344,256]{1,0:T(8,128)(2,1)S(1)}, u32[]{:S(2)}, u32[]{:S(2)}) collective-permute-start(bf16[1344,256]{1,0:T(8,128)(2,1)S(1)} %add_convert_fusion.4.after), channel_id=1, source_target_pairs={{0,8},{8,0},{4,12},{12,4},{1,9},{9,1},{5,13},{13,5},{2,10},{10,2},... | collective-permute-start | bytes 2064392 | tf_op jit(solution)/shard_map/ppermute | solution.py:178
  154.3 30.3 %collective-permute-start.18 = (bf16[1344,256]{1,0:T(8,128)(2,1)S(1)}, bf16[1344,256]{1,0:T(8,128)(2,1)S(1)}, u32[]{:S(2)}, u32[]{:S(2)}) collective-permute-start(bf16[1344,256]{1,0:T(8,128)(2,1)S(1)} %collective-permute-done.17.mid_b), channel_id=1, source_target_pairs={{1,0},{2,3},{5,4},{6,7},{9,8},{10,11},{13,12},{14,15},{17,16},{18,... | collective-permute-start | bytes 2064392 | tf_op jit(solution)/shard_map/ppermute | solution.py:166
  168.6 16.5 %collective-permute-start.16 = (bf16[1344,256]{1,0:T(8,128)(2,1)S(1)}, bf16[1344,256]{1,0:T(8,128)(2,1)S(1)}, u32[]{:S(2)}, u32[]{:S(2)}) collective-permute-start(bf16[1344,256]{1,0:T(8,128)(2,1)S(1)} %collective-permute-done.15.mid_a), channel_id=1, source_target_pairs={{1,0},{2,3},{5,4},{6,7},{9,8},{10,11},{13,12},{14,15},{17,16},{18,... | collective-permute-start | bytes 2064392 | tf_op jit(solution)/shard_map/ppermute | solution.py:165
  194.0 14.9 %collective-permute-start.22 = (bf16[1344,256]{1,0:T(8,128)(2,1)S(1)}, bf16[1344,256]{1,0:T(8,128)(2,1)S(1)}, u32[]{:S(2)}, u32[]{:S(2)}) collective-permute-start(bf16[1344,256]{1,0:T(8,128)(2,1)S(1)} %get-tuple-element.39), channel_id=1, source_target_pairs={{0,4},{4,0},{8,12},{12,8},{1,5},{5,1},{9,13},{13,9},{2,6},{6,2},{1... | collective-permute-start | bytes 2064392 | tf_op jit(solution)/shard_map/ppermute | solution.py:177
  194.0 21.1 %collective-permute-start.28 = (bf16[1344,256]{1,0:T(8,128)(2,1)S(1)}, bf16[1344,256]{1,0:T(8,128)(2,1)S(1)}, u32[]{:S(2)}, u32[]{:S(2)}) collective-permute-start(bf16[1344,256]{1,0:T(8,128)(2,1)S(1)} %get-tuple-element.59.after.own), channel_id=1, source_target_pairs={{0,2},{3,1},{4,6},{7,5},{8,10},{11,9},{12,14},{15,13},{16,18},{19,... | collective-permute-start | bytes 2064392 | tf_op jit(solution)/shard_map/ppermute | solution.py:164
  195.3 34.3 %collective-permute-start.26 = (bf16[1344,256]{1,0:T(8,128)(2,1)S(1)}, bf16[1344,256]{1,0:T(8,128)(2,1)S(1)}, u32[]{:S(2)}, u32[]{:S(2)}) collective-permute-start(bf16[1344,256]{1,0:T(8,128)(2,1)S(1)} %get-tuple-element.59.after.own), channel_id=1, source_target_pairs={{1,2},{2,1},{5,6},{6,5},{9,10},{10,9},{13,14},{14,13},{17,18},{18,... | collective-permute-start | bytes 2064392 | tf_op jit(solution)/shard_map/ppermute | solution.py:163
  198.8 32.1 %collective-permute-start.25 = (bf16[1344,256]{1,0:T(8,128)(2,1)S(1)}, bf16[1344,256]{1,0:T(8,128)(2,1)S(1)}, u32[]{:S(2)}, u32[]{:S(2)}) collective-permute-start(bf16[1344,256]{1,0:T(8,128)(2,1)S(1)} %get-tuple-element.59.after.own), channel_id=1, source_target_pairs={{0,1},{1,0},{2,3},{3,2},{4,5},{5,4},{6,7},{7,6},{8,9},{9,8},{10,11... | collective-permute-start | bytes 2064392 | tf_op jit(solution)/shard_map/ppermute | solution.py:162
  208.8 36.1 %collective-permute-start.21 = (bf16[1344,256]{1,0:T(8,128)(2,1)S(1)}, bf16[1344,256]{1,0:T(8,128)(2,1)S(1)}, u32[]{:S(2)}, u32[]{:S(2)}) collective-permute-start(bf16[1344,256]{1,0:T(8,128)(2,1)S(1)} %get-tuple-element.38), channel_id=1, source_target_pairs={{0,4},{4,0},{8,12},{12,8},{1,5},{5,1},{9,13},{13,9},{2,6},{6,2},{1... | collective-permute-start | bytes 2064392 | tf_op jit(solution)/shard_map/ppermute | solution.py:178
  209.0 35.9 %collective-permute-start.23 = (bf16[1344,256]{1,0:T(8,128)(2,1)S(1)}, bf16[1344,256]{1,0:T(8,128)(2,1)S(1)}, u32[]{:S(2)}, u32[]{:S(2)}) collective-permute-start(bf16[1344,256]{1,0:T(8,128)(2,1)S(1)} %add_convert_fusion.3.after), channel_id=1, source_target_pairs={{0,8},{8,0},{4,12},{12,4},{1,9},{9,1},{5,13},{13,5},{2,10},{10,2},... | collective-permute-start | bytes 2064392 | tf_op jit(solution)/shard_map/ppermute | solution.py:178
  215.2 30.4 %collective-permute-start.29 = (bf16[1344,256]{1,0:T(8,128)(2,1)S(1)}, bf16[1344,256]{1,0:T(8,128)(2,1)S(1)}, u32[]{:S(2)}, u32[]{:S(2)}) collective-permute-start(bf16[1344,256]{1,0:T(8,128)(2,1)S(1)} %collective-permute-done.28.mid_b), channel_id=1, source_target_pairs={{1,0},{2,3},{5,4},{6,7},{9,8},{10,11},{13,12},{14,15},{17,16},{18,... | collective-permute-start | bytes 2064392 | tf_op jit(solution)/shard_map/ppermute | solution.py:166
  229.7 16.5 %collective-permute-start.27 = (bf16[1344,256]{1,0:T(8,128)(2,1)S(1)}, bf16[1344,256]{1,0:T(8,128)(2,1)S(1)}, u32[]{:S(2)}, u32[]{:S(2)}) collective-permute-start(bf16[1344,256]{1,0:T(8,128)(2,1)S(1)} %collective-permute-done.26.mid_a), channel_id=1, source_target_pairs={{1,0},{2,3},{5,4},{6,7},{9,8},{10,11},{13,12},{14,15},{17,16},{18,... | collective-permute-start | bytes 2064392 | tf_op jit(solution)/shard_map/ppermute | solution.py:165
  255.1 14.6 %collective-permute-start.30 = (bf16[1344,256]{1,0:T(8,128)(2,1)S(1)}, bf16[1344,256]{1,0:T(8,128)(2,1)S(1)}, u32[]{:S(2)}, u32[]{:S(2)}) collective-permute-start(bf16[1344,256]{1,0:T(8,128)(2,1)S(1)} %get-tuple-element.41), channel_id=1, source_target_pairs={{0,4},{4,0},{8,12},{12,8},{1,5},{5,1},{9,13},{13,9},{2,6},{6,2},{1... | collective-permute-start | bytes 2064392 | tf_op jit(solution)/shard_map/ppermute | solution.py:177
  255.2 21.1 %collective-permute-start.33 = (bf16[1344,256]{1,0:T(8,128)(2,1)S(1)}, bf16[1344,256]{1,0:T(8,128)(2,1)S(1)}, u32[]{:S(2)}, u32[]{:S(2)}) collective-permute-start(bf16[1344,256]{1,0:T(8,128)(2,1)S(1)} %get-tuple-element.57.after.own), channel_id=1, source_target_pairs={{0,2},{3,1},{4,6},{7,5},{8,10},{11,9},{12,14},{15,13},{16,18},{19,... | collective-permute-start | bytes 2064392 | tf_op jit(solution)/shard_map/ppermute | solution.py:164
  256.5 34.1 %collective-permute-start.31 = (bf16[1344,256]{1,0:T(8,128)(2,1)S(1)}, bf16[1344,256]{1,0:T(8,128)(2,1)S(1)}, u32[]{:S(2)}, u32[]{:S(2)}) collective-permute-start(bf16[1344,256]{1,0:T(8,128)(2,1)S(1)} %get-tuple-element.57.after.own), channel_id=1, source_target_pairs={{1,2},{2,1},{5,6},{6,5},{9,10},{10,9},{13,14},{14,13},{17,18},{18,... | collective-permute-start | bytes 2064392 | tf_op jit(solution)/shard_map/ppermute | solution.py:163
  259.7 32.4 %collective-permute-start.24 = (bf16[1344,256]{1,0:T(8,128)(2,1)S(1)}, bf16[1344,256]{1,0:T(8,128)(2,1)S(1)}, u32[]{:S(2)}, u32[]{:S(2)}) collective-permute-start(bf16[1344,256]{1,0:T(8,128)(2,1)S(1)} %get-tuple-element.57.after.own), channel_id=1, source_target_pairs={{0,1},{1,0},{2,3},{3,2},{4,5},{5,4},{6,7},{7,6},{8,9},{9,8},{10,11... | collective-permute-start | bytes 2064392 | tf_op jit(solution)/shard_map/ppermute | solution.py:162
  269.6 36.3 %collective-permute-start.35 = (bf16[1344,256]{1,0:T(8,128)(2,1)S(1)}, bf16[1344,256]{1,0:T(8,128)(2,1)S(1)}, u32[]{:S(2)}, u32[]{:S(2)}) collective-permute-start(bf16[1344,256]{1,0:T(8,128)(2,1)S(1)} %get-tuple-element.43), channel_id=1, source_target_pairs={{0,4},{4,0},{8,12},{12,8},{1,5},{5,1},{9,13},{13,9},{2,6},{6,2},{1... | collective-permute-start | bytes 2064392 | tf_op jit(solution)/shard_map/ppermute | solution.py:178
  269.9 36.1 %collective-permute-start.36 = (bf16[1344,256]{1,0:T(8,128)(2,1)S(1)}, bf16[1344,256]{1,0:T(8,128)(2,1)S(1)}, u32[]{:S(2)}, u32[]{:S(2)}) collective-permute-start(bf16[1344,256]{1,0:T(8,128)(2,1)S(1)} %add_convert_fusion.2.after), channel_id=1, source_target_pairs={{0,8},{8,0},{4,12},{12,4},{1,9},{9,1},{5,13},{13,5},{2,10},{10,2},... | collective-permute-start | bytes 2064392 | tf_op jit(solution)/shard_map/ppermute | solution.py:178
  276.2 30.4 %collective-permute-start.34 = (bf16[1344,256]{1,0:T(8,128)(2,1)S(1)}, bf16[1344,256]{1,0:T(8,128)(2,1)S(1)}, u32[]{:S(2)}, u32[]{:S(2)}) collective-permute-start(bf16[1344,256]{1,0:T(8,128)(2,1)S(1)} %collective-permute-done.33.mid_b), channel_id=1, source_target_pairs={{1,0},{2,3},{5,4},{6,7},{9,8},{10,11},{13,12},{14,15},{17,16},{18,... | collective-permute-start | bytes 2064392 | tf_op jit(solution)/shard_map/ppermute | solution.py:166
  290.5 16.5 %collective-permute-start.32 = (bf16[1344,256]{1,0:T(8,128)(2,1)S(1)}, bf16[1344,256]{1,0:T(8,128)(2,1)S(1)}, u32[]{:S(2)}, u32[]{:S(2)}) collective-permute-start(bf16[1344,256]{1,0:T(8,128)(2,1)S(1)} %collective-permute-done.31.mid_a), channel_id=1, source_target_pairs={{1,0},{2,3},{5,4},{6,7},{9,8},{10,11},{13,12},{14,15},{17,16},{18,... | collective-permute-start | bytes 2064392 | tf_op jit(solution)/shard_map/ppermute | solution.py:165
  315.9 14.6 %collective-permute-start.38 = (bf16[1344,256]{1,0:T(8,128)(2,1)S(1)}, bf16[1344,256]{1,0:T(8,128)(2,1)S(1)}, u32[]{:S(2)}, u32[]{:S(2)}) collective-permute-start(bf16[1344,256]{1,0:T(8,128)(2,1)S(1)} %get-tuple-element.47), channel_id=1, source_target_pairs={{0,4},{4,0},{8,12},{12,8},{1,5},{5,1},{9,13},{13,9},{2,6},{6,2},{1... | collective-permute-start | bytes 2064392 | tf_op jit(solution)/shard_map/ppermute | solution.py:177
  316.0 21.1 %collective-permute-start.43 = (bf16[1344,256]{1,0:T(8,128)(2,1)S(1)}, bf16[1344,256]{1,0:T(8,128)(2,1)S(1)}, u32[]{:S(2)}, u32[]{:S(2)}) collective-permute-start(bf16[1344,256]{1,0:T(8,128)(2,1)S(1)} %get-tuple-element.55.after.own), channel_id=1, source_target_pairs={{0,2},{3,1},{4,6},{7,5},{8,10},{11,9},{12,14},{15,13},{16,18},{19,... | collective-permute-start | bytes 2064392 | tf_op jit(solution)/shard_map/ppermute | solution.py:164
  317.3 34.1 %collective-permute-start.41 = (bf16[1344,256]{1,0:T(8,128)(2,1)S(1)}, bf16[1344,256]{1,0:T(8,128)(2,1)S(1)}, u32[]{:S(2)}, u32[]{:S(2)}) collective-permute-start(bf16[1344,256]{1,0:T(8,128)(2,1)S(1)} %get-tuple-element.55.after.own), channel_id=1, source_target_pairs={{1,2},{2,1},{5,6},{6,5},{9,10},{10,9},{13,14},{14,13},{17,18},{18,... | collective-permute-start | bytes 2064392 | tf_op jit(solution)/shard_map/ppermute | solution.py:163
  320.6 32.1 %collective-permute-start.40 = (bf16[1344,256]{1,0:T(8,128)(2,1)S(1)}, bf16[1344,256]{1,0:T(8,128)(2,1)S(1)}, u32[]{:S(2)}, u32[]{:S(2)}) collective-permute-start(bf16[1344,256]{1,0:T(8,128)(2,1)S(1)} %get-tuple-element.55.after.own), channel_id=1, source_target_pairs={{0,1},{1,0},{2,3},{3,2},{4,5},{5,4},{6,7},{7,6},{8,9},{9,8},{10,11... | collective-permute-start | bytes 2064392 | tf_op jit(solution)/shard_map/ppermute | solution.py:162
  330.5 36.1 %collective-permute-start.37 = (bf16[1344,256]{1,0:T(8,128)(2,1)S(1)}, bf16[1344,256]{1,0:T(8,128)(2,1)S(1)}, u32[]{:S(2)}, u32[]{:S(2)}) collective-permute-start(bf16[1344,256]{1,0:T(8,128)(2,1)S(1)} %get-tuple-element.46), channel_id=1, source_target_pairs={{0,4},{4,0},{8,12},{12,8},{1,5},{5,1},{9,13},{13,9},{2,6},{6,2},{1... | collective-permute-start | bytes 2064392 | tf_op jit(solution)/shard_map/ppermute | solution.py:178
  330.7 35.9 %collective-permute-start.39 = (bf16[1344,256]{1,0:T(8,128)(2,1)S(1)}, bf16[1344,256]{1,0:T(8,128)(2,1)S(1)}, u32[]{:S(2)}, u32[]{:S(2)}) collective-permute-start(bf16[1344,256]{1,0:T(8,128)(2,1)S(1)} %add_convert_fusion.1.after), channel_id=1, source_target_pairs={{0,8},{8,0},{4,12},{12,4},{1,9},{9,1},{5,13},{13,5},{2,10},{10,2},... | collective-permute-start | bytes 2064392 | tf_op jit(solution)/shard_map/ppermute | solution.py:178
  337.1 30.2 %collective-permute-start.44 = (bf16[1344,256]{1,0:T(8,128)(2,1)S(1)}, bf16[1344,256]{1,0:T(8,128)(2,1)S(1)}, u32[]{:S(2)}, u32[]{:S(2)}) collective-permute-start(bf16[1344,256]{1,0:T(8,128)(2,1)S(1)} %collective-permute-done.43.mid_b), channel_id=1, source_target_pairs={{1,0},{2,3},{5,4},{6,7},{9,8},{10,11},{13,12},{14,15},{17,16},{18,... | collective-permute-start | bytes 2064392 | tf_op jit(solution)/shard_map/ppermute | solution.py:166
  351.4 16.5 %collective-permute-start.42 = (bf16[1344,256]{1,0:T(8,128)(2,1)S(1)}, bf16[1344,256]{1,0:T(8,128)(2,1)S(1)}, u32[]{:S(2)}, u32[]{:S(2)}) collective-permute-start(bf16[1344,256]{1,0:T(8,128)(2,1)S(1)} %collective-permute-done.41.mid_a), channel_id=1, source_target_pairs={{1,0},{2,3},{5,4},{6,7},{9,8},{10,11},{13,12},{14,15},{17,16},{18,... | collective-permute-start | bytes 2064392 | tf_op jit(solution)/shard_map/ppermute | solution.py:165
  376.8 9.6 %collective-permute-start.46 = (bf16[1344,256]{1,0:T(8,128)(2,1)S(1)}, bf16[1344,256]{1,0:T(8,128)(2,1)S(1)}, u32[]{:S(2)}, u32[]{:S(2)}) collective-permute-start(bf16[1344,256]{1,0:T(8,128)(2,1)S(1)} %get-tuple-element.51), channel_id=1, source_target_pairs={{0,4},{4,0},{8,12},{12,8},{1,5},{5,1},{9,13},{13,9},{2,6},{6,2},{1... | collective-permute-start | bytes 2064392 | tf_op jit(solution)/shard_map/ppermute | solution.py:177
  385.8 2.3 collective-permute-start.45
  386.6 17.4 %collective-permute-start.47 = (bf16[1344,256]{1,0:T(8,128)(2,1)S(1)}, bf16[1344,256]{1,0:T(8,128)(2,1)S(1)}, u32[]{:S(2)}, u32[]{:S(2)}) collective-permute-start(bf16[1344,256]{1,0:T(8,128)(2,1)S(1)} %add_convert_fusion), channel_id=1, source_target_pairs={{0,8},{8,0},{4,12},{12,4},{1,9},{9,1},{5,13},{13,5},{2,10},{10,2},... | collective-permute-start | bytes 2064392 | tf_op jit(solution)/shard_map/ppermute | solution.py:178

commit v3 on v2

--- a/solution.py
+++ b/solution.py
@@ -12,13 +12,14 @@
 
 OUTER = [(0, 1), (1, 0), (2, 3), (3, 2)]
 INNER = [(1, 2), (2, 1)]
-SKIP = [(0, 2), (3, 1)]
 ENDS = [(1, 0), (2, 3)]
 CORE = [(0, 1), (1, 0), (2, 3), (3, 2)]
 ACROSS = [(0, 2), (2, 0), (1, 3), (3, 1)]
 
 
-def first_pair_kernel(place, matrix, own, near, after, out, pair, sems):
+def first_pair_kernel(place, matrix, own, near, *rest):
+    out, token, pair, sems = rest[-4:]
+
     shard = own.shape[0]
 
     @pl.when(pl.program_id(0) == 0)
@@ -35,6 +36,7 @@
             copy.wait()
 
     out[...] = jnp.dot(matrix[...], pair[...], preferred_element_type=F32)
+    token[...] = jnp.zeros_like(token)
 
 
 def first_pair(place, matrix, own, near, after, tile):
@@ -47,20 +49,21 @@
             grid=(slab // tile,),
             in_specs=[
                 pl.BlockSpec((tile, 2 * shard), lambda i, place: (i, place[0])),
-                pl.BlockSpec(memory_space=pl.ANY),
-                pl.BlockSpec(memory_space=pl.ANY),
-                pl.BlockSpec(memory_space=pl.ANY),
+            ]
+            + [pl.BlockSpec(memory_space=pl.ANY)] * (2 + len(after)),
+            out_specs=[
+                pl.BlockSpec((tile, width), lambda i, place: (i, 0)),
+                pl.BlockSpec((1, width), lambda i, place: (0, 0)),
             ],
-            out_specs=pl.BlockSpec((tile, width), lambda i, place: (i, 0)),
             scratch_shapes=[pltpu.VMEM((2 * shard, width), BF16), pltpu.SemaphoreType.DMA((2,))],
         ),
-        out_shape=jax.ShapeDtypeStruct((slab, width), F32),
-        compiler_params=pltpu.CompilerParams(vmem_limit_bytes=32 * 2**20),
+        out_shape=[jax.ShapeDtypeStruct((slab, width), F32), jax.ShapeDtypeStruct((1, width), F32)],
+        compiler_params=pltpu.CompilerParams(vmem_limit_bytes=20 * 2**20),
         cost_estimate=pl.CostEstimate(
             flops=4 * slab * shard * width, bytes_accessed=4 * slab * shard + 4 * slab * width, transcendentals=0
         ),
         name="first_pair",
-    )(place, matrix, own, near, after)
+    )(place, matrix, own, near, *after)
 
 
 def second_pair_kernel(place, matrix, before, end_a, end_b, mid_a, mid_b, after, send, keep, pair, sems):
@@ -126,12 +129,27 @@
             scratch_shapes=[pltpu.VMEM((2 * shard, width), BF16), pltpu.SemaphoreType.DMA((2,))],
         ),
         out_shape=[jax.ShapeDtypeStruct((shard, width), BF16), jax.ShapeDtypeStruct((shard, width), F32)],
-        compiler_params=pltpu.CompilerParams(vmem_limit_bytes=32 * 2**20),
+        compiler_params=pltpu.CompilerParams(vmem_limit_bytes=14 * 2**20),
         cost_estimate=pl.CostEstimate(
             flops=8 * shard * shard * width, bytes_accessed=8 * shard * shard + 14 * shard * width, transcendentals=0
         ),
         name="second_pair",
     )(place, matrix, before, *ends, *mids, after)
+
+
+def hold_kernel(*refs):
+    refs[-1][...] = jnp.zeros_like(refs[-1])
+
+
+def hold(width, *others):
+    return pl.pallas_call(
+        hold_kernel,
+        in_specs=[pl.BlockSpec(memory_space=pl.ANY)] * len(others),
+        out_specs=pl.BlockSpec(memory_space=pltpu.VMEM),
+        out_shape=jax.ShapeDtypeStruct((1, width), F32),
+        compiler_params=pltpu.CompilerParams(vmem_limit_bytes=2**20),
+        name="hold",
+    )(*others)
 
 
 def pipelined(inverse_rows, hess_weight, pruned_start, dual_start, prune_mask, dual_rate):
@@ -161,40 +179,45 @@
     def gather(own):
         outer = lax.ppermute(own, "col", OUTER)
         inner = lax.ppermute(own, "col", INNER)
-        skip = lax.ppermute(own, "col", SKIP)
+        next_inner = lax.ppermute(outer, "col", INNER)
         end_a = lax.ppermute(inner, "col", ENDS)
-        end_b = lax.ppermute(skip, "col", ENDS)
-        return own, outer, (end_a, end_b), (inner, skip)
+        end_b = lax.ppermute(next_inner, "col", ENDS)
+        return own, outer, (end_a, end_b), (inner, next_inner)
 
     def multiply_first(gathered, after):
         own, outer, _, _ = gathered
         return first_pair(first_place, inverse_rows, own, outer, after, 1344)
 
-    def multiply_rest(gathered, before, after):
+    def multiply_rest(gathered, before, after, upcoming):
         _, _, ends, mids = gathered
         send_far, keep_far = second_pair(far_place, inverse_rows, before, ends, mids, after, tile)
-        send_near, keep_near = second_pair(near_place, inverse_rows, before, ends, mids, keep_far, tile)
-        far = (keep_far + lax.ppermute(send_far, "row", CORE).astype(F32)).astype(BF16)
-        return far, keep_near, lax.ppermute(send_near, "row", CORE), lax.ppermute(far, "row", ACROSS)
-
-    def update(chunk, reduced):
+        far = keep_far + lax.ppermute(send_far, "row", CORE).astype(F32)
+        if upcoming is not None:
+            far = far + hold(width, upcoming[1], upcoming[3][0])
+        far = far.astype(BF16)
+        send_near, keep_near = second_pair(near_place, inverse_rows, before, ends, mids, far, tile)
+        return send_near, keep_near, lax.ppermute(send_near, "row", CORE), lax.ppermute(far, "row", ACROSS)
+
+    def update(chunk, reduced, ahead):
         _, near, core_sum, far_sum = reduced
+        step = step_size[:, parts[chunk]]
+        for zeros in ahead:
+            step = step + zeros
         iterate = near + core_sum.astype(F32) + far_sum.astype(F32)
         projected[chunk] = kept[:, parts[chunk]] * (iterate + scaled[chunk])
-        scaled[chunk] = scaled[chunk] + step_size[:, parts[chunk]] * (iterate - projected[chunk])
+        scaled[chunk] = scaled[chunk] + step * (iterate - projected[chunk])
 
     gathered = gather(right_side(0))
-    before = multiply_first(gathered, gathered[0])
-    after = before
-    waiting = right_side(1)
-    waiting, _ = lax.optimization_barrier((waiting, gathered[3][1]))
+    before, after = multiply_first(gathered, (gathered[3][0],))
+    waiting = (right_side(1).astype(F32) + after).astype(BF16)
     for step in range(ITERS * CHUNKS):
         chunk, last = step % CHUNKS, step == ITERS * CHUNKS - 1
         upcoming = None if last else gather(waiting)
-        reduced = multiply_rest(gathered, before, after)
+        reduced = multiply_rest(gathered, before, after, upcoming)
         if not last:
-            before = multiply_first(upcoming, reduced[0])
-        update(chunk, reduced)
+            _, _, _, far_sum = reduced
+            before, token = multiply_first(upcoming, (reduced[0], far_sum, upcoming[2][0], upcoming[3][1]))
+        update(chunk, reduced, () if last else (token,))
         waiting = after = right_side(chunk)
         gathered = upcoming
     return jnp.concatenate(projected, 1), jnp.concatenate(scaled, 1)

time: 414 us -> 373 us (0.901)
  waiting for transfers between devices: 126 us -> 86.5 us
    ppermute x6, waiting for transfers between devices: 58 us -> 11.6 us  [gather(): inner = lax.ppermute(own, 'col', INNER)]
    ppermute x6, waiting for transfers between devices: 0.02 us -> 22 us  [gather(): outer = lax.ppermute(own, 'col', OUTER)]
    ppermute x6, waiting for transfers between devices: 16.1 us -> 1.23 us  [gather(): end_a = lax.ppermute(inner, 'col', ENDS)]
    unnamed x20 -> x36, local copies, waits for them, and re-layouts: 4.79 us -> 8.32 us
  transfers between devices with their start and end apart: 48 -> 48, of which waited for: 18 -> 17; matrix products, arithmetic and copies ran while one was open for 2% -> 3% of each run, Pallas kernels for 36% -> 47%
where the time goes in v3:
time: 373 us; the launch traced here: 369 us
  Pallas kernels  191 us (51%)
  waiting for transfers between devices  86.5 us (23%)
  starting transfers between devices  64.2 us (17%)
  other arithmetic  18.1 us (5%)
  local copies, waits for them, and re-layouts  8.32 us (2%)
    pallas_call x12, Pallas kernels, second_pair(): pl.pallas_call(second_pair_kernel, grid_spec=pltpu.PrefetchScalarGridSpec...  107 us
    pallas_call x6, Pallas kernels, first_pair(): pl.pallas_call(first_pair_kernel, grid_spec=pltpu.PrefetchScalarGridSpec(...  83.4 us
    ppermute x6, waiting for transfers between devices, gather(): next_inner = lax.ppermute(outer, 'col', INNER)  33 us
    ppermute x6, waiting for transfers between devices, gather(): outer = lax.ppermute(own, 'col', OUTER)  22 us
    ppermute x6, starting transfers between devices, gather(): next_inner = lax.ppermute(outer, 'col', INNER)  16.4 us
    ppermute x6, starting transfers between devices, gather(): inner = lax.ppermute(own, 'col', INNER)  16.1 us
    ppermute x6, waiting for transfers between devices, multiply_rest(): lax.ppermute(far, 'row', ACROSS)  15.7 us
    ppermute x6, waiting for transfers between devices, gather(): inner = lax.ppermute(own, 'col', INNER)  11.6 us
  transfers between devices with their start and end apart: 48, of which 17 were waited for; matrix products, arithmetic and copies ran while one was open for 3% of the time, Pallas kernels for 47%

profile of v3, /device:TPU:16, one launch (start us, length us, event | category | flops | bytes accessed | tf_op | source)
XLA Modules:
  0.0 369.5 jit_solution(14967746750796763405)
XLA Ops:
  0.6 2.6 subtract_convert_fusion.6.own
  3.2 1.6 collective-permute-start
  4.8 1.9 collective-permute-start.1
  6.7 13.7 %collective-permute-done.near = bf16[1344,256]{1,0:T(8,128)(2,1)S(1)} collective-permute-done((bf16[1344,256]{1,0:T(8,128)(2,1)S(1)}, bf16[1344,256]{1,0:T(8,128)(2,1)S(1)}, u32[]{:S(2)}, u32[]{:S(2)}) %collective-permute-start) | collective-permute-done | bytes 688160 | tf_op jit(solution)/shard_map/ppermute | solution.py:180
  20.4 2.3 collective-permute-start.3
  23.6 1.7 collective-permute-start.2
  25.3 13.3 %collective-permute-done.3.mid_b = bf16[1344,256]{1,0:T(8,128)(2,1)S(1)} collective-permute-done((bf16[1344,256]{1,0:T(8,128)(2,1)S(1)}, bf16[1344,256]{1,0:T(8,128)(2,1)S(1)}, u32[]{:S(2)}, u32[]{:S(2)}) %collective-permute-start.3) | collective-permute-done | bytes 688160 | tf_op jit(solution)/shard_map/ppermute | solution.py:182
  39.9 13.9 %first_pair.6 = (f32[5376,256]{1,0:T(8,128)S(1)}, f32[1,256]{1,0:T(1,128)S(1)}) custom-call(s32[2]{0:T(128)S(1)} %pad_add_fusion.2.place, bf16[5376,5376]{1,0:T(8,128)(2,1)} %matrix.35, bf16[1344,256]{1,0:T(8,128)(2,1)S(1)} %subtract_convert_fusion.6.own, bf16[1344,256]{1,0:T(8,128)(2,1)S(1)} %collective-permute-done.near, ...), custom_call_target="tpu_custom_call" | custom-call | flops 7398752256 | bytes 34406400 | tf_op jit(solution)/shard_map/first_pair/pallas_call | solution.py:45
  54.5 2.4 collective-permute-start.7
  57.0 8.9 %second_pair.12 = (bf16[1344,256]{1,0:T(8,128)(2,1)S(1)}, f32[1344,256]{1,0:T(8,128)S(1)}) custom-call(s32[4]{0:T(128)S(1)} %pad_add_fusion.3.place, bf16[5376,5376]{1,0:T(8,128)(2,1)} %matrix.35, f32[5376,256]{1,0:T(8,128)S(1)} %get-tuple-element.38.before, bf16[1344,256]{1,0:T(8,128)(2,1)S(1)} %collective-permute-done.2.end_a, ...), custom_call_target="tpu_custom_call" | custom-call | flops 3699376128 | bytes 19267584 | tf_op jit(solution)/shard_map/second_pair/pallas_call | solution.py:115
  65.9 2.4 copy-done
  68.4 3.5 collective-permute-done.7.refs_1_.mid_a
  71.8 1.3 collective-permute-start.10
  73.2 2.4 collective-permute-start.11
  76.6 1.5 collective-permute-start.9
  78.1 3.6 convert_element_type.107
  81.9 8.3 %collective-permute-done.11.rest_3_.mid_b = bf16[1344,256]{1,0:T(8,128)(2,1)S(1)} collective-permute-done((bf16[1344,256]{1,0:T(8,128)(2,1)S(1)}, bf16[1344,256]{1,0:T(8,128)(2,1)S(1)}, u32[]{:S(2)}, u32[]{:S(2)}) %collective-permute-start.11) | collective-permute-done | bytes 688160 | tf_op jit(solution)/shard_map/ppermute | solution.py:182
  90.1 1.3 collective-permute-start.13
  91.5 2.6 copy-done.1
  97.3 8.9 %second_pair.13 = (bf16[1344,256]{1,0:T(8,128)(2,1)S(1)}, f32[1344,256]{1,0:T(8,128)S(1)}) custom-call(s32[4]{0:T(128)S(1)} %pad_add_fusion.place, bf16[5376,5376]{1,0:T(8,128)(2,1)} %matrix.35, f32[5376,256]{1,0:T(8,128)S(1)} %copy-done.1, bf16[1344,256]{1,0:T(8,128)(2,1)S(1)} %copy-done.7, bf16[1344,256]{1,0:T(8,128)(2,1)S(1)} %copy-done.9, ...), custom_call_target="tpu_custom_call" | custom-call | flops 3699376128 | bytes 19267584 | tf_op jit(solution)/shard_map/second_pair/pallas_call | solution.py:115
  106.4 14.2 %first_pair.7 = (f32[5376,256]{1,0:T(8,128)S(1)}, f32[1,256]{1,0:T(1,128)S(1)}) custom-call(s32[2]{0:T(128)S(1)} %pad_add_fusion.2.place, bf16[5376,5376]{1,0:T(8,128)(2,1)} %matrix.35, bf16[1344,256]{1,0:T(8,128)(2,1)S(1)} %copy-done.3, bf16[1344,256]{1,0:T(8,128)(2,1)S(1)} %collective-permute-done.6.refs_0_.near, ...), custom_call_target="tpu_custom_call" | custom-call | flops 7398752256 | bytes 34406400 | tf_op jit(solution)/shard_map/first_pair/pallas_call | solution.py:45
  120.6 1.9 subtract_convert_fusion.4
  122.6 3.0 collective-permute-start.15
  125.6 8.9 %second_pair.14 = (bf16[1344,256]{1,0:T(8,128)(2,1)S(1)}, f32[1344,256]{1,0:T(8,128)S(1)}) custom-call(s32[4]{0:T(128)S(1)} %pad_add_fusion.3.place, bf16[5376,5376]{1,0:T(8,128)(2,1)} %matrix.35, f32[5376,256]{1,0:T(8,128)S(1)} %get-tuple-element.45.before, bf16[1344,256]{1,0:T(8,128)(2,1)S(1)} %collective-permute-done.10.rest_2_.end_a, ...), custom_call_target="tpu_custom_call" | custom-call | flops 3699376128 | bytes 19267584 | tf_op jit(solution)/shard_map/second_pair/pallas_call | solution.py:115
  134.6 5.5 %collective-permute-done.12.refs_0_.near = bf16[1344,256]{1,0:T(8,128)(2,1)S(1)} collective-permute-done((bf16[1344,256]{1,0:T(8,128)(2,1)S(1)}, bf16[1344,256]{1,0:T(8,128)(2,1)S(1)}, u32[]{:S(2)}, u32[]{:S(2)}) %collective-permute-start.12) | collective-permute-done | bytes 688160 | tf_op jit(solution)/shard_map/ppermute | solution.py:180
  140.1 3.0 collective-permute-start.18
  143.3 1.6 collective-permute-start.16
  144.8 1.5 collective-permute-start.17
  146.3 8.9 %second_pair.15 = (bf16[1344,256]{1,0:T(8,128)(2,1)S(1)}, f32[1344,256]{1,0:T(8,128)S(1)}) custom-call(s32[4]{0:T(128)S(1)} %pad_add_fusion.place, bf16[5376,5376]{1,0:T(8,128)(2,1)} %matrix.35, f32[5376,256]{1,0:T(8,128)S(1)} %get-tuple-element.45.before, bf16[1344,256]{1,0:T(8,128)(2,1)S(1)} %collective-permute-done.10.rest_2_.end_a, ...), custom_call_target="tpu_custom_call" | custom-call | flops 3699376128 | bytes 19267584 | tf_op jit(solution)/shard_map/second_pair/pallas_call | solution.py:115
  155.4 3.3 collective-permute-done.18.rest_3_.mid_b
  158.6 1.3 collective-permute-start.19
  161.2 13.9 %first_pair.8 = (f32[5376,256]{1,0:T(8,128)S(1)}, f32[1,256]{1,0:T(1,128)S(1)}) custom-call(s32[2]{0:T(128)S(1)} %pad_add_fusion.2.place, bf16[5376,5376]{1,0:T(8,128)(2,1)} %matrix.35, bf16[1344,256]{1,0:T(8,128)(2,1)S(1)} %get-tuple-element.83.after.own, bf16[1344,256]{1,0:T(8,128)(2,1)S(1)} %collective-permute-done.12.refs_0_.near, ...), custom_call_target="tpu_custom_call" | custom-call | flops 7398752256 | bytes 34406400 | tf_op jit(solution)/shard_map/first_pair/pallas_call | solution.py:45
  176.4 2.5 collective-permute-start.22
  178.9 2.9 collective-permute-start.23
  181.8 8.9 %second_pair.16 = (bf16[1344,256]{1,0:T(8,128)(2,1)S(1)}, f32[1344,256]{1,0:T(8,128)S(1)}) custom-call(s32[4]{0:T(128)S(1)} %pad_add_fusion.3.place, bf16[5376,5376]{1,0:T(8,128)(2,1)} %matrix.35, f32[5376,256]{1,0:T(8,128)S(1)} %get-tuple-element.49.before, bf16[1344,256]{1,0:T(8,128)(2,1)S(1)} %collective-permute-done.17.rest_2_.end_a, ...), custom_call_target="tpu_custom_call" | custom-call | flops 3699376128 | bytes 19267584 | tf_op jit(solution)/shard_map/second_pair/pallas_call | solution.py:115
  190.9 3.9 %collective-permute-done.23.refs_1_.mid_a = bf16[1344,256]{1,0:T(8,128)(2,1)S(1)} collective-permute-done((bf16[1344,256]{1,0:T(8,128)(2,1)S(1)}, bf16[1344,256]{1,0:T(8,128)(2,1)S(1)}, u32[]{:S(2)}, u32[]{:S(2)}) %collective-permute-start.23) | collective-permute-done | bytes 688160 | tf_op jit(solution)/shard_map/ppermute | solution.py:181
  194.8 1.3 collective-permute-start.26
  196.1 2.9 collective-permute-start.27
  199.9 8.9 %second_pair.17 = (bf16[1344,256]{1,0:T(8,128)(2,1)S(1)}, f32[1344,256]{1,0:T(8,128)S(1)}) custom-call(s32[4]{0:T(128)S(1)} %pad_add_fusion.place, bf16[5376,5376]{1,0:T(8,128)(2,1)} %matrix.35, f32[5376,256]{1,0:T(8,128)S(1)} %get-tuple-element.49.before, bf16[1344,256]{1,0:T(8,128)(2,1)S(1)} %collective-permute-done.17.rest_2_.end_a, ...), custom_call_target="tpu_custom_call" | custom-call | flops 3699376128 | bytes 19267584 | tf_op jit(solution)/shard_map/second_pair/pallas_call | solution.py:115
  208.9 3.0 collective-permute-done.27.rest_3_.mid_b
  213.3 13.9 %first_pair.9 = (f32[5376,256]{1,0:T(8,128)S(1)}, f32[1,256]{1,0:T(1,128)S(1)}) custom-call(s32[2]{0:T(128)S(1)} %pad_add_fusion.2.place, bf16[5376,5376]{1,0:T(8,128)(2,1)} %matrix.35, bf16[1344,256]{1,0:T(8,128)(2,1)S(1)} %get-tuple-element.81.after.own, bf16[1344,256]{1,0:T(8,128)(2,1)S(1)} %collective-permute-done.22.refs_0_.near, ...), custom_call_target="tpu_custom_call" | custom-call | flops 7398752256 | bytes 34406400 | tf_op jit(solution)/shard_map/first_pair/pallas_call | solution.py:45
  228.0 3.0 collective-permute-start.31
  230.9 8.9 %second_pair.18 = (bf16[1344,256]{1,0:T(8,128)(2,1)S(1)}, f32[1344,256]{1,0:T(8,128)S(1)}) custom-call(s32[4]{0:T(128)S(1)} %pad_add_fusion.3.place, bf16[5376,5376]{1,0:T(8,128)(2,1)} %matrix.35, f32[5376,256]{1,0:T(8,128)S(1)} %get-tuple-element.57.before, bf16[1344,256]{1,0:T(8,128)(2,1)S(1)} %collective-permute-done.26.rest_2_.end_a, ...), custom_call_target="tpu_custom_call" | custom-call | flops 3699376128 | bytes 19267584 | tf_op jit(solution)/shard_map/second_pair/pallas_call | solution.py:115
  239.9 2.8 collective-permute-done.28.refs_0_.near
  242.7 2.9 collective-permute-start.34
  245.9 1.6 collective-permute-start.32
  247.4 1.5 collective-permute-start.33
  249.0 8.9 %second_pair.19 = (bf16[1344,256]{1,0:T(8,128)(2,1)S(1)}, f32[1344,256]{1,0:T(8,128)S(1)}) custom-call(s32[4]{0:T(128)S(1)} %pad_add_fusion.place, bf16[5376,5376]{1,0:T(8,128)(2,1)} %matrix.35, f32[5376,256]{1,0:T(8,128)S(1)} %get-tuple-element.57.before, bf16[1344,256]{1,0:T(8,128)(2,1)S(1)} %collective-permute-done.26.rest_2_.end_a, ...), custom_call_target="tpu_custom_call" | custom-call | flops 3699376128 | bytes 19267584 | tf_op jit(solution)/shard_map/second_pair/pallas_call | solution.py:115
  258.0 1.7 collective-permute-done.34.rest_3_.mid_b
  261.0 13.9 %first_pair.10 = (f32[5376,256]{1,0:T(8,128)S(1)}, f32[1,256]{1,0:T(1,128)S(1)}) custom-call(s32[2]{0:T(128)S(1)} %pad_add_fusion.2.place, bf16[5376,5376]{1,0:T(8,128)(2,1)} %matrix.35, bf16[1344,256]{1,0:T(8,128)(2,1)S(1)} %get-tuple-element.79.after.own, bf16[1344,256]{1,0:T(8,128)(2,1)S(1)} %collective-permute-done.28.refs_0_.near, ...), custom_call_target="tpu_custom_call" | custom-call | flops 7398752256 | bytes 34406400 | tf_op jit(solution)/shard_map/first_pair/pallas_call | solution.py:45
  275.6 2.5 collective-permute-start.38
  278.1 3.0 collective-permute-start.39
  281.2 8.9 %second_pair.20 = (bf16[1344,256]{1,0:T(8,128)(2,1)S(1)}, f32[1344,256]{1,0:T(8,128)S(1)}) custom-call(s32[4]{0:T(128)S(1)} %pad_add_fusion.3.place, bf16[5376,5376]{1,0:T(8,128)(2,1)} %matrix.35, f32[5376,256]{1,0:T(8,128)S(1)} %get-tuple-element.61.before, bf16[1344,256]{1,0:T(8,128)(2,1)S(1)} %collective-permute-done.33.rest_2_.end_a, ...), custom_call_target="tpu_custom_call" | custom-call | flops 3699376128 | bytes 19267584 | tf_op jit(solution)/shard_map/second_pair/pallas_call | solution.py:115
  290.2 3.5 collective-permute-done.39.refs_1_.mid_a
  295.1 2.9 collective-permute-start.43
  298.9 8.9 %second_pair.21 = (bf16[1344,256]{1,0:T(8,128)(2,1)S(1)}, f32[1344,256]{1,0:T(8,128)S(1)}) custom-call(s32[4]{0:T(128)S(1)} %pad_add_fusion.place, bf16[5376,5376]{1,0:T(8,128)(2,1)} %matrix.35, f32[5376,256]{1,0:T(8,128)S(1)} %get-tuple-element.61.before, bf16[1344,256]{1,0:T(8,128)(2,1)S(1)} %collective-permute-done.33.rest_2_.end_a, ...), custom_call_target="tpu_custom_call" | custom-call | flops 3699376128 | bytes 19267584 | tf_op jit(solution)/shard_map/second_pair/pallas_call | solution.py:115
  307.9 3.4 collective-permute-done.43.rest_3_.mid_b
  311.3 1.6 collective-permute-start.44
  312.9 13.9 %first_pair.11 = (f32[5376,256]{1,0:T(8,128)S(1)}, f32[1,256]{1,0:T(1,128)S(1)}) custom-call(s32[2]{0:T(128)S(1)} %pad_add_fusion.2.place, bf16[5376,5376]{1,0:T(8,128)(2,1)} %matrix.35, bf16[1344,256]{1,0:T(8,128)(2,1)S(1)} %get-tuple-element.77.after.own, bf16[1344,256]{1,0:T(8,128)(2,1)S(1)} %collective-permute-done.38.refs_0_.near, ...), custom_call_target="tpu_custom_call" | custom-call | flops 7398752256 | bytes 34406400 | tf_op jit(solution)/shard_map/first_pair/pallas_call | solution.py:45
  327.5 8.9 %second_pair.22 = (bf16[1344,256]{1,0:T(8,128)(2,1)S(1)}, f32[1344,256]{1,0:T(8,128)S(1)}) custom-call(s32[4]{0:T(128)S(1)} %pad_add_fusion.3.place, bf16[5376,5376]{1,0:T(8,128)(2,1)} %matrix.35, f32[5376,256]{1,0:T(8,128)S(1)} %get-tuple-element.68.before, bf16[1344,256]{1,0:T(8,128)(2,1)S(1)} %collective-permute-done.42.rest_2_.end_a, ...), custom_call_target="tpu_custom_call" | custom-call | flops 3699376128 | bytes 19267584 | tf_op jit(solution)/shard_map/second_pair/pallas_call | solution.py:115
  336.5 2.1 collective-permute-done.45
  338.8 8.9 %second_pair.23 = (bf16[1344,256]{1,0:T(8,128)(2,1)S(1)}, f32[1344,256]{1,0:T(8,128)S(1)}) custom-call(s32[4]{0:T(128)S(1)} %pad_add_fusion.place, bf16[5376,5376]{1,0:T(8,128)(2,1)} %matrix.35, f32[5376,256]{1,0:T(8,128)S(1)} %get-tuple-element.68.before, bf16[1344,256]{1,0:T(8,128)(2,1)S(1)} %collective-permute-done.42.rest_2_.end_a, ...), custom_call_target="tpu_custom_call" | custom-call | flops 3699376128 | bytes 19267584 | tf_op jit(solution)/shard_map/second_pair/pallas_call | solution.py:115
  350.0 15.7 %collective-permute-done.47 = bf16[1344,256]{1,0:T(8,128)(2,1)S(1)} collective-permute-done((bf16[1344,256]{1,0:T(8,128)(2,1)S(1)}, bf16[1344,256]{1,0:T(8,128)(2,1)S(1)}, u32[]{:S(2)}, u32[]{:S(2)}) %collective-permute-start.47) | collective-permute-done | bytes 688160 | tf_op jit(solution)/shard_map/ppermute | solution.py:199
  366.2 3.3 pad_maximum_fusion
  (116 shorter events, 21.7 us)
Async XLA Ops:
  3.2 17.2 %collective-permute-start = (bf16[1344,256]{1,0:T(8,128)(2,1)S(1)}, bf16[1344,256]{1,0:T(8,128)(2,1)S(1)}, u32[]{:S(2)}, u32[]{:S(2)}) collective-permute-start(bf16[1344,256]{1,0:T(8,128)(2,1)S(1)} %subtract_convert_fusion.6.own), channel_id=1, source_target_pairs={{0,1},{1,0},{2,3},{3,2},{4,5},{5,4},{6,7},{7,6},{8,9},{9,8},{10,11... | collective-permute-start | bytes 2064392 | tf_op jit(solution)/shard_map/ppermute | solution.py:180
  4.8 18.8 %collective-permute-start.1 = (bf16[1344,256]{1,0:T(8,128)(2,1)S(1)}, bf16[1344,256]{1,0:T(8,128)(2,1)S(1)}, u32[]{:S(2)}, u32[]{:S(2)}) collective-permute-start(bf16[1344,256]{1,0:T(8,128)(2,1)S(1)} %subtract_convert_fusion.6.own), channel_id=1, source_target_pairs={{1,2},{2,1},{5,6},{6,5},{9,10},{10,9},{13,14},{14,13},{17,18},{18,... | collective-permute-start | bytes 2064392 | tf_op jit(solution)/shard_map/ppermute | solution.py:181
  20.4 18.2 %collective-permute-start.3 = (bf16[1344,256]{1,0:T(8,128)(2,1)S(1)}, bf16[1344,256]{1,0:T(8,128)(2,1)S(1)}, u32[]{:S(2)}, u32[]{:S(2)}) collective-permute-start(bf16[1344,256]{1,0:T(8,128)(2,1)S(1)} %collective-permute-done.near), channel_id=1, source_target_pairs={{1,2},{2,1},{5,6},{6,5},{9,10},{10,9},{13,14},{14,13},{17,18},{18,... | collective-permute-start | bytes 2064392 | tf_op jit(solution)/shard_map/ppermute | solution.py:182
  23.0 30.8 %copy-start.11 = (f32[1344,512]{1,0:T(8,128)S(1)}, f32[1344,512]{1,0:T(8,128)}, u32[]{:S(2)}) copy-start(f32[1344,512]{1,0:T(8,128)} %param.7) | copy-start | bytes 8257540
  23.0 30.8 %copy-start.13 = (f32[1344,512]{1,0:T(8,128)S(1)}, f32[1344,512]{1,0:T(8,128)}, u32[]{:S(2)}) copy-start(f32[1344,512]{1,0:T(8,128)} %param.9) | copy-start | bytes 8257540
  23.0 30.8 %copy-start.15 = (f32[1344,512]{1,0:T(8,128)S(1)}, f32[1344,512]{1,0:T(8,128)}, u32[]{:S(2)}) copy-start(f32[1344,512]{1,0:T(8,128)} %param.8) | copy-start | bytes 8257540
  23.6 33.3 %collective-permute-start.2 = (bf16[1344,256]{1,0:T(8,128)(2,1)S(1)}, bf16[1344,256]{1,0:T(8,128)(2,1)S(1)}, u32[]{:S(2)}, u32[]{:S(2)}) collective-permute-start(bf16[1344,256]{1,0:T(8,128)(2,1)S(1)} %collective-permute-done.1.rest_0_.mid_a), channel_id=1, source_target_pairs={{1,0},{2,3},{5,4},{6,7},{9,8},{10,11},{13,12},{14,15},{17,16},{18,... | collective-permute-start | bytes 2064392 | tf_op jit(solution)/shard_map/ppermute | solution.py:183
  38.6 18.3 %copy-start.4 = (bf16[1344,256]{1,0:T(8,128)(2,1)}, bf16[1344,256]{1,0:T(8,128)(2,1)S(1)}, u32[]{:S(2)}) copy-start(bf16[1344,256]{1,0:T(8,128)(2,1)S(1)} %collective-permute-done.3.mid_b) | copy-start | bytes 2064388
  38.6 18.3 %collective-permute-start.4 = (bf16[1344,256]{1,0:T(8,128)(2,1)S(1)}, bf16[1344,256]{1,0:T(8,128)(2,1)S(1)}, u32[]{:S(2)}, u32[]{:S(2)}) collective-permute-start(bf16[1344,256]{1,0:T(8,128)(2,1)S(1)} %collective-permute-done.3.mid_b), channel_id=1, source_target_pairs={{1,0},{2,3},{5,4},{6,7},{9,8},{10,11},{13,12},{14,15},{17,16},{18,... | collective-permute-start | bytes 2064392 | tf_op jit(solution)/shard_map/ppermute | solution.py:184
  54.5 11.5 %copy-start.2 = (bf16[1344,256]{1,0:T(8,128)(2,1)}, bf16[1344,256]{1,0:T(8,128)(2,1)S(1)}, u32[]{:S(2)}) copy-start(bf16[1344,256]{1,0:T(8,128)(2,1)S(1)} %add_convert_fusion.6.own) | copy-start | bytes 2064388
  54.5 18.7 %collective-permute-start.6 = (bf16[1344,256]{1,0:T(8,128)(2,1)S(1)}, bf16[1344,256]{1,0:T(8,128)(2,1)S(1)}, u32[]{:S(2)}, u32[]{:S(2)}) collective-permute-start(bf16[1344,256]{1,0:T(8,128)(2,1)S(1)} %add_convert_fusion.6.own), channel_id=1, source_target_pairs={{0,1},{1,0},{2,3},{3,2},{4,5},{5,4},{6,7},{7,6},{8,9},{9,8},{10,11... | collective-permute-start | bytes 2064392 | tf_op jit(solution)/shard_map/ppermute | solution.py:180
  54.5 17.3 %collective-permute-start.7 = (bf16[1344,256]{1,0:T(8,128)(2,1)S(1)}, bf16[1344,256]{1,0:T(8,128)(2,1)S(1)}, u32[]{:S(2)}, u32[]{:S(2)}) collective-permute-start(bf16[1344,256]{1,0:T(8,128)(2,1)S(1)} %add_convert_fusion.6.own), channel_id=1, source_target_pairs={{1,2},{2,1},{5,6},{6,5},{9,10},{10,9},{13,14},{14,13},{17,18},{18,... | collective-permute-start | bytes 2064392 | tf_op jit(solution)/shard_map/ppermute | solution.py:181
  56.9 9.0 %copy-start.6 = (bf16[1344,256]{1,0:T(8,128)(2,1)}, bf16[1344,256]{1,0:T(8,128)(2,1)S(1)}, u32[]{:S(2)}) copy-start(bf16[1344,256]{1,0:T(8,128)(2,1)S(1)} %collective-permute-done.2.end_a) | copy-start | bytes 2064388
  56.9 9.0 %copy-start.8 = (bf16[1344,256]{1,0:T(8,128)(2,1)}, bf16[1344,256]{1,0:T(8,128)(2,1)S(1)}, u32[]{:S(2)}) copy-start(bf16[1344,256]{1,0:T(8,128)(2,1)S(1)} %collective-permute-done.4.end_b) | copy-start | bytes 2064388
  65.9 2.4 copy-start
  68.3 7.2 %collective-permute-start.5 = (bf16[1344,256]{1,0:T(8,128)(2,1)S(1)}, bf16[1344,256]{1,0:T(8,128)(2,1)S(1)}, u32[]{:S(2)}, u32[]{:S(2)}) collective-permute-start(bf16[1344,256]{1,0:T(8,128)(2,1)S(1)} %get-tuple-element.41), channel_id=1, source_target_pairs={{0,4},{4,0},{8,12},{12,8},{1,5},{5,1},{9,13},{13,9},{2,6},{6,2},{1... | collective-permute-start | bytes 2064392 | tf_op jit(solution)/shard_map/ppermute | solution.py:194
  71.8 34.6 %collective-permute-start.10 = (bf16[1344,256]{1,0:T(8,128)(2,1)S(1)}, bf16[1344,256]{1,0:T(8,128)(2,1)S(1)}, u32[]{:S(2)}, u32[]{:S(2)}) collective-permute-start(bf16[1344,256]{1,0:T(8,128)(2,1)S(1)} %collective-permute-done.7.refs_1_.mid_a), channel_id=1, source_target_pairs={{1,0},{2,3},{5,4},{6,7},{9,8},{10,11},{13,12},{14,15},{17,16},{18,... | collective-permute-start | bytes 2064392 | tf_op jit(solution)/shard_map/ppermute | solution.py:183
  73.2 17.0 %collective-permute-start.11 = (bf16[1344,256]{1,0:T(8,128)(2,1)S(1)}, bf16[1344,256]{1,0:T(8,128)(2,1)S(1)}, u32[]{:S(2)}, u32[]{:S(2)}) collective-permute-start(bf16[1344,256]{1,0:T(8,128)(2,1)S(1)} %collective-permute-done.6.refs_0_.near), channel_id=1, source_target_pairs={{1,2},{2,1},{5,6},{6,5},{9,10},{10,9},{13,14},{14,13},{17,18},{18,... | collective-permute-start | bytes 2064392 | tf_op jit(solution)/shard_map/ppermute | solution.py:182
  76.6 29.7 %collective-permute-start.9 = (bf16[1344,256]{1,0:T(8,128)(2,1)}, bf16[1344,256]{1,0:T(8,128)(2,1)}, u32[]{:S(2)}, u32[]{:S(2)}) collective-permute-start(bf16[1344,256]{1,0:T(8,128)(2,1)} %add_convert_fusion.5.after), channel_id=1, source_target_pairs={{0,8},{8,0},{4,12},{12,4},{1,9},{9,1},{5,13},{13,5},{2,10},{10,2},... | collective-permute-start | bytes 2064392 | tf_op jit(solution)/shard_map/ppermute | solution.py:199
  78.1 3.7 %copy-start.17 = (s32[512]{0:T(512)S(1)}, s32[512]{0:T(512)}, u32[]{:S(2)}) copy-start(s32[512]{0:T(512)} %param.11) | copy-start | bytes 6148
  90.1 35.5 %collective-permute-start.13 = (bf16[1344,256]{1,0:T(8,128)(2,1)S(1)}, bf16[1344,256]{1,0:T(8,128)(2,1)S(1)}, u32[]{:S(2)}, u32[]{:S(2)}) collective-permute-start(bf16[1344,256]{1,0:T(8,128)(2,1)S(1)} %collective-permute-done.11.rest_3_.mid_b), channel_id=1, source_target_pairs={{1,0},{2,3},{5,4},{6,7},{9,8},{10,11},{13,12},{14,15},{17,16},{18,... | collective-permute-start | bytes 2064392 | tf_op jit(solution)/shard_map/ppermute | solution.py:184
  91.5 2.6 copy-start.1
  94.0 1.1 copy-start.5
  97.3 9.1 %copy-start.3 = (bf16[1344,256]{1,0:T(8,128)(2,1)S(1)}, bf16[1344,256]{1,0:T(8,128)(2,1)}, u32[]{:S(2)}) copy-start(bf16[1344,256]{1,0:T(8,128)(2,1)} %copy-done.2) | copy-start | bytes 2064388
  106.3 14.3 %copy-start.10 = (f32[1344,512]{1,0:T(8,128)S(1)}, f32[1344,512]{1,0:T(8,128)}, u32[]{:S(2)}) copy-start(f32[1344,512]{1,0:T(8,128)} %convert_element_type.107) | copy-start | bytes 8257540
  106.3 14.3 %copy-start.12 = (f32[1344,512]{1,0:T(8,128)S(1)}, f32[1344,512]{1,0:T(8,128)}, u32[]{:S(2)}) copy-start(f32[1344,512]{1,0:T(8,128)} %param.7) | copy-start | bytes 8257540
  106.3 14.3 %copy-start.14 = (f32[1344,512]{1,0:T(8,128)S(1)}, f32[1344,512]{1,0:T(8,128)}, u32[]{:S(2)}) copy-start(f32[1344,512]{1,0:T(8,128)} %param.9) | copy-start | bytes 8257540
  106.3 14.3 %collective-permute-start.8 = (bf16[1344,256]{1,0:T(8,128)(2,1)S(1)}, bf16[1344,256]{1,0:T(8,128)(2,1)S(1)}, u32[]{:S(2)}, u32[]{:S(2)}) collective-permute-start(bf16[1344,256]{1,0:T(8,128)(2,1)S(1)} %get-tuple-element.43.rest_0_), channel_id=1, source_target_pairs={{0,4},{4,0},{8,12},{12,8},{1,5},{5,1},{9,13},{13,9},{2,6},{6,2},{1... | collective-permute-start | bytes 2064392 | tf_op jit(solution)/shard_map/ppermute | solution.py:199
  122.5 17.6 %collective-permute-start.12 = (bf16[1344,256]{1,0:T(8,128)(2,1)S(1)}, bf16[1344,256]{1,0:T(8,128)(2,1)S(1)}, u32[]{:S(2)}, u32[]{:S(2)}) collective-permute-start(bf16[1344,256]{1,0:T(8,128)(2,1)S(1)} %get-tuple-element.83.after.own), channel_id=1, source_target_pairs={{0,1},{1,0},{2,3},{3,2},{4,5},{5,4},{6,7},{7,6},{8,9},{9,8},{10,11... | collective-permute-start | bytes 2064392 | tf_op jit(solution)/shard_map/ppermute | solution.py:180
  122.6 20.5 %collective-permute-start.15 = (bf16[1344,256]{1,0:T(8,128)(2,1)S(1)}, bf16[1344,256]{1,0:T(8,128)(2,1)S(1)}, u32[]{:S(2)}, u32[]{:S(2)}) collective-permute-start(bf16[1344,256]{1,0:T(8,128)(2,1)S(1)} %get-tuple-element.83.after.own), channel_id=1, source_target_pairs={{1,2},{2,1},{5,6},{6,5},{9,10},{10,9},{13,14},{14,13},{17,18},{18,... | collective-permute-start | bytes 2064392 | tf_op jit(solution)/shard_map/ppermute | solution.py:181
  134.5 8.5 %collective-permute-start.14 = (bf16[1344,256]{1,0:T(8,128)(2,1)S(1)}, bf16[1344,256]{1,0:T(8,128)(2,1)S(1)}, u32[]{:S(2)}, u32[]{:S(2)}) collective-permute-start(bf16[1344,256]{1,0:T(8,128)(2,1)S(1)} %get-tuple-element.47), channel_id=1, source_target_pairs={{0,4},{4,0},{8,12},{12,8},{1,5},{5,1},{9,13},{13,9},{2,6},{6,2},{1... | collective-permute-start | bytes 2064392 | tf_op jit(solution)/shard_map/ppermute | solution.py:194
  140.1 18.6 %collective-permute-start.18 = (bf16[1344,256]{1,0:T(8,128)(2,1)S(1)}, bf16[1344,256]{1,0:T(8,128)(2,1)S(1)}, u32[]{:S(2)}, u32[]{:S(2)}) collective-permute-start(bf16[1344,256]{1,0:T(8,128)(2,1)S(1)} %collective-permute-done.12.refs_0_.near), channel_id=1, source_target_pairs={{1,2},{2,1},{5,6},{6,5},{9,10},{10,9},{13,14},{14,13},{17,18},{18,... | collective-permute-start | bytes 2064392 | tf_op jit(solution)/shard_map/ppermute | solution.py:182
  143.3 16.7 %collective-permute-start.16 = (bf16[1344,256]{1,0:T(8,128)(2,1)S(1)}, bf16[1344,256]{1,0:T(8,128)(2,1)S(1)}, u32[]{:S(2)}, u32[]{:S(2)}) collective-permute-start(bf16[1344,256]{1,0:T(8,128)(2,1)S(1)} %add_convert_fusion.4.after), channel_id=1, source_target_pairs={{0,8},{8,0},{4,12},{12,4},{1,9},{9,1},{5,13},{13,5},{2,10},{10,2},... | collective-permute-start | bytes 2064392 | tf_op jit(solution)/shard_map/ppermute | solution.py:199
  144.8 16.4 %collective-permute-start.17 = (bf16[1344,256]{1,0:T(8,128)(2,1)S(1)}, bf16[1344,256]{1,0:T(8,128)(2,1)S(1)}, u32[]{:S(2)}, u32[]{:S(2)}) collective-permute-start(bf16[1344,256]{1,0:T(8,128)(2,1)S(1)} %collective-permute-done.15.refs_1_.mid_a), channel_id=1, source_target_pairs={{1,0},{2,3},{5,4},{6,7},{9,8},{10,11},{13,12},{14,15},{17,16},{18,... | collective-permute-start | bytes 2064392 | tf_op jit(solution)/shard_map/ppermute | solution.py:183
  155.3 20.3 %collective-permute-start.20 = (bf16[1344,256]{1,0:T(8,128)(2,1)S(1)}, bf16[1344,256]{1,0:T(8,128)(2,1)S(1)}, u32[]{:S(2)}, u32[]{:S(2)}) collective-permute-start(bf16[1344,256]{1,0:T(8,128)(2,1)S(1)} %get-tuple-element.48.rest_0_), channel_id=1, source_target_pairs={{0,4},{4,0},{8,12},{12,8},{1,5},{5,1},{9,13},{13,9},{2,6},{6,2},{1... | collective-permute-start | bytes 2064392 | tf_op jit(solution)/shard_map/ppermute | solution.py:199
  158.6 23.2 %collective-permute-start.19 = (bf16[1344,256]{1,0:T(8,128)(2,1)S(1)}, bf16[1344,256]{1,0:T(8,128)(2,1)S(1)}, u32[]{:S(2)}, u32[]{:S(2)}) collective-permute-start(bf16[1344,256]{1,0:T(8,128)(2,1)S(1)} %collective-permute-done.18.rest_3_.mid_b), channel_id=1, source_target_pairs={{1,0},{2,3},{5,4},{6,7},{9,8},{10,11},{13,12},{14,15},{17,16},{18,... | collective-permute-start | bytes 2064392 | tf_op jit(solution)/shard_map/ppermute | solution.py:184
  176.4 19.7 %collective-permute-start.22 = (bf16[1344,256]{1,0:T(8,128)(2,1)S(1)}, bf16[1344,256]{1,0:T(8,128)(2,1)S(1)}, u32[]{:S(2)}, u32[]{:S(2)}) collective-permute-start(bf16[1344,256]{1,0:T(8,128)(2,1)S(1)} %get-tuple-element.81.after.own), channel_id=1, source_target_pairs={{0,1},{1,0},{2,3},{3,2},{4,5},{5,4},{6,7},{7,6},{8,9},{9,8},{10,11... | collective-permute-start | bytes 2064392 | tf_op jit(solution)/shard_map/ppermute | solution.py:180
  178.9 15.8 %collective-permute-start.23 = (bf16[1344,256]{1,0:T(8,128)(2,1)S(1)}, bf16[1344,256]{1,0:T(8,128)(2,1)S(1)}, u32[]{:S(2)}, u32[]{:S(2)}) collective-permute-start(bf16[1344,256]{1,0:T(8,128)(2,1)S(1)} %get-tuple-element.81.after.own), channel_id=1, source_target_pairs={{1,2},{2,1},{5,6},{6,5},{9,10},{10,9},{13,14},{14,13},{17,18},{18,... | collective-permute-start | bytes 2064392 | tf_op jit(solution)/shard_map/ppermute | solution.py:181
  190.8 8.3 %collective-permute-start.21 = (bf16[1344,256]{1,0:T(8,128)(2,1)S(1)}, bf16[1344,256]{1,0:T(8,128)(2,1)S(1)}, u32[]{:S(2)}, u32[]{:S(2)}) collective-permute-start(bf16[1344,256]{1,0:T(8,128)(2,1)S(1)} %get-tuple-element.53), channel_id=1, source_target_pairs={{0,4},{4,0},{8,12},{12,8},{1,5},{5,1},{9,13},{13,9},{2,6},{6,2},{1... | collective-permute-start | bytes 2064392 | tf_op jit(solution)/shard_map/ppermute | solution.py:194
  194.8 18.5 %collective-permute-start.26 = (bf16[1344,256]{1,0:T(8,128)(2,1)S(1)}, bf16[1344,256]{1,0:T(8,128)(2,1)S(1)}, u32[]{:S(2)}, u32[]{:S(2)}) collective-permute-start(bf16[1344,256]{1,0:T(8,128)(2,1)S(1)} %collective-permute-done.23.refs_1_.mid_a), channel_id=1, source_target_pairs={{1,0},{2,3},{5,4},{6,7},{9,8},{10,11},{13,12},{14,15},{17,16},{18,... | collective-permute-start | bytes 2064392 | tf_op jit(solution)/shard_map/ppermute | solution.py:183
  196.1 15.8 %collective-permute-start.27 = (bf16[1344,256]{1,0:T(8,128)(2,1)S(1)}, bf16[1344,256]{1,0:T(8,128)(2,1)S(1)}, u32[]{:S(2)}, u32[]{:S(2)}) collective-permute-start(bf16[1344,256]{1,0:T(8,128)(2,1)S(1)} %collective-permute-done.22.refs_0_.near), channel_id=1, source_target_pairs={{1,2},{2,1},{5,6},{6,5},{9,10},{10,9},{13,14},{14,13},{17,18},{18,... | collective-permute-start | bytes 2064392 | tf_op jit(solution)/shard_map/ppermute | solution.py:182
  199.3 14.0 %collective-permute-start.25 = (bf16[1344,256]{1,0:T(8,128)(2,1)S(1)}, bf16[1344,256]{1,0:T(8,128)(2,1)S(1)}, u32[]{:S(2)}, u32[]{:S(2)}) collective-permute-start(bf16[1344,256]{1,0:T(8,128)(2,1)S(1)} %add_convert_fusion.3.after), channel_id=1, source_target_pairs={{0,8},{8,0},{4,12},{12,4},{1,9},{9,1},{5,13},{13,5},{2,10},{10,2},... | collective-permute-start | bytes 2064392 | tf_op jit(solution)/shard_map/ppermute | solution.py:199
  208.8 18.3 %collective-permute-start.24 = (bf16[1344,256]{1,0:T(8,128)(2,1)S(1)}, bf16[1344,256]{1,0:T(8,128)(2,1)S(1)}, u32[]{:S(2)}, u32[]{:S(2)}) collective-permute-start(bf16[1344,256]{1,0:T(8,128)(2,1)S(1)} %get-tuple-element.55.rest_0_), channel_id=1, source_target_pairs={{0,4},{4,0},{8,12},{12,8},{1,5},{5,1},{9,13},{13,9},{2,6},{6,2},{1... | collective-permute-start | bytes 2064392 | tf_op jit(solution)/shard_map/ppermute | solution.py:199
  211.9 19.0 %collective-permute-start.29 = (bf16[1344,256]{1,0:T(8,128)(2,1)S(1)}, bf16[1344,256]{1,0:T(8,128)(2,1)S(1)}, u32[]{:S(2)}, u32[]{:S(2)}) collective-permute-start(bf16[1344,256]{1,0:T(8,128)(2,1)S(1)} %collective-permute-done.27.rest_3_.mid_b), channel_id=1, source_target_pairs={{1,0},{2,3},{5,4},{6,7},{9,8},{10,11},{13,12},{14,15},{17,16},{18,... | collective-permute-start | bytes 2064392 | tf_op jit(solution)/shard_map/ppermute | solution.py:184
  227.9 14.9 %collective-permute-start.28 = (bf16[1344,256]{1,0:T(8,128)(2,1)S(1)}, bf16[1344,256]{1,0:T(8,128)(2,1)S(1)}, u32[]{:S(2)}, u32[]{:S(2)}) collective-permute-start(bf16[1344,256]{1,0:T(8,128)(2,1)S(1)} %get-tuple-element.79.after.own), channel_id=1, source_target_pairs={{0,1},{1,0},{2,3},{3,2},{4,5},{5,4},{6,7},{7,6},{8,9},{9,8},{10,11... | collective-permute-start | bytes 2064392 | tf_op jit(solution)/shard_map/ppermute | solution.py:180
  228.0 17.7 %collective-permute-start.31 = (bf16[1344,256]{1,0:T(8,128)(2,1)S(1)}, bf16[1344,256]{1,0:T(8,128)(2,1)S(1)}, u32[]{:S(2)}, u32[]{:S(2)}) collective-permute-start(bf16[1344,256]{1,0:T(8,128)(2,1)S(1)} %get-tuple-element.79.after.own), channel_id=1, source_target_pairs={{1,2},{2,1},{5,6},{6,5},{9,10},{10,9},{13,14},{14,13},{17,18},{18,... | collective-permute-start | bytes 2064392 | tf_op jit(solution)/shard_map/ppermute | solution.py:181
  239.9 5.8 %collective-permute-start.30 = (bf16[1344,256]{1,0:T(8,128)(2,1)S(1)}, bf16[1344,256]{1,0:T(8,128)(2,1)S(1)}, u32[]{:S(2)}, u32[]{:S(2)}) collective-permute-start(bf16[1344,256]{1,0:T(8,128)(2,1)S(1)} %get-tuple-element.59), channel_id=1, source_target_pairs={{0,4},{4,0},{8,12},{12,8},{1,5},{5,1},{9,13},{13,9},{2,6},{6,2},{1... | collective-permute-start | bytes 2064392 | tf_op jit(solution)/shard_map/ppermute | solution.py:194
  242.7 16.9 %collective-permute-start.34 = (bf16[1344,256]{1,0:T(8,128)(2,1)S(1)}, bf16[1344,256]{1,0:T(8,128)(2,1)S(1)}, u32[]{:S(2)}, u32[]{:S(2)}) collective-permute-start(bf16[1344,256]{1,0:T(8,128)(2,1)S(1)} %collective-permute-done.28.refs_0_.near), channel_id=1, source_target_pairs={{1,2},{2,1},{5,6},{6,5},{9,10},{10,9},{13,14},{14,13},{17,18},{18,... | collective-permute-start | bytes 2064392 | tf_op jit(solution)/shard_map/ppermute | solution.py:182
  245.9 15.1 %collective-permute-start.32 = (bf16[1344,256]{1,0:T(8,128)(2,1)S(1)}, bf16[1344,256]{1,0:T(8,128)(2,1)S(1)}, u32[]{:S(2)}, u32[]{:S(2)}) collective-permute-start(bf16[1344,256]{1,0:T(8,128)(2,1)S(1)} %add_convert_fusion.2.after), channel_id=1, source_target_pairs={{0,8},{8,0},{4,12},{12,4},{1,9},{9,1},{5,13},{13,5},{2,10},{10,2},... | collective-permute-start | bytes 2064392 | tf_op jit(solution)/shard_map/ppermute | solution.py:199
  247.4 13.6 %collective-permute-start.33 = (bf16[1344,256]{1,0:T(8,128)(2,1)S(1)}, bf16[1344,256]{1,0:T(8,128)(2,1)S(1)}, u32[]{:S(2)}, u32[]{:S(2)}) collective-permute-start(bf16[1344,256]{1,0:T(8,128)(2,1)S(1)} %collective-permute-done.31.refs_1_.mid_a), channel_id=1, source_target_pairs={{1,0},{2,3},{5,4},{6,7},{9,8},{10,11},{13,12},{14,15},{17,16},{18,... | collective-permute-start | bytes 2064392 | tf_op jit(solution)/shard_map/ppermute | solution.py:183
  257.9 17.0 %collective-permute-start.36 = (bf16[1344,256]{1,0:T(8,128)(2,1)S(1)}, bf16[1344,256]{1,0:T(8,128)(2,1)S(1)}, u32[]{:S(2)}, u32[]{:S(2)}) collective-permute-start(bf16[1344,256]{1,0:T(8,128)(2,1)S(1)} %get-tuple-element.60.rest_0_), channel_id=1, source_target_pairs={{0,4},{4,0},{8,12},{12,8},{1,5},{5,1},{9,13},{13,9},{2,6},{6,2},{1... | collective-permute-start | bytes 2064392 | tf_op jit(solution)/shard_map/ppermute | solution.py:199
  259.7 21.5 %collective-permute-start.35 = (bf16[1344,256]{1,0:T(8,128)(2,1)S(1)}, bf16[1344,256]{1,0:T(8,128)(2,1)S(1)}, u32[]{:S(2)}, u32[]{:S(2)}) collective-permute-start(bf16[1344,256]{1,0:T(8,128)(2,1)S(1)} %collective-permute-done.34.rest_3_.mid_b), channel_id=1, source_target_pairs={{1,0},{2,3},{5,4},{6,7},{9,8},{10,11},{13,12},{14,15},{17,16},{18,... | collective-permute-start | bytes 2064392 | tf_op jit(solution)/shard_map/ppermute | solution.py:184
  275.6 19.5 %collective-permute-start.38 = (bf16[1344,256]{1,0:T(8,128)(2,1)S(1)}, bf16[1344,256]{1,0:T(8,128)(2,1)S(1)}, u32[]{:S(2)}, u32[]{:S(2)}) collective-permute-start(bf16[1344,256]{1,0:T(8,128)(2,1)S(1)} %get-tuple-element.77.after.own), channel_id=1, source_target_pairs={{0,1},{1,0},{2,3},{3,2},{4,5},{5,4},{6,7},{7,6},{8,9},{9,8},{10,11... | collective-permute-start | bytes 2064392 | tf_op jit(solution)/shard_map/ppermute | solution.py:180
  278.1 15.6 %collective-permute-start.39 = (bf16[1344,256]{1,0:T(8,128)(2,1)S(1)}, bf16[1344,256]{1,0:T(8,128)(2,1)S(1)}, u32[]{:S(2)}, u32[]{:S(2)}) collective-permute-start(bf16[1344,256]{1,0:T(8,128)(2,1)S(1)} %get-tuple-element.77.after.own), channel_id=1, source_target_pairs={{1,2},{2,1},{5,6},{6,5},{9,10},{10,9},{13,14},{14,13},{17,18},{18,... | collective-permute-start | bytes 2064392 | tf_op jit(solution)/shard_map/ppermute | solution.py:181
  290.1 7.9 %collective-permute-start.37 = (bf16[1344,256]{1,0:T(8,128)(2,1)S(1)}, bf16[1344,256]{1,0:T(8,128)(2,1)S(1)}, u32[]{:S(2)}, u32[]{:S(2)}) collective-permute-start(bf16[1344,256]{1,0:T(8,128)(2,1)S(1)} %get-tuple-element.65), channel_id=1, source_target_pairs={{0,4},{4,0},{8,12},{12,8},{1,5},{5,1},{9,13},{13,9},{2,6},{6,2},{1... | collective-permute-start | bytes 2064392 | tf_op jit(solution)/shard_map/ppermute | solution.py:194
  293.8 19.1 %collective-permute-start.42 = (bf16[1344,256]{1,0:T(8,128)(2,1)S(1)}, bf16[1344,256]{1,0:T(8,128)(2,1)S(1)}, u32[]{:S(2)}, u32[]{:S(2)}) collective-permute-start(bf16[1344,256]{1,0:T(8,128)(2,1)S(1)} %collective-permute-done.39.refs_1_.mid_a), channel_id=1, source_target_pairs={{1,0},{2,3},{5,4},{6,7},{9,8},{10,11},{13,12},{14,15},{17,16},{18,... | collective-permute-start | bytes 2064392 | tf_op jit(solution)/shard_map/ppermute | solution.py:183
  295.1 16.2 %collective-permute-start.43 = (bf16[1344,256]{1,0:T(8,128)(2,1)S(1)}, bf16[1344,256]{1,0:T(8,128)(2,1)S(1)}, u32[]{:S(2)}, u32[]{:S(2)}) collective-permute-start(bf16[1344,256]{1,0:T(8,128)(2,1)S(1)} %collective-permute-done.38.refs_0_.near), channel_id=1, source_target_pairs={{1,2},{2,1},{5,6},{6,5},{9,10},{10,9},{13,14},{14,13},{17,18},{18,... | collective-permute-start | bytes 2064392 | tf_op jit(solution)/shard_map/ppermute | solution.py:182
  298.3 14.7 %collective-permute-start.41 = (bf16[1344,256]{1,0:T(8,128)(2,1)S(1)}, bf16[1344,256]{1,0:T(8,128)(2,1)S(1)}, u32[]{:S(2)}, u32[]{:S(2)}) collective-permute-start(bf16[1344,256]{1,0:T(8,128)(2,1)S(1)} %add_convert_fusion.1.after), channel_id=1, source_target_pairs={{0,8},{8,0},{4,12},{12,4},{1,9},{9,1},{5,13},{13,5},{2,10},{10,2},... | collective-permute-start | bytes 2064392 | tf_op jit(solution)/shard_map/ppermute | solution.py:199
  307.8 19.0 %collective-permute-start.40 = (bf16[1344,256]{1,0:T(8,128)(2,1)S(1)}, bf16[1344,256]{1,0:T(8,128)(2,1)S(1)}, u32[]{:S(2)}, u32[]{:S(2)}) collective-permute-start(bf16[1344,256]{1,0:T(8,128)(2,1)S(1)} %get-tuple-element.67.rest_0_), channel_id=1, source_target_pairs={{0,4},{4,0},{8,12},{12,8},{1,5},{5,1},{9,13},{13,9},{2,6},{6,2},{1... | collective-permute-start | bytes 2064392 | tf_op jit(solution)/shard_map/ppermute | solution.py:199
  311.3 16.2 %collective-permute-start.44 = (bf16[1344,256]{1,0:T(8,128)(2,1)S(1)}, bf16[1344,256]{1,0:T(8,128)(2,1)S(1)}, u32[]{:S(2)}, u32[]{:S(2)}) collective-permute-start(bf16[1344,256]{1,0:T(8,128)(2,1)S(1)} %collective-permute-done.43.rest_3_.mid_b), channel_id=1, source_target_pairs={{1,0},{2,3},{5,4},{6,7},{9,8},{10,11},{13,12},{14,15},{17,16},{18,... | collective-permute-start | bytes 2064392 | tf_op jit(solution)/shard_map/ppermute | solution.py:184
  336.5 2.2 collective-permute-start.45
  338.8 26.9 %copy-start.16 = (f32[1,256]{1,0:T(1,128)S(1)}, f32[1,256]{1,0:T(1,128)}, u32[]{:S(2)}) copy-start(f32[1,256]{1,0:T(1,128)} %get-tuple-element.87) | copy-start | bytes 3076
  347.8 2.2 collective-permute-start.46
  348.0 17.7 %collective-permute-start.47 = (bf16[1344,256]{1,0:T(8,128)(2,1)S(1)}, bf16[1344,256]{1,0:T(8,128)(2,1)S(1)}, u32[]{:S(2)}, u32[]{:S(2)}) collective-permute-start(bf16[1344,256]{1,0:T(8,128)(2,1)S(1)} %add_convert_fusion.after), channel_id=1, source_target_pairs={{0,8},{8,0},{4,12},{12,4},{1,9},{9,1},{5,13},{13,5},{2,10},{10,2},... | collective-permute-start | bytes 2064392 | tf_op jit(solution)/shard_map/ppermute | solution.py:199
  (2 other events, 2.2 us)
